TPU v7x, 128 devices: a whole 4x4x4 slice. The times are simulated.
128 devices in a mesh: leaf: 16 (over y, z), node: 8 (over x, core).
Axes of the slice: x: 4, y: 4, z: 4, core: 2. Of those that a mesh axis runs over, the one named last changes fastest.
Arguments:
- x_start: float32 [36864, 512], P(('leaf', 'node')), may hold values from 0 to 1
- y_start: float32 [36864, 2048], P(('leaf', 'node')), may hold values from 0 to 1
- cost_vec: float32 [36864, 512], P(('leaf', 'node')), may hold values from -40 to 40
- right_side: float32 [36864, 2048], P(('leaf', 'node')), may hold values from -40 to 40
- omega: float32 [1], replicated, may hold values from 0.5 to 2
- coupling: bfloat16 [3, 2048, 512], replicated, may hold values from -0.25 to 0.25
- linking: bfloat16 [2, 2048, 512], replicated, may hold values from -0.25 to 0.25
- parent: int32 [36864], P(('leaf', 'node')), may hold values from -1 to 36863, as said below
- section: int32 [36864], P(('leaf', 'node')), may hold values from 0 to 2, as said below
Outputs:
- x_average: float32 [36864, 512], P(('leaf', 'node'))
- y_average: float32 [36864, 2048], P(('leaf', 'node'))
- omega_new: float32 [1], replicated
Inputs may be any that keep to these rules, and one draw needn't show every extreme that they name: Nodes of section 0 have parent -1; a node of section s >= 1 has a parent of section s - 1. On each device the first 32 nodes have section 0, then the section-1 nodes, then the section-2 nodes, 256 of the later sections together, at least one of each; the number of section-1 nodes differs from device to device. A section-1 node's parent lies on a device with the same index along node; a section-2 node's parent lies on a device with the same index along leaf. From one device, at most 32 section-1 nodes have their parents on one given device and at most 64 section-2 nodes have theirs on one given device; both bounds are reached in every draw.
All inputs are finite; a program needn't handle non-finite values.
Results may differ from a plain program's by a relative error of at most 0.0035.
Values may be sent and summed in bfloat16 or wider, within the bound.
No kernel may reach another device: no remote copies, remote signals or barrier semaphores. Data moves between devices by JAX's collectives and lax.ppermute only.
A program may use at most 128 MiB of HBM per device.

v0:
```python
import jax
import jax.numpy as jnp
from jax import lax
from jax.experimental import pallas as pl
from jax.experimental.pallas import tpu as pltpu
from jax.sharding import PartitionSpec as P

NS = 512
NC = 2048
ROOTS = 32
CHILD = 256
NODES = 288
N_LEAF = 16
N_NODE = 8
CAP_NODE = 64
SLOTS = 512
TILE = 512
VMEM_LIMIT = 24 * 2**20
STEP = 0.3
F32 = jnp.float32
BF16 = jnp.bfloat16
ROWS = slice(ROOTS, NODES)


def times(a, b):
    return lax.dot_general(a, b, (((1,), (0,)), ((), ())), preferred_element_type=F32)


def times_t(a, b):
    return lax.dot_general(a, b, (((1,), (1,)), ((), ())), preferred_element_type=F32)


def hot_rows(code, count):
    places = lax.broadcasted_iota(jnp.int32, (count, code.shape[1]), 0).astype(F32)
    return jnp.where(places == code, 1.0, 0.0).astype(BF16)


def hot_lanes(code, count):
    wide = jnp.concatenate([code] * (count // 128), axis=1)
    places = lax.broadcasted_iota(jnp.int32, wide.shape, 1).astype(F32)
    return jnp.where(places == wide, 1.0, 0.0).astype(BF16)


def to_lanes(row):
    return jnp.broadcast_to(row, (128, row.shape[1])).T


def call(kernel, outs, arrays, flops, scratch=(), far=()):
    out_shapes = [jax.ShapeDtypeStruct(shape, dtype) for shape, dtype in outs]
    moved = sum(a.size * a.dtype.itemsize for a in list(arrays) + out_shapes)
    out_shapes = [pltpu.VMEM(shape, dtype) for shape, dtype in outs]
    arrays = [
        pltpu.with_memory_space_constraint(a, pltpu.HBM) if i in far else a for i, a in enumerate(arrays)
    ]
    return pl.pallas_call(
        kernel,
        out_shape=out_shapes,
        in_specs=[pl.BlockSpec(memory_space=pl.ANY if i in far else pltpu.VMEM) for i in range(len(arrays))],
        out_specs=[pl.BlockSpec(memory_space=pltpu.VMEM)] * len(outs),
        scratch_shapes=list(scratch),
        compiler_params=pltpu.CompilerParams(vmem_limit_bytes=VMEM_LIMIT),
        cost_estimate=pl.CostEstimate(flops=flops, bytes_accessed=moved // 8, transcendentals=0),
    )(*arrays)


def parts():
    return [slice(i * TILE, (i + 1) * TILE) for i in range(NC // TILE)]


def first(parent_of, section_of, y_far, linking_far, x_far, cost_far, *refs):
    *outs, y, linking, ylow, nsend, nback, lsend, lback, scol, x_top, cost_top, state, sem = refs
    chunks = parts()
    copies = []
    for cols in chunks:
        copies.append((y_far.at[:, cols], y.at[:, cols]))
        copies.append((linking_far.at[1, cols], linking.at[1, cols]))
    for cols in chunks:
        copies.append((linking_far.at[0, cols], linking.at[0, cols]))
    copies += [(x_far.at[:ROOTS], x_top), (cost_far.at[:ROOTS], cost_top)]
    copies = [pltpu.make_async_copy(a, b, sem.at[i]) for i, (a, b) in enumerate(copies)]
    for copy in copies:
        copy.start()
    upper = section_of[...][:, ROWS] == 1
    parent = parent_of[...][:, ROWS]
    here = lax.axis_index("leaf") * N_NODE + lax.axis_index("node")
    owner = ((parent.astype(F32) + 0.5) * (1.0 / NODES)).astype(jnp.int32)
    local = parent - owner * NODES
    ry = ((owner >> 5) - (here >> 5)) & 3
    rz = ((owner >> 3) - (here >> 3)) & 3
    rx = ((owner >> 1) - (here >> 1)) & 3
    rc = (owner ^ here) & 1
    odd = (here & 1) == 1
    outer = jnp.where(odd, rz, ry)
    inner = jnp.where(odd, ry, rz)
    lrow = jnp.where(upper, outer * 128 + inner * ROOTS + local, -1).astype(F32)
    lend = jnp.where(upper, ((-outer) & 3) * 128 + inner * ROOTS + local, -1).astype(F32)
    peer = rx * 2 + rc
    peers = lax.broadcasted_iota(jnp.int32, (N_NODE, CHILD), 0)
    member = jnp.where((peers == peer) & jnp.logical_not(upper), 1.0, 0.0)
    before = lax.broadcasted_iota(jnp.int32, (CHILD, CHILD), 0) <= lax.broadcasted_iota(
        jnp.int32, (CHILD, CHILD), 1
    )
    counts = times(member.astype(BF16), jnp.where(before, 1.0, 0.0).astype(BF16))
    rank = jnp.sum(member * counts, axis=0, keepdims=True) - 1.0
    nrow = jnp.where(upper, -1.0, (peer * CAP_NODE).astype(F32) + rank)
    nend = jnp.where(upper, -1.0, (rc * 256 + rx * CAP_NODE).astype(F32) + rank)
    mark = jnp.where(upper, 0, local - (ROOTS - 1)).astype(F32)
    nsend[...] = nrow
    lsend[...] = lrow
    nback[...] = to_lanes(nend)
    lback[...] = to_lanes(lend)
    scol[...] = to_lanes(jnp.where(upper, 1.0, 2.0))
    total = None
    for i, cols in enumerate(chunks):
        copies[2 * i].wait()
        copies[2 * i + 1].wait()
        low = y[:, cols].astype(BF16)
        ylow[:, cols] = low
        term = times(low[ROWS], linking[1, cols])
        total = term if total is None else total + term
    load = jnp.concatenate([total.astype(BF16), to_lanes(mark).astype(BF16)], axis=1)
    spread(nrow, load, outs[:4])
    total = None
    for i, cols in enumerate(chunks):
        copies[2 * len(chunks) + i].wait()
        term = times(ylow[ROWS, cols], linking[0, cols])
        total = term if total is None else total + term
    spread(lrow, total.astype(BF16), outs[4:])
    copies[-2].wait()
    copies[-1].wait()
    state[...] = x_top[...].astype(BF16)


def spread(row, load, outs):
    hot = hot_rows(row, SLOTS)
    for k, out in enumerate(outs):
        out[...] = times(hot[k * 128 : (k + 1) * 128], load).astype(BF16)


def own_adjoint(ylow, scol, coupling, own):
    upper = jnp.concatenate([scol[...]] * (NS // 128), axis=1) == 1.0
    low = ylow[ROWS]
    own[...] = jnp.where(upper, times(low, coupling[0]), times(low, coupling[1]))


def own_root_first(ylow, cost_top, coupling_far, own_root, coupling_root, sem):
    copies = [
        pltpu.make_async_copy(coupling_far.at[0, cols], coupling_root.at[cols], sem.at[i])
        for i, cols in enumerate(parts())
    ]
    for copy in copies:
        copy.start()
    total = -cost_top[...]
    for copy, cols in zip(copies, parts()):
        copy.wait()
        total = total + times(ylow[:ROOTS, cols], coupling_root[cols])
    own_root[...] = total


def own_first(ylow, scol, coupling_far, own, coupling, sem):
    copies = [
        pltpu.make_async_copy(coupling_far.at[pl.ds(1, 2), cols], coupling.at[:, cols], sem.at[i])
        for i, cols in enumerate(parts())
    ]
    for copy in copies:
        copy.start()
    first_total, second_total = None, None
    for copy, cols in zip(copies, parts()):
        copy.wait()
        low = ylow[ROWS, cols]
        one, two = times(low, coupling[0, cols]), times(low, coupling[1, cols])
        first_total = one if first_total is None else first_total + one
        second_total = two if second_total is None else second_total + two
    upper = jnp.concatenate([scol[...]] * (NS // 128), axis=1) == 1.0
    own[...] = jnp.where(upper, first_total, second_total)


def join(blocks, swapped, held):
    for k, block in enumerate(blocks):
        held[k * CAP_NODE : (k + 1) * CAP_NODE] = block[:CAP_NODE]
    held[256:] = swapped[...]


def primal_first(g0, g1, g2, g3, swapped, own, x, cost, rates, wrow, wcol, x_next, extra, *refs):
    *sends, held = refs
    join((g0, g1, g2, g3), swapped, held)
    mark = held[:, NS:].astype(F32)
    row = mark.T[:8]
    wcol[...] = mark
    wrow[...] = row
    primal_child(held[:, :NS], own, x[ROWS], cost, rates, mark, row, x_next, extra, sends)


def primal_second(g0, g1, g2, g3, swapped, own, x, cost, rates, wrow, wcol, x_next, extra, *refs):
    *sends, held = refs
    join((g0, g1, g2, g3), swapped, held)
    primal_child(held[...], own, x[...], cost, rates, wcol[...], wrow[...], x_next, extra, sends)


def primal_child(got, own, x_old, cost, rates, mark, row, x_next, extra, sends):
    tau = rates[:1, :1]
    adjoint = own[...] + times(hot_rows(row[:1] - 1.0, CHILD), got)
    new = jnp.maximum(x_old - tau * (cost[ROWS] - adjoint), 0.0)
    low = (2.0 * new - x_old).astype(BF16)
    x_next[...] = new
    extra[...] = low
    reply = times(hot_lanes(mark - 1.0, CHILD), low).astype(BF16)
    for k, send in enumerate(sends):
        send[:CAP_NODE] = reply[k * CAP_NODE : (k + 1) * CAP_NODE]
        send[CAP_NODE:] = reply[256 + k * CAP_NODE : 256 + (k + 1) * CAP_NODE]


def rooted(j):
    return slice(j * ROOTS, (j + 1) * ROOTS)


def summed(blocks, j):
    return sum(block[rooted((j + k) & 3)].astype(F32) for k, block in enumerate(blocks))


def root_first(g0, g1, g2, g3, own, x, rates, x_next, extra):
    blocks = (g0, g1, g2, g3)
    tau = rates[:1, :1]
    for j in range(4):
        slope = summed(blocks, j)
        if j == 0:
            x_old = x[...]
            slope = slope + own[...]
        else:
            x_old = blocks[(-j) & 3][rooted(4)].astype(F32)
        new = jnp.maximum(x_old + tau * slope, 0.0)
        x_next[rooted(j)] = new
        extra[rooted(j)] = (2.0 * new - x_old).astype(BF16)


def root_second(g0, g1, g2, g3, own, x, rates, extra, x_next):
    blocks = (g0, g1, g2, g3)
    tau = rates[:1, :1]
    for j in range(4):
        slope = summed(blocks, j)
        if j == 0:
            slope = slope + own[...]
        x_old = x[rooted(j)]
        new = jnp.maximum(x_old + tau * slope, 0.0)
        extra[rooted(j)] = (2.0 * new - x_old).astype(BF16)
        if j == 0:
            x_next[...] = new


def averages(x_start, x_root, x_root_next, x_child, x_child_next, average, move):
    roots = (x_root[:ROOTS] + x_root_next[...]) * 0.5
    children = (x_child[...] + x_child_next[...]) * 0.5
    average[:ROOTS] = roots
    average[ROWS] = children
    gap_roots = roots - x_start[:ROOTS]
    gap_children = children - x_start[ROWS]
    total = jnp.sum(gap_roots * gap_roots) + jnp.sum(gap_children * gap_children)
    move[...] = jnp.full((8, 128), total, F32)


def own_image(
    last, extra_child, extra_root, scol, coupling_root, coupling, y, right, rates, cost_top, base, *refs
):
    sigma = rates[1:2, :1]
    upper = jnp.concatenate([scol[...]] * (TILE // 128), axis=1) == 1.0
    child = extra_child[...]
    root = extra_root[:ROOTS]
    total = -cost_top[...]
    for cols in parts():
        image = jnp.where(
            upper, times_t(child, coupling[0, cols]), times_t(child, coupling[1, cols])
        )
        weights = coupling_root[cols]
        base_root = y[:ROOTS, cols] + sigma * (right[:ROOTS, cols] - times_t(root, weights))
        base[:ROOTS, cols] = base_root
        if not last:
            total = total + times(jnp.maximum(base_root, 0.0).astype(BF16), weights)
        base[ROWS, cols] = y[ROWS, cols] + sigma * (right[ROWS, cols] - image)
    if not last:
        (own_root,) = refs
        own_root[...] = total


def from_leaf(blocks, lback):
    hot = hot_lanes(lback[...], SLOTS)
    rows = None
    for k, block in enumerate(blocks):
        term = times(hot[:, k * 128 : (k + 1) * 128], block[...])
        rows = term if rows is None else rows + term
    return rows.astype(BF16)


def dual_leaf(last, b0, b1, b2, b3, lback, linking, base, rates, *refs):
    if last:
        (later,) = refs
    else:
        lsend, later, *outs = refs
    rows = from_leaf((b0, b1, b2, b3), lback)
    sigma = rates[1:2, :1]
    total = None
    for cols in parts():
        weights = linking[0, cols]
        new = base[ROWS, cols] - sigma * times_t(rows, weights)
        later[:, cols] = new
        if not last:
            product = times(jnp.maximum(new, 0.0).astype(BF16), weights)
            total = product if total is None else total + product
    if not last:
        spread(lsend[...], total.astype(BF16), outs)


def from_node(blocks, swapped, nback, held):
    join(blocks, swapped, held)
    return times(hot_lanes(nback[...], SLOTS), held[...]).astype(BF16)


def dual_node(g0, g1, g2, g3, swapped, nback, linking, base, later, rates, nsend, *refs):
    y_next, ylow, *outs, held = refs
    rows = from_node((g0, g1, g2, g3), swapped, nback, held)
    sigma = rates[1:2, :1]
    total = None
    for cols in parts():
        weights = linking[1, cols]
        new_root = jnp.maximum(base[:ROOTS, cols], 0.0)
        new = jnp.maximum(later[:, cols] - sigma * times_t(rows, weights), 0.0)
        low = new.astype(BF16)
        y_next[:ROOTS, cols] = new_root
        y_next[ROWS, cols] = new
        ylow[:ROOTS, cols] = new_root.astype(BF16)
        ylow[ROWS, cols] = low
        product = times(low, weights)
        total = product if total is None else total + product
    spread(nsend[...], total.astype(BF16), outs)


def dual_last(
    g0, g1, g2, g3, swapped, nback, linking, base, later, rates, y, y_start, primal_move, average, load, held
):
    rows = from_node((g0, g1, g2, g3), swapped, nback, held)
    sigma = rates[1:2, :1]
    move = jnp.zeros((1, TILE), F32)
    for cols in parts():
        new_root = jnp.maximum(base[:ROOTS, cols], 0.0)
        new = jnp.maximum(later[:, cols] - sigma * times_t(rows, linking[1, cols]), 0.0)
        mean_root = (y[:ROOTS, cols] + new_root) * 0.5
        mean = (y[ROWS, cols] + new) * 0.5
        average[:ROOTS, cols] = mean_root
        average[ROWS, cols] = mean
        gap_root = mean_root - y_start[:ROOTS, cols]
        gap = mean - y_start[ROWS, cols]
        move = move + jnp.sum(gap_root * gap_root, axis=0, keepdims=True)
        move = move + jnp.sum(gap * gap, axis=0, keepdims=True)
    lane = lax.broadcasted_iota(jnp.int32, load.shape, 2)
    load[...] = jnp.where(lane == 0, primal_move[:1], jnp.sum(move))


def pairs_of(place):
    pairs = []
    for i in range(N_LEAF * N_NODE):
        y, z, x, core = place(i >> 5, (i >> 3) & 3, (i >> 1) & 3, i & 1)
        pairs.append((i, ((y & 3) * 4 + (z & 3)) * N_NODE + (x & 3) * 2 + core))
    return ("leaf", "node"), pairs


def outer_ring(k):
    return pairs_of(lambda y, z, x, c: (y, z + k, x, c) if c else (y + k, z, x, c))


def inner_ring(k):
    return pairs_of(lambda y, z, x, c: (y + k, z, x, c) if c else (y, z + k, x, c))


def ring_x(k):
    return pairs_of(lambda y, z, x, c: (y, z, x + k, c))


def sibling(array):
    return lax.ppermute(array, *pairs_of(lambda y, z, x, c: (y, z, x, 1 - c)))


def shifted(blocks, ring, sign=1):
    got = {0: blocks[0]}
    for k in (2, 1, 3):
        got[k] = lax.ppermute(blocks[k], *ring((sign * k) % 4))
    return [got[k] for k in range(4)]


def swap_node(blocks, sign, before):
    got = shifted(blocks, ring_x, sign)
    halves = jnp.concatenate([block[CAP_NODE:] for block in got], axis=0)
    halves, before = lax.optimization_barrier((halves, before))
    return got + [sibling(halves)], before


def sum_leaf(blocks, own, state, before):
    got, before = lax.optimization_barrier((shifted(blocks, outer_ring), before))
    got = [block.astype(F32) for block in got]
    total = ((got[0] + got[1]) + got[2]) + got[3]
    sent = jnp.concatenate([total[:ROOTS] + own, total[ROOTS:]], axis=0).astype(BF16)
    if state is not None:
        sent = jnp.concatenate([sent, state], axis=0)
    return [total.astype(BF16)] + shifted([sent] * 4, inner_ring)[1:], before


def part_of(kernel, flag):
    def run(*refs):
        kernel(flag, *refs)

    return run


def shards(x_start, y_start, cost_vec, right_side, omega, coupling, linking, parent, section):
    unit = 2 * CHILD * NS * NC
    rates = jnp.broadcast_to(jnp.stack([STEP / omega[0], STEP * omega[0]])[:, None], (2, 128))
    field = ((NODES, NC), F32)
    field_low = ((NODES, NC), BF16)
    states = ((NODES, NS), F32)
    block = ((128, NS), BF16)
    block_mark = ((128, NS + 128), BF16)
    kids = ((CHILD, NS), F32)
    kids_low = ((CHILD, NS), BF16)
    kids_field = ((CHILD, NC), F32)
    tops = ((ROOTS, NS), F32)
    plane = ((4 * ROOTS, NS), F32)
    row = ((1, CHILD), F32)
    col = ((CHILD, 128), F32)
    held = [pltpu.VMEM((SLOTS, NS), BF16)]

    *sent, y_start, linking, ylow, nsend, nback, lsend, lback, scol, x_top, cost_top, state = call(
        first,
        [block_mark] * 4 + [block] * 4
        + [field, ((2, NC, NS), BF16), field_low, row, col, row, col, col, tops, tops, ((ROOTS, NS), BF16)],
        [parent.reshape(1, NODES), section.reshape(1, NODES), y_start, linking, x_start, cost_vec],
        2 * unit,
        [pltpu.SemaphoreType.DMA((3 * NC // TILE + 2,))],
        (2, 3, 4, 5),
    )
    chunk_sems = [pltpu.SemaphoreType.DMA((NC // TILE,))]
    own_root, coupling_root = call(
        own_root_first, [tops, ((NC, NS), BF16)], [ylow, cost_top, coupling], unit // 8, chunk_sems, (2,)
    )
    own, coupling = call(
        own_first, [kids, ((2, NC, NS), BF16)], [ylow, scol, coupling], 2 * unit, chunk_sems, (2,)
    )
    got_leaf, _ = sum_leaf(sent[4:], own_root, state, own_root)
    got_node, (got_leaf, own) = swap_node(sent[:4], 1, (got_leaf, own))

    x_root, extra_root = call(
        root_first,
        [plane, block],
        got_leaf + [own_root, x_top, rates],
        0,
    )
    own, extra_root = lax.optimization_barrier((own, extra_root))
    wrow, wcol, x_child, extra_child, *out_node = call(
        primal_first,
        [((8, SLOTS), F32), ((SLOTS, 128), F32), kids, kids_low] + [block] * 4,
        got_node + [own, x_start, cost_vec, rates],
        unit // 4,
        [pltpu.VMEM((SLOTS, NS + 128), BF16)],
    )
    base, own_root = call(
        part_of(own_image, False),
        [field, tops],
        [
            extra_child, extra_root, scol, coupling_root, coupling, y_start, right_side, rates, cost_top
        ],
        2 * unit,
    )
    back_leaf = shifted([extra_root] * 4, outer_ring)
    back_node, (back_leaf, base) = swap_node(out_node, -1, (back_leaf, base))
    later, *out_leaf = call(
        part_of(dual_leaf, False),
        [kids_field] + [block] * 4,
        back_leaf + [lback, linking, base, rates, lsend],
        2 * unit,
    )
    y_next, ylow, *out_node = call(
        dual_node,
        [field, field_low] + [block] * 4,
        back_node + [nback, linking, base, later, rates, nsend],
        2 * unit,
        held,
    )
    got_leaf, ylow = sum_leaf(out_leaf, own_root, None, ylow)
    (own,) = call(own_adjoint, [kids], [ylow, scol, coupling], 2 * unit)
    got_node, (got_leaf, own) = swap_node(out_node, 1, (got_leaf, own))

    extra_root, x_top = call(
        root_second,
        [block, tops],
        got_leaf + [own_root, x_root, rates],
        0,
    )
    own, extra_root = lax.optimization_barrier((own, extra_root))
    x_child_next, extra_child, *out_node = call(
        primal_second,
        [kids, kids_low] + [block] * 4,
        got_node + [own, x_child, cost_vec, rates, wrow, wcol],
        unit // 4,
        held,
    )
    x_average, primal_move = call(
        averages,
        [states, ((8, 128), F32)],
        [x_start, x_root, x_top, x_child, x_child_next],
        0,
    )
    (base,) = call(
        part_of(own_image, True),
        [field],
        [extra_child, extra_root, scol, coupling_root, coupling, y_next, right_side, rates, cost_top],
        2 * unit,
    )
    back_leaf = shifted([extra_root] * 4, outer_ring)
    back_node, (back_leaf, base) = swap_node(out_node, -1, (back_leaf, base))
    (later,) = call(
        part_of(dual_leaf, True), [kids_field], back_leaf + [lback, linking, base, rates], unit
    )
    y_average, load = call(
        dual_last,
        [field, ((N_LEAF * N_NODE, 1, 128), F32)],
        back_node + [nback, linking, base, later, rates, y_next, y_start, primal_move],
        unit,
        held,
    )
    moves = lax.all_to_all(load, ("leaf", "node"), split_axis=0, concat_axis=0, tiled=True)
    moves = jnp.sum(moves[:, 0, :2], axis=0)
    omega_new = jnp.sqrt((moves[1:] + 1e-06) / (moves[:1] + 1e-06))
    return (x_average, y_average, omega_new)


def solution(mesh):
    both = P(("leaf", "node"), None)
    flat = P(("leaf", "node"))
    return jax.shard_map(
        shards,
        mesh=mesh,
        in_specs=(both, both, both, both, P(), P(), P(), flat, flat),
        out_specs=(both, both, P()),
        check_vma=False,
    )
```

profile of v0, /device:TPU:1, one launch (start us, length us, event | category | flops | bytes accessed | tf_op | source)
XLA Modules:
  0.0 107.0 jit_solution(13336449967738736589)
XLA Ops:
  2.0 4.4 %shard_map.112 = (bf16[128,640]{1,0:T(8,128)(2,1)S(1)}, bf16[128,640]{1,0:T(8,128)(2,1)S(1)}, bf16[128,640]{1,0:T(8,128)(2,1)S(1)}, bf16[128,640]{1,0:T(8,128)(2...) custom-call(s32[1,288]{1,0:T(1,128)S(1)} %reshape.19.parent_of, ...), custom_call_target="tpu_custom_call" | custom-call | flops 1073741824 | bytes 2150944 | tf_op jit(solution)/shard_map/pallas_call | solution.py:55
  6.4 2.5 %collective-permute-start.3 = (bf16[128,512]{1,0:T(8,128)(2,1)S(1)}, bf16[128,512]{1,0:T(8,128)(2,1)S(1)}, u32[]{:S(2)}, u32[]{:S(2)}) collective-permute-start(bf16[128,512]{1,0:T(8,128)(2,1)S(1)} %get-tuple-element.103), channel_id=1, source_target_pairs={{0,32},{1,9},{2,34},{3,11},{4,36},{5,13},{6,38},{7,15},{8,40},{9,1... | collective-permute-start | bytes 393224 | tf_op jit(solution)/shard_map/ppermute | solution.py:384
  8.9 3.3 %collective-permute-start.4 = (bf16[128,512]{1,0:T(8,128)(2,1)S(1)}, bf16[128,512]{1,0:T(8,128)(2,1)S(1)}, u32[]{:S(2)}, u32[]{:S(2)}) collective-permute-start(bf16[128,512]{1,0:T(8,128)(2,1)S(1)} %get-tuple-element.104), channel_id=1, source_target_pairs={{0,64},{1,17},{2,66},{3,19},{4,68},{5,21},{6,70},{7,23},{8,72},{9,... | collective-permute-start | bytes 393224 | tf_op jit(solution)/shard_map/ppermute | solution.py:384
  14.1 2.5 %collective-permute-start.1 = (bf16[128,640]{1,0:T(8,128)(2,1)S(1)}, bf16[128,640]{1,0:T(8,128)(2,1)S(1)}, u32[]{:S(2)}, u32[]{:S(2)}) collective-permute-start(bf16[128,640]{1,0:T(8,128)(2,1)S(1)} %get-tuple-element.100), channel_id=1, source_target_pairs={{0,4},{1,5},{2,6},{3,7},{4,0},{5,1},{6,2},{7,3},{8,12},{9,13},{10,... | collective-permute-start | bytes 491528 | tf_op jit(solution)/shard_map/ppermute | solution.py:384
  16.6 1.7 %shard_map.113 = (f32[32,512]{1,0:T(8,128)S(1)}, bf16[2048,512]{1,0:T(8,128)(2,1)S(1)}) custom-call(bf16[288,2048]{1,0:T(8,128)(2,1)S(1)} %get-tuple-element.106.ylow, f32[32,512]{1,0:T(8,128)S(1)} %get-tuple-element.107.cost_top.refs_8_, bf16[3,2048,512]{2,1,0:T(8,128)(2,1)} %coupling_far.3), custom_call_target="tpu_custom_call" | custom-call | flops 67108864 | bytes 1212416 | tf_op jit(solution)/shard_map/pallas_call | solution.py:55
  19.7 2.8 %collective-permute-start.8 = (bf16[160,512]{1,0:T(8,128)(2,1)S(1)}, bf16[160,512]{1,0:T(8,128)(2,1)S(1)}, u32[]{:S(2)}, u32[]{:S(2)}) collective-permute-start(bf16[160,512]{1,0:T(8,128)(2,1)S(1)} %pad_maximum_fusion.4), channel_id=1, source_target_pairs={{0,24},{1,97},{2,26},{3,99},{4,28},{5,101},{6,30},{7,103},{8,0},{9... | collective-permute-start | bytes 491528 | tf_op jit(solution)/shard_map/ppermute | solution.py:384
  23.6 2.9 %shard_map.114 = (f32[256,512]{1,0:T(8,128)S(1)}, bf16[2,2048,512]{2,1,0:T(8,128)(2,1)S(1)}) custom-call(bf16[288,2048]{1,0:T(8,128)(2,1)S(1)} %get-tuple-element.106.ylow, f32[256,128]{1,0:T(8,128)S(1)} %get-tuple-element.114.scol.refs_2_, bf16[3,2048,512]{2,1,0:T(8,128)(2,1)} %coupling_far.3), custom_call_target="tpu_custom_call" | custom-call | flops 1073741824 | bytes 1540096 | tf_op jit(solution)/shard_map/pallas_call | solution.py:55
  26.7 1.6 %collective-permute-done.7.g2 = bf16[160,512]{1,0:T(8,128)(2,1)S(1)} collective-permute-done((bf16[160,512]{1,0:T(8,128)(2,1)S(1)}, bf16[160,512]{1,0:T(8,128)(2,1)S(1)}, u32[]{:S(2)}, u32[]{:S(2)}) %collective-permute-start.7) | collective-permute-done | bytes 163872 | tf_op jit(solution)/shard_map/ppermute | solution.py:384
  28.3 1.9 %collective-permute-done.6.g1 = bf16[160,512]{1,0:T(8,128)(2,1)S(1)} collective-permute-done((bf16[160,512]{1,0:T(8,128)(2,1)S(1)}, bf16[160,512]{1,0:T(8,128)(2,1)S(1)}, u32[]{:S(2)}, u32[]{:S(2)}) %collective-permute-start.6) | collective-permute-done | bytes 163872 | tf_op jit(solution)/shard_map/ppermute | solution.py:384
  30.2 3.5 %collective-permute-start.9 = (bf16[256,640]{1,0:T(8,128)(2,1)S(1)}, bf16[256,640]{1,0:T(8,128)(2,1)S(1)}, u32[]{:S(2)}, u32[]{:S(2)}) collective-permute-start(bf16[256,640]{1,0:T(8,128)(2,1)S(1)} %pad_maximum_fusion), channel_id=1, source_target_pairs={{0,1},{1,0},{2,3},{3,2},{4,5},{5,4},{6,7},{7,6},{8,9},{9,8},{10,11... | collective-permute-start | bytes 983048 | tf_op jit(solution)/shard_map/ppermute | solution.py:378
  35.9 2.1 %collective-permute-start.11 = (bf16[128,512]{1,0:T(8,128)(2,1)S(1)}, bf16[128,512]{1,0:T(8,128)(2,1)S(1)}, u32[]{:S(2)}, u32[]{:S(2)}) collective-permute-start(bf16[128,512]{1,0:T(8,128)(2,1)S(1)} %get-tuple-element.128), channel_id=1, source_target_pairs={{0,4},{1,5},{2,6},{3,7},{4,0},{5,1},{6,2},{7,3},{8,12},{9,13},{10,... | collective-permute-start | bytes 393224 | tf_op jit(solution)/shard_map/ppermute | solution.py:384
  38.6 2.0 %collective-permute-done.10.g1 = bf16[128,512]{1,0:T(8,128)(2,1)S(1)} collective-permute-done((bf16[128,512]{1,0:T(8,128)(2,1)S(1)}, bf16[128,512]{1,0:T(8,128)(2,1)S(1)}, u32[]{:S(2)}, u32[]{:S(2)}) %collective-permute-start.10) | collective-permute-done | bytes 131104 | tf_op jit(solution)/shard_map/ppermute | solution.py:384
  40.6 2.5 %shard_map.117 = (f32[288,2048]{1,0:T(8,128)S(1)}, f32[32,512]{1,0:T(8,128)S(1)}) custom-call(bf16[256,512]{1,0:T(8,128)(2,1)S(1)} %get-tuple-element.131.refs_0_, bf16[128,512]{1,0:T(8,128)(2,1)S(1)} %get-tuple-element.140.refs_1_.refs_0_, f32[256,128]{1,0:T(8,128)S(1)} %get-tuple-element.114.scol.refs_2_, ...), custom_call_target="tpu_custom_call" | custom-call | flops 1073741824 | bytes 1753216 | tf_op jit(solution)/shard_map/pallas_call | solution.py:55
  43.2 2.0 %collective-permute-done.12.g3 = bf16[128,512]{1,0:T(8,128)(2,1)S(1)} collective-permute-done((bf16[128,512]{1,0:T(8,128)(2,1)S(1)}, bf16[128,512]{1,0:T(8,128)(2,1)S(1)}, u32[]{:S(2)}, u32[]{:S(2)}) %collective-permute-start.12) | collective-permute-done | bytes 131104 | tf_op jit(solution)/shard_map/ppermute | solution.py:384
  45.8 3.0 %collective-permute-start.16 = (bf16[256,512]{1,0:T(8,128)(2,1)S(1)}, bf16[256,512]{1,0:T(8,128)(2,1)S(1)}, u32[]{:S(2)}, u32[]{:S(2)}) collective-permute-start(bf16[256,512]{1,0:T(8,128)(2,1)S(1)} %pad_maximum_fusion.1), channel_id=1, source_target_pairs={{0,1},{1,0},{2,3},{3,2},{4,5},{5,4},{6,7},{7,6},{8,9},{9,8},{10,11... | collective-permute-start | bytes 786440 | tf_op jit(solution)/shard_map/ppermute | solution.py:378
  48.8 2.1 %shard_map.118 = (f32[256,2048]{1,0:T(8,128)S(1)}, bf16[128,512]{1,0:T(8,128)(2,1)S(1)}, bf16[128,512]{1,0:T(8,128)(2,1)S(1)}, bf16[128,512]{1,0:T(8,128)(2,1)S(1)}, bf16[128,512]{1,0:T(8,128)(2,1)S(1)}) custom-call(bf16[128,512]{1,0:T(8,128)(2,1)S(1)} %get-tuple-element.140.refs_1_.refs_0_, bf16[128,512]{1,0:T(8,128)(2,1)S(1)} %collective-permute-done.13.refs_1_, ...), custom_call_target="tpu_custom_call" | custom-call | flops 1073741824 | bytes 1229056 | tf_op jit(solution)/shard_map/pallas_call | solution.py:55
  51.0 1.8 %collective-permute-start.21 = (bf16[128,512]{1,0:T(8,128)(2,1)S(1)}, bf16[128,512]{1,0:T(8,128)(2,1)S(1)}, u32[]{:S(2)}, u32[]{:S(2)}) collective-permute-start(bf16[128,512]{1,0:T(8,128)(2,1)S(1)} %get-tuple-element.154), channel_id=1, source_target_pairs={{0,64},{1,17},{2,66},{3,19},{4,68},{5,21},{6,70},{7,23},{8,72},{9,... | collective-permute-start | bytes 393224 | tf_op jit(solution)/shard_map/ppermute | solution.py:384
  53.6 2.0 %shard_map.119 = (f32[288,2048]{1,0:T(8,128)S(1)}, bf16[288,2048]{1,0:T(8,128)(2,1)S(1)}, bf16[128,512]{1,0:T(8,128)(2,1)S(1)}, bf16[128,512]{1,0:T(8,128)(2,1)S...) custom-call(bf16[128,512]{1,0:T(8,128)(2,1)S(1)} %get-tuple-element.126.g0, ...), custom_call_target="tpu_custom_call" | custom-call | flops 1073741824 | bytes 1704192 | tf_op jit(solution)/shard_map/pallas_call | solution.py:55
  55.7 2.4 %collective-permute-start.17 = (bf16[128,512]{1,0:T(8,128)(2,1)S(1)}, bf16[128,512]{1,0:T(8,128)(2,1)S(1)}, u32[]{:S(2)}, u32[]{:S(2)}) collective-permute-start(bf16[128,512]{1,0:T(8,128)(2,1)S(1)} %get-tuple-element.149), channel_id=1, source_target_pairs={{0,2},{1,3},{2,4},{3,5},{4,6},{5,7},{6,0},{7,1},{8,10},{9,11},{10,... | collective-permute-start | bytes 393224 | tf_op jit(solution)/shard_map/ppermute | solution.py:384
  58.9 1.6 %collective-permute-start.19 = (bf16[128,512]{1,0:T(8,128)(2,1)S(1)}, bf16[128,512]{1,0:T(8,128)(2,1)S(1)}, u32[]{:S(2)}, u32[]{:S(2)}) collective-permute-start(bf16[128,512]{1,0:T(8,128)(2,1)S(1)} %get-tuple-element.151), channel_id=1, source_target_pairs={{0,6},{1,7},{2,0},{3,1},{4,2},{5,3},{6,4},{7,5},{8,14},{9,15},{10,... | collective-permute-start | bytes 393224 | tf_op jit(solution)/shard_map/ppermute | solution.py:384
  60.8 1.3 %collective-permute-start.24 = (bf16[128,512]{1,0:T(8,128)(2,1)S(1)}, bf16[128,512]{1,0:T(8,128)(2,1)S(1)}, u32[]{:S(2)}, u32[]{:S(2)}) collective-permute-start(bf16[128,512]{1,0:T(8,128)(2,1)S(1)} %pad_maximum_fusion.5), channel_id=1, source_target_pairs={{0,16},{1,65},{2,18},{3,67},{4,20},{5,69},{6,22},{7,71},{8,24},{9,... | collective-permute-start | bytes 393224 | tf_op jit(solution)/shard_map/ppermute | solution.py:384
  63.5 1.5 %collective-permute-done.18.g2 = bf16[128,512]{1,0:T(8,128)(2,1)S(1)} collective-permute-done((bf16[128,512]{1,0:T(8,128)(2,1)S(1)}, bf16[128,512]{1,0:T(8,128)(2,1)S(1)}, u32[]{:S(2)}, u32[]{:S(2)}) %collective-permute-start.18) | collective-permute-done | bytes 131104 | tf_op jit(solution)/shard_map/ppermute | solution.py:384
  66.2 1.6 %collective-permute-done.23.g1 = bf16[128,512]{1,0:T(8,128)(2,1)S(1)} collective-permute-done((bf16[128,512]{1,0:T(8,128)(2,1)S(1)}, bf16[128,512]{1,0:T(8,128)(2,1)S(1)}, u32[]{:S(2)}, u32[]{:S(2)}) %collective-permute-start.23) | collective-permute-done | bytes 131104 | tf_op jit(solution)/shard_map/ppermute | solution.py:384
  67.8 3.0 %collective-permute-start.26 = (bf16[256,512]{1,0:T(8,128)(2,1)S(1)}, bf16[256,512]{1,0:T(8,128)(2,1)S(1)}, u32[]{:S(2)}, u32[]{:S(2)}) collective-permute-start(bf16[256,512]{1,0:T(8,128)(2,1)S(1)} %pad_maximum_fusion.2), channel_id=1, source_target_pairs={{0,1},{1,0},{2,3},{3,2},{4,5},{5,4},{6,7},{7,6},{8,9},{9,8},{10,11... | collective-permute-start | bytes 786440 | tf_op jit(solution)/shard_map/ppermute | solution.py:378
  76.1 1.4 %collective-permute-done.27.g1 = bf16[128,512]{1,0:T(8,128)(2,1)S(1)} collective-permute-done((bf16[128,512]{1,0:T(8,128)(2,1)S(1)}, bf16[128,512]{1,0:T(8,128)(2,1)S(1)}, u32[]{:S(2)}, u32[]{:S(2)}) %collective-permute-start.27) | collective-permute-done | bytes 131104 | tf_op jit(solution)/shard_map/ppermute | solution.py:384
  77.5 2.0 %shard_map.124.refs_6_.base = f32[288,2048]{1,0:T(8,128)S(1)} custom-call(bf16[256,512]{1,0:T(8,128)(2,1)S(1)} %get-tuple-element.182.refs_0_, bf16[128,512]{1,0:T(8,128)(2,1)S(1)} %get-tuple-element.186.refs_1_.refs_0_, f32[256,128]{1,0:T(8,128)S(1)} %get-tuple-element.114.scol.refs_2_, bf16[2048,512]{1,0:T(8,128)(2,1)S(1)} %get-tuple-element.132.refs_3_, ...), custom_call_target="tpu_custom_call" | custom-call | flops 1073741824 | bytes 1745024 | tf_op jit(solution)/shard_map/pallas_call | solution.py:55
  79.5 3.5 %collective-permute-done.29.g3 = bf16[128,512]{1,0:T(8,128)(2,1)S(1)} collective-permute-done((bf16[128,512]{1,0:T(8,128)(2,1)S(1)}, bf16[128,512]{1,0:T(8,128)(2,1)S(1)}, u32[]{:S(2)}, u32[]{:S(2)}) %collective-permute-start.29) | collective-permute-done | bytes 131104 | tf_op jit(solution)/shard_map/ppermute | solution.py:384
  83.1 2.5 %collective-permute-start.33 = (bf16[256,512]{1,0:T(8,128)(2,1)S(1)}, bf16[256,512]{1,0:T(8,128)(2,1)S(1)}, u32[]{:S(2)}, u32[]{:S(2)}) collective-permute-start(bf16[256,512]{1,0:T(8,128)(2,1)S(1)} %pad_maximum_fusion.3), channel_id=1, source_target_pairs={{0,1},{1,0},{2,3},{3,2},{4,5},{5,4},{6,7},{7,6},{8,9},{9,8},{10,11... | collective-permute-start | bytes 786440 | tf_op jit(solution)/shard_map/ppermute | solution.py:378
  87.1 2.0 %shard_map.126 = (f32[288,2048]{1,0:T(8,128)S(1)}, f32[128,1,128]{2,1,0:T(1,128)}) custom-call(bf16[128,512]{1,0:T(8,128)(2,1)S(1)} %get-tuple-element.177.g0, bf16[128,512]{1,0:T(8,128)(2,1)S(1)} %collective-permute-done.27.g1, bf16[128,512]{1,0:T(8,128)(2,1)S(1)} %collective-permute-done.28.g2, bf16[128,512]{1,0:T(8,128)(2,1)S(1)} %collective-permute-done.29.g3, ...), custom_call_target="tpu_custom_call" | custom-call | flops 536870912 | bytes 2089600 | tf_op jit(solution)/shard_map/pallas_call | solution.py:55
  89.0 5.3 %all-to-all-start = ((f32[128,1,128]{2,1,0:T(1,128)}), f32[128,1,128]{2,1,0:T(1,128)S(1)}, u32[]{:S(2)}, u32[]{:S(2)}) async-start(f32[128,1,128]{2,1,0:T(1,128)} %get-tuple-element.192), calls=%async_computation | async-start | bytes 131072 | tf_op jit(solution)/shard_map/all_to_all | solution.py:527
  95.1 1.4 %copy.13 = f32[288,2048]{1,0:T(8,128)} copy(f32[288,2048]{1,0:T(8,128)S(1)} %get-tuple-element.200) | data formatting | bytes 4718592
  96.5 7.3 %all-to-all-done = f32[128,1,128]{2,1,0:T(1,128)S(1)} async-done(((f32[128,1,128]{2,1,0:T(1,128)}), f32[128,1,128]{2,1,0:T(1,128)S(1)}, u32[]{:S(2)}, u32[]{:S(2)}) %all-to-all-start) | async-done | bytes 65568 | tf_op jit(solution)/shard_map/all_to_all | solution.py:527
  (95 shorter events, 21.3 us)
Async XLA Ops:
  6.4 12.0 %collective-permute-start.3 = (bf16[128,512]{1,0:T(8,128)(2,1)S(1)}, bf16[128,512]{1,0:T(8,128)(2,1)S(1)}, u32[]{:S(2)}, u32[]{:S(2)}) collective-permute-start(bf16[128,512]{1,0:T(8,128)(2,1)S(1)} %get-tuple-element.103), channel_id=1, source_target_pairs={{0,32},{1,9},{2,34},{3,11},{4,36},{5,13},{6,38},{7,15},{8,40},{9,1... | collective-permute-start | bytes 393224 | tf_op jit(solution)/shard_map/ppermute | solution.py:384
  8.9 10.7 %collective-permute-start.4 = (bf16[128,512]{1,0:T(8,128)(2,1)S(1)}, bf16[128,512]{1,0:T(8,128)(2,1)S(1)}, u32[]{:S(2)}, u32[]{:S(2)}) collective-permute-start(bf16[128,512]{1,0:T(8,128)(2,1)S(1)} %get-tuple-element.104), channel_id=1, source_target_pairs={{0,64},{1,17},{2,66},{3,19},{4,68},{5,21},{6,70},{7,23},{8,72},{9,... | collective-permute-start | bytes 393224 | tf_op jit(solution)/shard_map/ppermute | solution.py:384
  12.2 7.4 %collective-permute-start.5 = (bf16[128,512]{1,0:T(8,128)(2,1)S(1)}, bf16[128,512]{1,0:T(8,128)(2,1)S(1)}, u32[]{:S(2)}, u32[]{:S(2)}) collective-permute-start(bf16[128,512]{1,0:T(8,128)(2,1)S(1)} %get-tuple-element.105), channel_id=1, source_target_pairs={{0,96},{1,25},{2,98},{3,27},{4,100},{5,29},{6,102},{7,31},{8,104},... | collective-permute-start | bytes 393224 | tf_op jit(solution)/shard_map/ppermute | solution.py:384
  12.9 9.9 %collective-permute-start = (bf16[128,640]{1,0:T(8,128)(2,1)S(1)}, bf16[128,640]{1,0:T(8,128)(2,1)S(1)}, u32[]{:S(2)}, u32[]{:S(2)}) collective-permute-start(bf16[128,640]{1,0:T(8,128)(2,1)S(1)} %get-tuple-element.99), channel_id=1, source_target_pairs={{0,2},{1,3},{2,4},{3,5},{4,6},{5,7},{6,0},{7,1},{8,10},{9,11},{10,... | collective-permute-start | bytes 491528 | tf_op jit(solution)/shard_map/ppermute | solution.py:384
  14.1 12.4 %collective-permute-start.1 = (bf16[128,640]{1,0:T(8,128)(2,1)S(1)}, bf16[128,640]{1,0:T(8,128)(2,1)S(1)}, u32[]{:S(2)}, u32[]{:S(2)}) collective-permute-start(bf16[128,640]{1,0:T(8,128)(2,1)S(1)} %get-tuple-element.100), channel_id=1, source_target_pairs={{0,4},{1,5},{2,6},{3,7},{4,0},{5,1},{6,2},{7,3},{8,12},{9,13},{10,... | collective-permute-start | bytes 491528 | tf_op jit(solution)/shard_map/ppermute | solution.py:384
  18.4 8.2 %collective-permute-start.2 = (bf16[128,640]{1,0:T(8,128)(2,1)S(1)}, bf16[128,640]{1,0:T(8,128)(2,1)S(1)}, u32[]{:S(2)}, u32[]{:S(2)}) collective-permute-start(bf16[128,640]{1,0:T(8,128)(2,1)S(1)} %get-tuple-element.101), channel_id=1, source_target_pairs={{0,6},{1,7},{2,0},{3,1},{4,2},{5,3},{6,4},{7,5},{8,14},{9,15},{10,... | collective-permute-start | bytes 491528 | tf_op jit(solution)/shard_map/ppermute | solution.py:384
  19.7 6.9 %collective-permute-start.8 = (bf16[160,512]{1,0:T(8,128)(2,1)S(1)}, bf16[160,512]{1,0:T(8,128)(2,1)S(1)}, u32[]{:S(2)}, u32[]{:S(2)}) collective-permute-start(bf16[160,512]{1,0:T(8,128)(2,1)S(1)} %pad_maximum_fusion.4), channel_id=1, source_target_pairs={{0,24},{1,97},{2,26},{3,99},{4,28},{5,101},{6,30},{7,103},{8,0},{9... | collective-permute-start | bytes 491528 | tf_op jit(solution)/shard_map/ppermute | solution.py:384
  22.5 5.8 %collective-permute-start.7 = (bf16[160,512]{1,0:T(8,128)(2,1)S(1)}, bf16[160,512]{1,0:T(8,128)(2,1)S(1)}, u32[]{:S(2)}, u32[]{:S(2)}) collective-permute-start(bf16[160,512]{1,0:T(8,128)(2,1)S(1)} %pad_maximum_fusion.4), channel_id=1, source_target_pairs={{0,16},{1,65},{2,18},{3,67},{4,20},{5,69},{6,22},{7,71},{8,24},{9,... | collective-permute-start | bytes 491528 | tf_op jit(solution)/shard_map/ppermute | solution.py:384
  22.9 7.4 %collective-permute-start.6 = (bf16[160,512]{1,0:T(8,128)(2,1)S(1)}, bf16[160,512]{1,0:T(8,128)(2,1)S(1)}, u32[]{:S(2)}, u32[]{:S(2)}) collective-permute-start(bf16[160,512]{1,0:T(8,128)(2,1)S(1)} %pad_maximum_fusion.4), channel_id=1, source_target_pairs={{0,8},{1,33},{2,10},{3,35},{4,12},{5,37},{6,14},{7,39},{8,16},{9,4... | collective-permute-start | bytes 491528 | tf_op jit(solution)/shard_map/ppermute | solution.py:384
  30.2 4.8 %collective-permute-start.9 = (bf16[256,640]{1,0:T(8,128)(2,1)S(1)}, bf16[256,640]{1,0:T(8,128)(2,1)S(1)}, u32[]{:S(2)}, u32[]{:S(2)}) collective-permute-start(bf16[256,640]{1,0:T(8,128)(2,1)S(1)} %pad_maximum_fusion), channel_id=1, source_target_pairs={{0,1},{1,0},{2,3},{3,2},{4,5},{5,4},{6,7},{7,6},{8,9},{9,8},{10,11... | collective-permute-start | bytes 983048 | tf_op jit(solution)/shard_map/ppermute | solution.py:378
  35.8 4.8 %collective-permute-start.10 = (bf16[128,512]{1,0:T(8,128)(2,1)S(1)}, bf16[128,512]{1,0:T(8,128)(2,1)S(1)}, u32[]{:S(2)}, u32[]{:S(2)}) collective-permute-start(bf16[128,512]{1,0:T(8,128)(2,1)S(1)} %get-tuple-element.127), channel_id=1, source_target_pairs={{0,6},{1,7},{2,0},{3,1},{4,2},{5,3},{6,4},{7,5},{8,14},{9,15},{10,... | collective-permute-start | bytes 393224 | tf_op jit(solution)/shard_map/ppermute | solution.py:384
  35.9 7.3 %collective-permute-start.11 = (bf16[128,512]{1,0:T(8,128)(2,1)S(1)}, bf16[128,512]{1,0:T(8,128)(2,1)S(1)}, u32[]{:S(2)}, u32[]{:S(2)}) collective-permute-start(bf16[128,512]{1,0:T(8,128)(2,1)S(1)} %get-tuple-element.128), channel_id=1, source_target_pairs={{0,4},{1,5},{2,6},{3,7},{4,0},{5,1},{6,2},{7,3},{8,12},{9,13},{10,... | collective-permute-start | bytes 393224 | tf_op jit(solution)/shard_map/ppermute | solution.py:384
  38.0 7.2 %collective-permute-start.12 = (bf16[128,512]{1,0:T(8,128)(2,1)S(1)}, bf16[128,512]{1,0:T(8,128)(2,1)S(1)}, u32[]{:S(2)}, u32[]{:S(2)}) collective-permute-start(bf16[128,512]{1,0:T(8,128)(2,1)S(1)} %get-tuple-element.129), channel_id=1, source_target_pairs={{0,2},{1,3},{2,4},{3,5},{4,6},{5,7},{6,0},{7,1},{8,10},{9,11},{10,... | collective-permute-start | bytes 393224 | tf_op jit(solution)/shard_map/ppermute | solution.py:384
  38.0 7.3 %collective-permute-start.15 = (bf16[128,512]{1,0:T(8,128)(2,1)S(1)}, bf16[128,512]{1,0:T(8,128)(2,1)S(1)}, u32[]{:S(2)}, u32[]{:S(2)}) collective-permute-start(bf16[128,512]{1,0:T(8,128)(2,1)S(1)} %get-tuple-element.140.refs_1_.refs_0_), channel_id=1, source_target_pairs={{0,96},{1,25},{2,98},{3,27},{4,100},{5,29},{6,102},{7,31},{8,104},... | collective-permute-start | bytes 393224 | tf_op jit(solution)/shard_map/ppermute | solution.py:384
  38.6 6.7 %collective-permute-start.14 = (bf16[128,512]{1,0:T(8,128)(2,1)S(1)}, bf16[128,512]{1,0:T(8,128)(2,1)S(1)}, u32[]{:S(2)}, u32[]{:S(2)}) collective-permute-start(bf16[128,512]{1,0:T(8,128)(2,1)S(1)} %get-tuple-element.140.refs_1_.refs_0_), channel_id=1, source_target_pairs={{0,64},{1,17},{2,66},{3,19},{4,68},{5,21},{6,70},{7,23},{8,72},{9,... | collective-permute-start | bytes 393224 | tf_op jit(solution)/shard_map/ppermute | solution.py:384
  40.6 5.2 %collective-permute-start.13 = (bf16[128,512]{1,0:T(8,128)(2,1)S(1)}, bf16[128,512]{1,0:T(8,128)(2,1)S(1)}, u32[]{:S(2)}, u32[]{:S(2)}) collective-permute-start(bf16[128,512]{1,0:T(8,128)(2,1)S(1)} %get-tuple-element.140.refs_1_.refs_0_), channel_id=1, source_target_pairs={{0,32},{1,9},{2,34},{3,11},{4,36},{5,13},{6,38},{7,15},{8,40},{9,1... | collective-permute-start | bytes 393224 | tf_op jit(solution)/shard_map/ppermute | solution.py:384
  45.8 7.8 %collective-permute-start.16 = (bf16[256,512]{1,0:T(8,128)(2,1)S(1)}, bf16[256,512]{1,0:T(8,128)(2,1)S(1)}, u32[]{:S(2)}, u32[]{:S(2)}) collective-permute-start(bf16[256,512]{1,0:T(8,128)(2,1)S(1)} %pad_maximum_fusion.1), channel_id=1, source_target_pairs={{0,1},{1,0},{2,3},{3,2},{4,5},{5,4},{6,7},{7,6},{8,9},{9,8},{10,11... | collective-permute-start | bytes 786440 | tf_op jit(solution)/shard_map/ppermute | solution.py:378
  50.9 8.1 %collective-permute-start.20 = (bf16[128,512]{1,0:T(8,128)(2,1)S(1)}, bf16[128,512]{1,0:T(8,128)(2,1)S(1)}, u32[]{:S(2)}, u32[]{:S(2)}) collective-permute-start(bf16[128,512]{1,0:T(8,128)(2,1)S(1)} %get-tuple-element.153), channel_id=1, source_target_pairs={{0,32},{1,9},{2,34},{3,11},{4,36},{5,13},{6,38},{7,15},{8,40},{9,1... | collective-permute-start | bytes 393224 | tf_op jit(solution)/shard_map/ppermute | solution.py:384
  51.0 9.6 %collective-permute-start.21 = (bf16[128,512]{1,0:T(8,128)(2,1)S(1)}, bf16[128,512]{1,0:T(8,128)(2,1)S(1)}, u32[]{:S(2)}, u32[]{:S(2)}) collective-permute-start(bf16[128,512]{1,0:T(8,128)(2,1)S(1)} %get-tuple-element.154), channel_id=1, source_target_pairs={{0,64},{1,17},{2,66},{3,19},{4,68},{5,21},{6,70},{7,23},{8,72},{9,... | collective-permute-start | bytes 393224 | tf_op jit(solution)/shard_map/ppermute | solution.py:384
  52.7 7.8 %collective-permute-start.22 = (bf16[128,512]{1,0:T(8,128)(2,1)S(1)}, bf16[128,512]{1,0:T(8,128)(2,1)S(1)}, u32[]{:S(2)}, u32[]{:S(2)}) collective-permute-start(bf16[128,512]{1,0:T(8,128)(2,1)S(1)} %get-tuple-element.155), channel_id=1, source_target_pairs={{0,96},{1,25},{2,98},{3,27},{4,100},{5,29},{6,102},{7,31},{8,104},... | collective-permute-start | bytes 393224 | tf_op jit(solution)/shard_map/ppermute | solution.py:384
  55.7 6.4 %collective-permute-start.17 = (bf16[128,512]{1,0:T(8,128)(2,1)S(1)}, bf16[128,512]{1,0:T(8,128)(2,1)S(1)}, u32[]{:S(2)}, u32[]{:S(2)}) collective-permute-start(bf16[128,512]{1,0:T(8,128)(2,1)S(1)} %get-tuple-element.149), channel_id=1, source_target_pairs={{0,2},{1,3},{2,4},{3,5},{4,6},{5,7},{6,0},{7,1},{8,10},{9,11},{10,... | collective-permute-start | bytes 393224 | tf_op jit(solution)/shard_map/ppermute | solution.py:384
  58.0 7.0 %collective-permute-start.18 = (bf16[128,512]{1,0:T(8,128)(2,1)S(1)}, bf16[128,512]{1,0:T(8,128)(2,1)S(1)}, u32[]{:S(2)}, u32[]{:S(2)}) collective-permute-start(bf16[128,512]{1,0:T(8,128)(2,1)S(1)} %get-tuple-element.150), channel_id=1, source_target_pairs={{0,4},{1,5},{2,6},{3,7},{4,0},{5,1},{6,2},{7,3},{8,12},{9,13},{10,... | collective-permute-start | bytes 393224 | tf_op jit(solution)/shard_map/ppermute | solution.py:384
  58.9 6.1 %collective-permute-start.19 = (bf16[128,512]{1,0:T(8,128)(2,1)S(1)}, bf16[128,512]{1,0:T(8,128)(2,1)S(1)}, u32[]{:S(2)}, u32[]{:S(2)}) collective-permute-start(bf16[128,512]{1,0:T(8,128)(2,1)S(1)} %get-tuple-element.151), channel_id=1, source_target_pairs={{0,6},{1,7},{2,0},{3,1},{4,2},{5,3},{6,4},{7,5},{8,14},{9,15},{10,... | collective-permute-start | bytes 393224 | tf_op jit(solution)/shard_map/ppermute | solution.py:384
  60.8 5.4 %collective-permute-start.24 = (bf16[128,512]{1,0:T(8,128)(2,1)S(1)}, bf16[128,512]{1,0:T(8,128)(2,1)S(1)}, u32[]{:S(2)}, u32[]{:S(2)}) collective-permute-start(bf16[128,512]{1,0:T(8,128)(2,1)S(1)} %pad_maximum_fusion.5), channel_id=1, source_target_pairs={{0,16},{1,65},{2,18},{3,67},{4,20},{5,69},{6,22},{7,71},{8,24},{9,... | collective-permute-start | bytes 393224 | tf_op jit(solution)/shard_map/ppermute | solution.py:384
  62.0 5.8 %collective-permute-start.23 = (bf16[128,512]{1,0:T(8,128)(2,1)S(1)}, bf16[128,512]{1,0:T(8,128)(2,1)S(1)}, u32[]{:S(2)}, u32[]{:S(2)}) collective-permute-start(bf16[128,512]{1,0:T(8,128)(2,1)S(1)} %pad_maximum_fusion.5), channel_id=1, source_target_pairs={{0,8},{1,33},{2,10},{3,35},{4,12},{5,37},{6,14},{7,39},{8,16},{9,4... | collective-permute-start | bytes 393224 | tf_op jit(solution)/shard_map/ppermute | solution.py:384
  72.7 4.8 %collective-permute-start.27 = (bf16[128,512]{1,0:T(8,128)(2,1)S(1)}, bf16[128,512]{1,0:T(8,128)(2,1)S(1)}, u32[]{:S(2)}, u32[]{:S(2)}) collective-permute-start(bf16[128,512]{1,0:T(8,128)(2,1)S(1)} %get-tuple-element.178), channel_id=1, source_target_pairs={{0,6},{1,7},{2,0},{3,1},{4,2},{5,3},{6,4},{7,5},{8,14},{9,15},{10,... | collective-permute-start | bytes 393224 | tf_op jit(solution)/shard_map/ppermute | solution.py:384
  73.6 5.9 %collective-permute-start.28 = (bf16[128,512]{1,0:T(8,128)(2,1)S(1)}, bf16[128,512]{1,0:T(8,128)(2,1)S(1)}, u32[]{:S(2)}, u32[]{:S(2)}) collective-permute-start(bf16[128,512]{1,0:T(8,128)(2,1)S(1)} %get-tuple-element.179), channel_id=1, source_target_pairs={{0,4},{1,5},{2,6},{3,7},{4,0},{5,1},{6,2},{7,3},{8,12},{9,13},{10,... | collective-permute-start | bytes 393224 | tf_op jit(solution)/shard_map/ppermute | solution.py:384
  74.9 8.2 %collective-permute-start.29 = (bf16[128,512]{1,0:T(8,128)(2,1)S(1)}, bf16[128,512]{1,0:T(8,128)(2,1)S(1)}, u32[]{:S(2)}, u32[]{:S(2)}) collective-permute-start(bf16[128,512]{1,0:T(8,128)(2,1)S(1)} %get-tuple-element.180), channel_id=1, source_target_pairs={{0,2},{1,3},{2,4},{3,5},{4,6},{5,7},{6,0},{7,1},{8,10},{9,11},{10,... | collective-permute-start | bytes 393224 | tf_op jit(solution)/shard_map/ppermute | solution.py:384
  74.9 8.2 %collective-permute-start.32 = (bf16[128,512]{1,0:T(8,128)(2,1)S(1)}, bf16[128,512]{1,0:T(8,128)(2,1)S(1)}, u32[]{:S(2)}, u32[]{:S(2)}) collective-permute-start(bf16[128,512]{1,0:T(8,128)(2,1)S(1)} %get-tuple-element.186.refs_1_.refs_0_), channel_id=1, source_target_pairs={{0,96},{1,25},{2,98},{3,27},{4,100},{5,29},{6,102},{7,31},{8,104},... | collective-permute-start | bytes 393224 | tf_op jit(solution)/shard_map/ppermute | solution.py:384
  75.5 7.6 %collective-permute-start.31 = (bf16[128,512]{1,0:T(8,128)(2,1)S(1)}, bf16[128,512]{1,0:T(8,128)(2,1)S(1)}, u32[]{:S(2)}, u32[]{:S(2)}) collective-permute-start(bf16[128,512]{1,0:T(8,128)(2,1)S(1)} %get-tuple-element.186.refs_1_.refs_0_), channel_id=1, source_target_pairs={{0,64},{1,17},{2,66},{3,19},{4,68},{5,21},{6,70},{7,23},{8,72},{9,... | collective-permute-start | bytes 393224 | tf_op jit(solution)/shard_map/ppermute | solution.py:384
  77.5 5.7 %collective-permute-start.30 = (bf16[128,512]{1,0:T(8,128)(2,1)S(1)}, bf16[128,512]{1,0:T(8,128)(2,1)S(1)}, u32[]{:S(2)}, u32[]{:S(2)}) collective-permute-start(bf16[128,512]{1,0:T(8,128)(2,1)S(1)} %get-tuple-element.186.refs_1_.refs_0_), channel_id=1, source_target_pairs={{0,32},{1,9},{2,34},{3,11},{4,36},{5,13},{6,38},{7,15},{8,40},{9,1... | collective-permute-start | bytes 393224 | tf_op jit(solution)/shard_map/ppermute | solution.py:384
  89.0 14.8 %all-to-all-start = ((f32[128,1,128]{2,1,0:T(1,128)}), f32[128,1,128]{2,1,0:T(1,128)S(1)}, u32[]{:S(2)}, u32[]{:S(2)}) async-start(f32[128,1,128]{2,1,0:T(1,128)} %get-tuple-element.192), calls=%async_computation | async-start | bytes 131072 | tf_op jit(solution)/shard_map/all_to_all | solution.py:527
  (6 other events, 43.6 us)
where the time goes:
time: 107 us
  starting transfers between devices  47.9 us (45%)
  waiting for transfers between devices  26 us (24%)
  Pallas kernels  24 us (22%)
  local copies, waits for them, and re-layouts  4.42 us (4%)
  between operations  4.28 us (4%)
    ppermute x30, starting transfers between devices, shifted(): got[k] = lax.ppermute(blocks[k], *ring(sign * k % 4))  30.6 us
    pallas_call x15, Pallas kernels, call(): pl.pallas_call(kernel, out_shape=out_shapes, in_specs=[pl.BlockSpec(memor...  24 us
    ppermute x30, waiting for transfers between devices, shifted(): got[k] = lax.ppermute(blocks[k], *ring(sign * k % 4))  17.4 us
    ppermute x4, starting transfers between devices, sibling(): return lax.ppermute(array, *pairs_of(lambda y, z, x, c: (y, z, x, 1 - c)))  12 us
    all_to_all x1, waiting for transfers between devices, shards(): lax.all_to_all(load, ('leaf', 'node'), split_axis=0, concat_axis=0, tiled...  7.27 us
    all_to_all x1, starting transfers between devices, shards(): lax.all_to_all(load, ('leaf', 'node'), split_axis=0, concat_axis=0, tiled...  5.26 us
    unnamed x8, local copies, waits for them, and re-layouts  2.24 us
  transfers between devices with their start and end apart: 35, of which 13 were waited for; matrix products, arithmetic and copies ran while one was open for 3% of the time, Pallas kernels for 15%

commit v1 on v0

--- a/solution.py
+++ b/solution.py
@@ -67,7 +67,7 @@
     return [slice(i * TILE, (i + 1) * TILE) for i in range(NC // TILE)]
 
 
-def first(parent_of, section_of, y_far, linking_far, x_far, cost_far, *refs):
+def first(code, y_far, linking_far, x_far, cost_far, *refs):
     *outs, y, linking, ylow, nsend, nback, lsend, lback, scol, x_top, cost_top, state, sem = refs
     chunks = parts()
     copies = []
@@ -80,8 +80,9 @@
     copies = [pltpu.make_async_copy(a, b, sem.at[i]) for i, (a, b) in enumerate(copies)]
     for copy in copies:
         copy.start()
-    upper = section_of[...][:, ROWS] == 1
-    parent = parent_of[...][:, ROWS]
+    packed = code[...]
+    upper = (packed >> 16) == 1
+    parent = packed & 0xFFFF
     here = lax.axis_index("leaf") * N_NODE + lax.axis_index("node")
     owner = ((parent.astype(F32) + 0.5) * (1.0 / NODES)).astype(jnp.int32)
     local = parent - owner * NODES
@@ -385,21 +386,34 @@
     return [got[k] for k in range(4)]
 
 
-def swap_node(blocks, sign, before):
-    got = shifted(blocks, ring_x, sign)
+def swap_node(got, before):
     halves = jnp.concatenate([block[CAP_NODE:] for block in got], axis=0)
     halves, before = lax.optimization_barrier((halves, before))
     return got + [sibling(halves)], before
 
 
-def sum_leaf(blocks, own, state, before):
-    got, before = lax.optimization_barrier((shifted(blocks, outer_ring), before))
-    got = [block.astype(F32) for block in got]
-    total = ((got[0] + got[1]) + got[2]) + got[3]
+def ring_gather(rows, ring):
+    one = lax.ppermute(rows, *ring(1))
+    three = lax.ppermute(rows, *ring(3))
+    return [rows, one, lax.ppermute(one, *ring(1)), three]
+
+
+def ring_sum(blocks, ring, before, beside):
+    ahead = lax.ppermute(blocks[2], *ring(1))
+    behind = lax.ppermute(blocks[3], *ring(3))
+    (ahead, behind), before = lax.optimization_barrier(((ahead, behind), before))
+    ahead = (ahead.astype(F32) + blocks[1].astype(F32)).astype(BF16)
+    ahead = lax.ppermute(ahead, *ring(1))
+    ahead, beside = lax.optimization_barrier((ahead, beside))
+    return (blocks[0].astype(F32) + behind.astype(F32)) + ahead.astype(F32), before, beside
+
+
+def sum_leaf(blocks, own, state, before, beside):
+    total, before, beside = ring_sum(blocks, outer_ring, before, beside)
     sent = jnp.concatenate([total[:ROOTS] + own, total[ROOTS:]], axis=0).astype(BF16)
     if state is not None:
         sent = jnp.concatenate([sent, state], axis=0)
-    return [total.astype(BF16)] + shifted([sent] * 4, inner_ring)[1:], before
+    return [total.astype(BF16)] + ring_gather(sent, inner_ring)[1:], before, beside
 
 
 def part_of(kernel, flag):
@@ -411,6 +425,7 @@
 
 def shards(x_start, y_start, cost_vec, right_side, omega, coupling, linking, parent, section):
     unit = 2 * CHILD * NS * NC
+    code = (section * 65536 + parent)[ROOTS:].reshape(1, CHILD)
     rates = jnp.broadcast_to(jnp.stack([STEP / omega[0], STEP * omega[0]])[:, None], (2, 128))
     field = ((NODES, NC), F32)
     field_low = ((NODES, NC), BF16)
@@ -430,10 +445,10 @@
         first,
         [block_mark] * 4 + [block] * 4
         + [field, ((2, NC, NS), BF16), field_low, row, col, row, col, col, tops, tops, ((ROOTS, NS), BF16)],
-        [parent.reshape(1, NODES), section.reshape(1, NODES), y_start, linking, x_start, cost_vec],
+        [code, y_start, linking, x_start, cost_vec],
         2 * unit,
         [pltpu.SemaphoreType.DMA((3 * NC // TILE + 2,))],
-        (2, 3, 4, 5),
+        (1, 2, 3, 4),
     )
     chunk_sems = [pltpu.SemaphoreType.DMA((NC // TILE,))]
     own_root, coupling_root = call(
@@ -442,8 +457,9 @@
     own, coupling = call(
         own_first, [kids, ((2, NC, NS), BF16)], [ylow, scol, coupling], 2 * unit, chunk_sems, (2,)
     )
-    got_leaf, _ = sum_leaf(sent[4:], own_root, state, own_root)
-    got_node, (got_leaf, own) = swap_node(sent[:4], 1, (got_leaf, own))
+    got_node = shifted(sent[:4], ring_x, 1)
+    got_leaf, _, (own, got_node[1]) = sum_leaf(sent[4:], own_root, state, own_root, (own, got_node[1]))
+    got_node, got_leaf = swap_node(got_node, got_leaf)
 
     x_root, extra_root = call(
         root_first,
@@ -467,8 +483,8 @@
         ],
         2 * unit,
     )
-    back_leaf = shifted([extra_root] * 4, outer_ring)
-    back_node, (back_leaf, base) = swap_node(out_node, -1, (back_leaf, base))
+    back_leaf = ring_gather(extra_root, outer_ring)
+    back_node, (back_leaf, base) = swap_node(shifted(out_node, ring_x, -1), (back_leaf, base))
     later, *out_leaf = call(
         part_of(dual_leaf, False),
         [kids_field] + [block] * 4,
@@ -482,9 +498,10 @@
         2 * unit,
         held,
     )
-    got_leaf, ylow = sum_leaf(out_leaf, own_root, None, ylow)
     (own,) = call(own_adjoint, [kids], [ylow, scol, coupling], 2 * unit)
-    got_node, (got_leaf, own) = swap_node(out_node, 1, (got_leaf, own))
+    got_node = shifted(out_node, ring_x, 1)
+    got_leaf, ylow, (own, got_node[1]) = sum_leaf(out_leaf, own_root, None, ylow, (own, got_node[1]))
+    got_node, got_leaf = swap_node(got_node, got_leaf)
 
     extra_root, x_top = call(
         root_second,
@@ -512,8 +529,8 @@
         [extra_child, extra_root, scol, coupling_root, coupling, y_next, right_side, rates, cost_top],
         2 * unit,
     )
-    back_leaf = shifted([extra_root] * 4, outer_ring)
-    back_node, (back_leaf, base) = swap_node(out_node, -1, (back_leaf, base))
+    back_leaf = ring_gather(extra_root, outer_ring)
+    back_node, (back_leaf, base) = swap_node(shifted(out_node, ring_x, -1), (back_leaf, base))
     (later,) = call(
         part_of(dual_leaf, True), [kids_field], back_leaf + [lback, linking, base, rates], unit
     )

time: 107 us -> 113 us (1.056)
  waiting for transfers between devices: 26 us -> 32 us
  local copies, waits for them, and re-layouts: 4.42 us -> 3.12 us
    ppermute x0 -> x18, starting transfers between devices: none -> 17.9 us  [the longest x4 8.45 us: ring_gather(): three = lax.ppermute(rows, *ring(3))]
    ppermute x30 -> x12, starting transfers between devices: 30.6 us -> 14.6 us  [shifted(): got[k] = lax.ppermute(blocks[k], *ring(sign * k % 4))]
    ppermute x0 -> x18, waiting for transfers between devices: none -> 9.39 us  [the longest x4 5.68 us: ring_gather(): return [rows, one, lax.ppermute(one, *ring(1)), three]]
    ppermute x30 -> x12, waiting for transfers between devices: 17.4 us -> 14.2 us  [shifted(): got[k] = lax.ppermute(blocks[k], *ring(sign * k % 4))]
    reshape x2 -> x0, local copies, waits for them, and re-layouts: 1.37 us -> none  [the longest x1 0.68 us: shards(): parent.reshape(1, NODES)]
  transfers between devices with their start and end apart: 35 -> 35, of which waited for: 13 -> 17; matrix products, arithmetic and copies ran while one was open for 3% -> 2% of each run, Pallas kernels for 15% -> 16%
where the time goes in v1:
time: 113 us
  starting transfers between devices  48.6 us (43%)
  waiting for transfers between devices  32 us (28%)
  Pallas kernels  23.9 us (21%)
  between operations  4.27 us (4%)
  local copies, waits for them, and re-layouts  3.12 us (3%)
  other arithmetic  1.26 us (1%)
    pallas_call x15, Pallas kernels, call(): pl.pallas_call(kernel, out_shape=out_shapes, in_specs=[pl.BlockSpec(memor...  23.9 us
    ppermute x12, starting transfers between devices, shifted(): got[k] = lax.ppermute(blocks[k], *ring(sign * k % 4))  14.6 us
    ppermute x12, waiting for transfers between devices, shifted(): got[k] = lax.ppermute(blocks[k], *ring(sign * k % 4))  14.2 us
    ppermute x4, starting transfers between devices, sibling(): return lax.ppermute(array, *pairs_of(lambda y, z, x, c: (y, z, x, 1 - c)))  11.3 us
    ppermute x4, starting transfers between devices, ring_gather(): three = lax.ppermute(rows, *ring(3))  8.45 us
    all_to_all x1, waiting for transfers between devices, shards(): lax.all_to_all(load, ('leaf', 'node'), split_axis=0, concat_axis=0, tiled...  7.27 us
    ppermute x4, waiting for transfers between devices, ring_gather(): return [rows, one, lax.ppermute(one, *ring(1)), three]  5.68 us
    ppermute x2, starting transfers between devices, ring_sum(): behind = lax.ppermute(blocks[3], *ring(3))  4.87 us
  transfers between devices with their start and end apart: 35, of which 17 were waited for; matrix products, arithmetic and copies ran while one was open for 2% of the time, Pallas kernels for 16%

profile of v1, /device:TPU:1, one launch (start us, length us, event | category | flops | bytes accessed | tf_op | source)
XLA Modules:
  0.0 113.1 jit_solution(5892012547389715537)
XLA Ops:
  1.4 4.2 %shard_map.112 = (bf16[128,640]{1,0:T(8,128)(2,1)S(1)}, bf16[128,640]{1,0:T(8,128)(2,1)S(1)}, bf16[128,640]{1,0:T(8,128)(2,1)S(1)}, bf16[128,640]{1,0:T(8,128)(2...) custom-call(s32[1,256]{1,0:T(1,128)S(1)} %bitcast.1, ...), custom_call_target="tpu_custom_call" | custom-call | flops 1073741824 | bytes 2150784 | tf_op jit(solution)/shard_map/pallas_call | solution.py:55
  5.7 2.5 %collective-permute-start = (bf16[128,512]{1,0:T(8,128)(2,1)S(1)}, bf16[128,512]{1,0:T(8,128)(2,1)S(1)}, u32[]{:S(2)}, u32[]{:S(2)}) collective-permute-start(bf16[128,512]{1,0:T(8,128)(2,1)S(1)} %get-tuple-element.98), channel_id=1, source_target_pairs={{0,32},{1,9},{2,34},{3,11},{4,36},{5,13},{6,38},{7,15},{8,40},{9,1... | collective-permute-start | bytes 393224 | tf_op jit(solution)/shard_map/ppermute | solution.py:402
  8.2 2.2 %collective-permute-start.1 = (bf16[128,512]{1,0:T(8,128)(2,1)S(1)}, bf16[128,512]{1,0:T(8,128)(2,1)S(1)}, u32[]{:S(2)}, u32[]{:S(2)}) collective-permute-start(bf16[128,512]{1,0:T(8,128)(2,1)S(1)} %get-tuple-element.99), channel_id=1, source_target_pairs={{0,96},{1,25},{2,98},{3,27},{4,100},{5,29},{6,102},{7,31},{8,104},... | collective-permute-start | bytes 393224 | tf_op jit(solution)/shard_map/ppermute | solution.py:403
  11.6 1.7 %shard_map.113 = (f32[32,512]{1,0:T(8,128)S(1)}, bf16[2048,512]{1,0:T(8,128)(2,1)S(1)}) custom-call(bf16[288,2048]{1,0:T(8,128)(2,1)S(1)} %get-tuple-element.100.ylow, f32[32,512]{1,0:T(8,128)S(1)} %get-tuple-element.101.cost_top.refs_8_, bf16[3,2048,512]{2,1,0:T(8,128)(2,1)} %coupling_far.3), custom_call_target="tpu_custom_call" | custom-call | flops 67108864 | bytes 1212416 | tf_op jit(solution)/shard_map/pallas_call | solution.py:55
  14.1 2.9 %shard_map.114 = (f32[256,512]{1,0:T(8,128)S(1)}, bf16[2,2048,512]{2,1,0:T(8,128)(2,1)S(1)}) custom-call(bf16[288,2048]{1,0:T(8,128)(2,1)S(1)} %get-tuple-element.100.ylow, f32[256,128]{1,0:T(8,128)S(1)} %get-tuple-element.105.scol.refs_2_, bf16[3,2048,512]{2,1,0:T(8,128)(2,1)} %coupling_far.3), custom_call_target="tpu_custom_call" | custom-call | flops 1073741824 | bytes 1540096 | tf_op jit(solution)/shard_map/pallas_call | solution.py:55
  20.0 2.5 %collective-permute-start.4 = (bf16[128,640]{1,0:T(8,128)(2,1)S(1)}, bf16[128,640]{1,0:T(8,128)(2,1)S(1)}, u32[]{:S(2)}, u32[]{:S(2)}) collective-permute-start(bf16[128,640]{1,0:T(8,128)(2,1)S(1)} %get-tuple-element.109), channel_id=1, source_target_pairs={{0,4},{1,5},{2,6},{3,7},{4,0},{5,1},{6,2},{7,3},{8,12},{9,13},{10,... | collective-permute-start | bytes 491528 | tf_op jit(solution)/shard_map/ppermute | solution.py:385
  23.6 1.7 %collective-permute-start.8 = (bf16[160,512]{1,0:T(8,128)(2,1)S(1)}, bf16[160,512]{1,0:T(8,128)(2,1)S(1)}, u32[]{:S(2)}, u32[]{:S(2)}) collective-permute-start(bf16[160,512]{1,0:T(8,128)(2,1)S(1)} %pad_maximum_fusion.4), channel_id=1, source_target_pairs={{0,24},{1,97},{2,26},{3,99},{4,28},{5,101},{6,30},{7,103},{8,0},{9... | collective-permute-start | bytes 491528 | tf_op jit(solution)/shard_map/ppermute | solution.py:397
  25.7 1.7 %collective-permute-done.5.g3 = bf16[128,640]{1,0:T(8,128)(2,1)S(1)} collective-permute-done((bf16[128,640]{1,0:T(8,128)(2,1)S(1)}, bf16[128,640]{1,0:T(8,128)(2,1)S(1)}, u32[]{:S(2)}, u32[]{:S(2)}) %collective-permute-start.5) | collective-permute-done | bytes 163872 | tf_op jit(solution)/shard_map/ppermute | solution.py:385
  28.1 2.6 %collective-permute-done.7.g2 = bf16[160,512]{1,0:T(8,128)(2,1)S(1)} collective-permute-done((bf16[160,512]{1,0:T(8,128)(2,1)S(1)}, bf16[160,512]{1,0:T(8,128)(2,1)S(1)}, u32[]{:S(2)}, u32[]{:S(2)}) %collective-permute-start.7) | collective-permute-done | bytes 163872 | tf_op jit(solution)/shard_map/ppermute | solution.py:398
  30.7 4.4 %collective-permute-start.9 = (bf16[256,640]{1,0:T(8,128)(2,1)S(1)}, bf16[256,640]{1,0:T(8,128)(2,1)S(1)}, u32[]{:S(2)}, u32[]{:S(2)}) collective-permute-start(bf16[256,640]{1,0:T(8,128)(2,1)S(1)} %pad_maximum_fusion), channel_id=1, source_target_pairs={{0,1},{1,0},{2,3},{3,2},{4,5},{5,4},{6,7},{7,6},{8,9},{9,8},{10,11... | collective-permute-start | bytes 983048 | tf_op jit(solution)/shard_map/ppermute | solution.py:379
  37.1 1.6 %collective-permute-start.10 = (bf16[128,512]{1,0:T(8,128)(2,1)S(1)}, bf16[128,512]{1,0:T(8,128)(2,1)S(1)}, u32[]{:S(2)}, u32[]{:S(2)}) collective-permute-start(bf16[128,512]{1,0:T(8,128)(2,1)S(1)} %get-tuple-element.126), channel_id=1, source_target_pairs={{0,6},{1,7},{2,0},{3,1},{4,2},{5,3},{6,4},{7,5},{8,14},{9,15},{10,... | collective-permute-start | bytes 393224 | tf_op jit(solution)/shard_map/ppermute | solution.py:385
  39.8 2.5 %collective-permute-start.15 = (bf16[128,512]{1,0:T(8,128)(2,1)S(1)}, bf16[128,512]{1,0:T(8,128)(2,1)S(1)}, u32[]{:S(2)}, u32[]{:S(2)}) collective-permute-start(bf16[128,512]{1,0:T(8,128)(2,1)S(1)} %get-tuple-element.139.refs_1_.refs_0_), channel_id=1, source_target_pairs={{0,96},{1,25},{2,98},{3,27},{4,100},{5,29},{6,102},{7,31},{8,104},... | collective-permute-start | bytes 393224 | tf_op jit(solution)/shard_map/ppermute | solution.py:397
  42.3 2.6 %shard_map.117 = (f32[288,2048]{1,0:T(8,128)S(1)}, f32[32,512]{1,0:T(8,128)S(1)}) custom-call(bf16[256,512]{1,0:T(8,128)(2,1)S(1)} %get-tuple-element.130.refs_0_, bf16[128,512]{1,0:T(8,128)(2,1)S(1)} %get-tuple-element.139.refs_1_.refs_0_, f32[256,128]{1,0:T(8,128)S(1)} %get-tuple-element.105.scol.refs_2_, ...), custom_call_target="tpu_custom_call" | custom-call | flops 1073741824 | bytes 1753216 | tf_op jit(solution)/shard_map/pallas_call | solution.py:55
  44.9 3.4 %collective-permute-done.12.g3 = bf16[128,512]{1,0:T(8,128)(2,1)S(1)} collective-permute-done((bf16[128,512]{1,0:T(8,128)(2,1)S(1)}, bf16[128,512]{1,0:T(8,128)(2,1)S(1)}, u32[]{:S(2)}, u32[]{:S(2)}) %collective-permute-start.12) | collective-permute-done | bytes 131104 | tf_op jit(solution)/shard_map/ppermute | solution.py:385
  48.4 1.5 %collective-permute-start.16 = (bf16[256,512]{1,0:T(8,128)(2,1)S(1)}, bf16[256,512]{1,0:T(8,128)(2,1)S(1)}, u32[]{:S(2)}, u32[]{:S(2)}) collective-permute-start(bf16[256,512]{1,0:T(8,128)(2,1)S(1)} %pad_maximum_fusion.1), channel_id=1, source_target_pairs={{0,1},{1,0},{2,3},{3,2},{4,5},{5,4},{6,7},{7,6},{8,9},{9,8},{10,11... | collective-permute-start | bytes 786440 | tf_op jit(solution)/shard_map/ppermute | solution.py:379
  49.9 2.1 %shard_map.118 = (f32[256,2048]{1,0:T(8,128)S(1)}, bf16[128,512]{1,0:T(8,128)(2,1)S(1)}, bf16[128,512]{1,0:T(8,128)(2,1)S(1)}, bf16[128,512]{1,0:T(8,128)(2,1)S(1)}, bf16[128,512]{1,0:T(8,128)(2,1)S(1)}) custom-call(bf16[128,512]{1,0:T(8,128)(2,1)S(1)} %get-tuple-element.139.refs_1_.refs_0_, bf16[128,512]{1,0:T(8,128)(2,1)S(1)} %collective-permute-done.13.refs_1_, ...), custom_call_target="tpu_custom_call" | custom-call | flops 1073741824 | bytes 1229056 | tf_op jit(solution)/shard_map/pallas_call | solution.py:55
  52.1 2.7 %collective-permute-start.18 = (bf16[128,512]{1,0:T(8,128)(2,1)S(1)}, bf16[128,512]{1,0:T(8,128)(2,1)S(1)}, u32[]{:S(2)}, u32[]{:S(2)}) collective-permute-start(bf16[128,512]{1,0:T(8,128)(2,1)S(1)} %get-tuple-element.149), channel_id=1, source_target_pairs={{0,96},{1,25},{2,98},{3,27},{4,100},{5,29},{6,102},{7,31},{8,104},... | collective-permute-start | bytes 393224 | tf_op jit(solution)/shard_map/ppermute | solution.py:403
  54.7 2.0 %shard_map.119 = (f32[288,2048]{1,0:T(8,128)S(1)}, bf16[288,2048]{1,0:T(8,128)(2,1)S(1)}, bf16[128,512]{1,0:T(8,128)(2,1)S(1)}, bf16[128,512]{1,0:T(8,128)(2,1)S...) custom-call(bf16[128,512]{1,0:T(8,128)(2,1)S(1)} %get-tuple-element.125.g0, ...), custom_call_target="tpu_custom_call" | custom-call | flops 1073741824 | bytes 1704192 | tf_op jit(solution)/shard_map/pallas_call | solution.py:55
  56.8 1.6 %collective-permute-start.20 = (bf16[128,512]{1,0:T(8,128)(2,1)S(1)}, bf16[128,512]{1,0:T(8,128)(2,1)S(1)}, u32[]{:S(2)}, u32[]{:S(2)}) collective-permute-start(bf16[128,512]{1,0:T(8,128)(2,1)S(1)} %get-tuple-element.153), channel_id=1, source_target_pairs={{0,2},{1,3},{2,4},{3,5},{4,6},{5,7},{6,0},{7,1},{8,10},{9,11},{10,... | collective-permute-start | bytes 393224 | tf_op jit(solution)/shard_map/ppermute | solution.py:385
  59.7 2.8 %collective-permute-done.20.g1 = bf16[128,512]{1,0:T(8,128)(2,1)S(1)} collective-permute-done((bf16[128,512]{1,0:T(8,128)(2,1)S(1)}, bf16[128,512]{1,0:T(8,128)(2,1)S(1)}, u32[]{:S(2)}, u32[]{:S(2)}) %collective-permute-start.20) | collective-permute-done | bytes 131104 | tf_op jit(solution)/shard_map/ppermute | solution.py:385
  64.0 2.2 %collective-permute-start.21 = (bf16[128,512]{1,0:T(8,128)(2,1)S(1)}, bf16[128,512]{1,0:T(8,128)(2,1)S(1)}, u32[]{:S(2)}, u32[]{:S(2)}) collective-permute-start(bf16[128,512]{1,0:T(8,128)(2,1)S(1)} %get-tuple-element.155), channel_id=1, source_target_pairs={{0,4},{1,5},{2,6},{3,7},{4,0},{5,1},{6,2},{7,3},{8,12},{9,13},{10,... | collective-permute-start | bytes 393224 | tf_op jit(solution)/shard_map/ppermute | solution.py:385
  67.0 2.6 %collective-permute-start.25 = (bf16[128,512]{1,0:T(8,128)(2,1)S(1)}, bf16[128,512]{1,0:T(8,128)(2,1)S(1)}, u32[]{:S(2)}, u32[]{:S(2)}) collective-permute-start(bf16[128,512]{1,0:T(8,128)(2,1)S(1)} %pad_maximum_fusion.5), channel_id=1, source_target_pairs={{0,24},{1,97},{2,26},{3,99},{4,28},{5,101},{6,30},{7,103},{8,0},{9... | collective-permute-start | bytes 393224 | tf_op jit(solution)/shard_map/ppermute | solution.py:397
  71.6 3.1 %collective-permute-done.24.g2 = bf16[128,512]{1,0:T(8,128)(2,1)S(1)} collective-permute-done((bf16[128,512]{1,0:T(8,128)(2,1)S(1)}, bf16[128,512]{1,0:T(8,128)(2,1)S(1)}, u32[]{:S(2)}, u32[]{:S(2)}) %collective-permute-start.24) | collective-permute-done | bytes 131104 | tf_op jit(solution)/shard_map/ppermute | solution.py:398
  74.7 4.0 %collective-permute-start.26 = (bf16[256,512]{1,0:T(8,128)(2,1)S(1)}, bf16[256,512]{1,0:T(8,128)(2,1)S(1)}, u32[]{:S(2)}, u32[]{:S(2)}) collective-permute-start(bf16[256,512]{1,0:T(8,128)(2,1)S(1)} %pad_maximum_fusion.2), channel_id=1, source_target_pairs={{0,1},{1,0},{2,3},{3,2},{4,5},{5,4},{6,7},{7,6},{8,9},{9,8},{10,11... | collective-permute-start | bytes 786440 | tf_op jit(solution)/shard_map/ppermute | solution.py:379
  81.4 1.5 %collective-permute-start.28 = (bf16[128,512]{1,0:T(8,128)(2,1)S(1)}, bf16[128,512]{1,0:T(8,128)(2,1)S(1)}, u32[]{:S(2)}, u32[]{:S(2)}) collective-permute-start(bf16[128,512]{1,0:T(8,128)(2,1)S(1)} %get-tuple-element.177), channel_id=1, source_target_pairs={{0,4},{1,5},{2,6},{3,7},{4,0},{5,1},{6,2},{7,3},{8,12},{9,13},{10,... | collective-permute-start | bytes 393224 | tf_op jit(solution)/shard_map/ppermute | solution.py:385
  82.9 1.7 %collective-permute-start.32 = (bf16[128,512]{1,0:T(8,128)(2,1)S(1)}, bf16[128,512]{1,0:T(8,128)(2,1)S(1)}, u32[]{:S(2)}, u32[]{:S(2)}) collective-permute-start(bf16[128,512]{1,0:T(8,128)(2,1)S(1)} %get-tuple-element.184.refs_1_.refs_0_), channel_id=1, source_target_pairs={{0,96},{1,25},{2,98},{3,27},{4,100},{5,29},{6,102},{7,31},{8,104},... | collective-permute-start | bytes 393224 | tf_op jit(solution)/shard_map/ppermute | solution.py:397
  84.6 2.0 %shard_map.124.refs_6_.base = f32[288,2048]{1,0:T(8,128)S(1)} custom-call(bf16[256,512]{1,0:T(8,128)(2,1)S(1)} %get-tuple-element.180.refs_0_, bf16[128,512]{1,0:T(8,128)(2,1)S(1)} %get-tuple-element.184.refs_1_.refs_0_, f32[256,128]{1,0:T(8,128)S(1)} %get-tuple-element.105.scol.refs_2_, bf16[2048,512]{1,0:T(8,128)(2,1)S(1)} %get-tuple-element.131.refs_3_, ...), custom_call_target="tpu_custom_call" | custom-call | flops 1073741824 | bytes 1745024 | tf_op jit(solution)/shard_map/pallas_call | solution.py:55
  87.3 3.4 %collective-permute-done.29.g3 = bf16[128,512]{1,0:T(8,128)(2,1)S(1)} collective-permute-done((bf16[128,512]{1,0:T(8,128)(2,1)S(1)}, bf16[128,512]{1,0:T(8,128)(2,1)S(1)}, u32[]{:S(2)}, u32[]{:S(2)}) %collective-permute-start.29) | collective-permute-done | bytes 131104 | tf_op jit(solution)/shard_map/ppermute | solution.py:385
  90.8 1.4 %collective-permute-start.33 = (bf16[256,512]{1,0:T(8,128)(2,1)S(1)}, bf16[256,512]{1,0:T(8,128)(2,1)S(1)}, u32[]{:S(2)}, u32[]{:S(2)}) collective-permute-start(bf16[256,512]{1,0:T(8,128)(2,1)S(1)} %pad_maximum_fusion.3), channel_id=1, source_target_pairs={{0,1},{1,0},{2,3},{3,2},{4,5},{5,4},{6,7},{7,6},{8,9},{9,8},{10,11... | collective-permute-start | bytes 786440 | tf_op jit(solution)/shard_map/ppermute | solution.py:379
  93.6 2.0 %shard_map.126 = (f32[288,2048]{1,0:T(8,128)S(1)}, f32[128,1,128]{2,1,0:T(1,128)}) custom-call(bf16[128,512]{1,0:T(8,128)(2,1)S(1)} %get-tuple-element.175.g0, bf16[128,512]{1,0:T(8,128)(2,1)S(1)} %collective-permute-done.27.g1, bf16[128,512]{1,0:T(8,128)(2,1)S(1)} %collective-permute-done.28.g2, bf16[128,512]{1,0:T(8,128)(2,1)S(1)} %collective-permute-done.29.g3, ...), custom_call_target="tpu_custom_call" | custom-call | flops 536870912 | bytes 2089600 | tf_op jit(solution)/shard_map/pallas_call | solution.py:55
  95.6 4.8 %all-to-all-start = ((f32[128,1,128]{2,1,0:T(1,128)}), f32[128,1,128]{2,1,0:T(1,128)S(1)}, u32[]{:S(2)}, u32[]{:S(2)}) async-start(f32[128,1,128]{2,1,0:T(1,128)} %get-tuple-element.190), calls=%async_computation | async-start | bytes 131072 | tf_op jit(solution)/shard_map/all_to_all | solution.py:544
  102.6 7.3 %all-to-all-done = f32[128,1,128]{2,1,0:T(1,128)S(1)} async-done(((f32[128,1,128]{2,1,0:T(1,128)}), f32[128,1,128]{2,1,0:T(1,128)S(1)}, u32[]{:S(2)}, u32[]{:S(2)}) %all-to-all-start) | async-done | bytes 65568 | tf_op jit(solution)/shard_map/all_to_all | solution.py:544
  (97 shorter events, 23.8 us)
Async XLA Ops:
  5.7 7.7 %collective-permute-start = (bf16[128,512]{1,0:T(8,128)(2,1)S(1)}, bf16[128,512]{1,0:T(8,128)(2,1)S(1)}, u32[]{:S(2)}, u32[]{:S(2)}) collective-permute-start(bf16[128,512]{1,0:T(8,128)(2,1)S(1)} %get-tuple-element.98), channel_id=1, source_target_pairs={{0,32},{1,9},{2,34},{3,11},{4,36},{5,13},{6,38},{7,15},{8,40},{9,1... | collective-permute-start | bytes 393224 | tf_op jit(solution)/shard_map/ppermute | solution.py:402
  8.2 5.2 %collective-permute-start.1 = (bf16[128,512]{1,0:T(8,128)(2,1)S(1)}, bf16[128,512]{1,0:T(8,128)(2,1)S(1)}, u32[]{:S(2)}, u32[]{:S(2)}) collective-permute-start(bf16[128,512]{1,0:T(8,128)(2,1)S(1)} %get-tuple-element.99), channel_id=1, source_target_pairs={{0,96},{1,25},{2,98},{3,27},{4,100},{5,29},{6,102},{7,31},{8,104},... | collective-permute-start | bytes 393224 | tf_op jit(solution)/shard_map/ppermute | solution.py:403
  10.4 7.1 %collective-permute-start.3 = (bf16[128,640]{1,0:T(8,128)(2,1)S(1)}, bf16[128,640]{1,0:T(8,128)(2,1)S(1)}, u32[]{:S(2)}, u32[]{:S(2)}) collective-permute-start(bf16[128,640]{1,0:T(8,128)(2,1)S(1)} %get-tuple-element.107), channel_id=1, source_target_pairs={{0,2},{1,3},{2,4},{3,5},{4,6},{5,7},{6,0},{7,1},{8,10},{9,11},{10,... | collective-permute-start | bytes 491528 | tf_op jit(solution)/shard_map/ppermute | solution.py:385
  13.4 5.4 %collective-permute-start.2 = (bf16[128,512]{1,0:T(8,128)(2,1)S(1)}, bf16[128,512]{1,0:T(8,128)(2,1)S(1)}, u32[]{:S(2)}, u32[]{:S(2)}) collective-permute-start(bf16[128,512]{1,0:T(8,128)(2,1)S(1)} %add_convert_fusion.1), channel_id=1, source_target_pairs={{0,32},{1,9},{2,34},{3,11},{4,36},{5,13},{6,38},{7,15},{8,40},{9,1... | collective-permute-start | bytes 393224 | tf_op jit(solution)/shard_map/ppermute | solution.py:406
  19.0 6.4 %collective-permute-start.6 = (bf16[160,512]{1,0:T(8,128)(2,1)S(1)}, bf16[160,512]{1,0:T(8,128)(2,1)S(1)}, u32[]{:S(2)}, u32[]{:S(2)}) collective-permute-start(bf16[160,512]{1,0:T(8,128)(2,1)S(1)} %pad_maximum_fusion.4), channel_id=1, source_target_pairs={{0,8},{1,33},{2,10},{3,35},{4,12},{5,37},{6,14},{7,39},{8,16},{9,4... | collective-permute-start | bytes 491528 | tf_op jit(solution)/shard_map/ppermute | solution.py:396
  20.0 5.7 %collective-permute-start.4 = (bf16[128,640]{1,0:T(8,128)(2,1)S(1)}, bf16[128,640]{1,0:T(8,128)(2,1)S(1)}, u32[]{:S(2)}, u32[]{:S(2)}) collective-permute-start(bf16[128,640]{1,0:T(8,128)(2,1)S(1)} %get-tuple-element.109), channel_id=1, source_target_pairs={{0,4},{1,5},{2,6},{3,7},{4,0},{5,1},{6,2},{7,3},{8,12},{9,13},{10,... | collective-permute-start | bytes 491528 | tf_op jit(solution)/shard_map/ppermute | solution.py:385
  22.5 4.9 %collective-permute-start.5 = (bf16[128,640]{1,0:T(8,128)(2,1)S(1)}, bf16[128,640]{1,0:T(8,128)(2,1)S(1)}, u32[]{:S(2)}, u32[]{:S(2)}) collective-permute-start(bf16[128,640]{1,0:T(8,128)(2,1)S(1)} %get-tuple-element.110), channel_id=1, source_target_pairs={{0,6},{1,7},{2,0},{3,1},{4,2},{5,3},{6,4},{7,5},{8,14},{9,15},{10,... | collective-permute-start | bytes 491528 | tf_op jit(solution)/shard_map/ppermute | solution.py:385
  25.3 5.4 %collective-permute-start.7 = (bf16[160,512]{1,0:T(8,128)(2,1)S(1)}, bf16[160,512]{1,0:T(8,128)(2,1)S(1)}, u32[]{:S(2)}, u32[]{:S(2)}) collective-permute-start(bf16[160,512]{1,0:T(8,128)(2,1)S(1)} %collective-permute-done.6.g1), channel_id=1, source_target_pairs={{0,8},{1,33},{2,10},{3,35},{4,12},{5,37},{6,14},{7,39},{8,16},{9,4... | collective-permute-start | bytes 491528 | tf_op jit(solution)/shard_map/ppermute | solution.py:398
  30.7 5.7 %collective-permute-start.9 = (bf16[256,640]{1,0:T(8,128)(2,1)S(1)}, bf16[256,640]{1,0:T(8,128)(2,1)S(1)}, u32[]{:S(2)}, u32[]{:S(2)}) collective-permute-start(bf16[256,640]{1,0:T(8,128)(2,1)S(1)} %pad_maximum_fusion), channel_id=1, source_target_pairs={{0,1},{1,0},{2,3},{3,2},{4,5},{5,4},{6,7},{7,6},{8,9},{9,8},{10,11... | collective-permute-start | bytes 983048 | tf_op jit(solution)/shard_map/ppermute | solution.py:379
  36.1 6.2 %collective-permute-start.13 = (bf16[128,512]{1,0:T(8,128)(2,1)S(1)}, bf16[128,512]{1,0:T(8,128)(2,1)S(1)}, u32[]{:S(2)}, u32[]{:S(2)}) collective-permute-start(bf16[128,512]{1,0:T(8,128)(2,1)S(1)} %get-tuple-element.139.refs_1_.refs_0_), channel_id=1, source_target_pairs={{0,32},{1,9},{2,34},{3,11},{4,36},{5,13},{6,38},{7,15},{8,40},{9,1... | collective-permute-start | bytes 393224 | tf_op jit(solution)/shard_map/ppermute | solution.py:396
  37.1 7.8 %collective-permute-start.10 = (bf16[128,512]{1,0:T(8,128)(2,1)S(1)}, bf16[128,512]{1,0:T(8,128)(2,1)S(1)}, u32[]{:S(2)}, u32[]{:S(2)}) collective-permute-start(bf16[128,512]{1,0:T(8,128)(2,1)S(1)} %get-tuple-element.126), channel_id=1, source_target_pairs={{0,6},{1,7},{2,0},{3,1},{4,2},{5,3},{6,4},{7,5},{8,14},{9,15},{10,... | collective-permute-start | bytes 393224 | tf_op jit(solution)/shard_map/ppermute | solution.py:385
  38.7 6.2 %collective-permute-start.11 = (bf16[128,512]{1,0:T(8,128)(2,1)S(1)}, bf16[128,512]{1,0:T(8,128)(2,1)S(1)}, u32[]{:S(2)}, u32[]{:S(2)}) collective-permute-start(bf16[128,512]{1,0:T(8,128)(2,1)S(1)} %get-tuple-element.127), channel_id=1, source_target_pairs={{0,4},{1,5},{2,6},{3,7},{4,0},{5,1},{6,2},{7,3},{8,12},{9,13},{10,... | collective-permute-start | bytes 393224 | tf_op jit(solution)/shard_map/ppermute | solution.py:385
  39.6 8.8 %collective-permute-start.12 = (bf16[128,512]{1,0:T(8,128)(2,1)S(1)}, bf16[128,512]{1,0:T(8,128)(2,1)S(1)}, u32[]{:S(2)}, u32[]{:S(2)}) collective-permute-start(bf16[128,512]{1,0:T(8,128)(2,1)S(1)} %get-tuple-element.128), channel_id=1, source_target_pairs={{0,2},{1,3},{2,4},{3,5},{4,6},{5,7},{6,0},{7,1},{8,10},{9,11},{10,... | collective-permute-start | bytes 393224 | tf_op jit(solution)/shard_map/ppermute | solution.py:385
  39.8 8.6 %collective-permute-start.15 = (bf16[128,512]{1,0:T(8,128)(2,1)S(1)}, bf16[128,512]{1,0:T(8,128)(2,1)S(1)}, u32[]{:S(2)}, u32[]{:S(2)}) collective-permute-start(bf16[128,512]{1,0:T(8,128)(2,1)S(1)} %get-tuple-element.139.refs_1_.refs_0_), channel_id=1, source_target_pairs={{0,96},{1,25},{2,98},{3,27},{4,100},{5,29},{6,102},{7,31},{8,104},... | collective-permute-start | bytes 393224 | tf_op jit(solution)/shard_map/ppermute | solution.py:397
  42.3 6.1 %collective-permute-start.14 = (bf16[128,512]{1,0:T(8,128)(2,1)S(1)}, bf16[128,512]{1,0:T(8,128)(2,1)S(1)}, u32[]{:S(2)}, u32[]{:S(2)}) collective-permute-start(bf16[128,512]{1,0:T(8,128)(2,1)S(1)} %collective-permute-done.13.refs_1_), channel_id=1, source_target_pairs={{0,32},{1,9},{2,34},{3,11},{4,36},{5,13},{6,38},{7,15},{8,40},{9,1... | collective-permute-start | bytes 393224 | tf_op jit(solution)/shard_map/ppermute | solution.py:398
  48.4 6.3 %collective-permute-start.16 = (bf16[256,512]{1,0:T(8,128)(2,1)S(1)}, bf16[256,512]{1,0:T(8,128)(2,1)S(1)}, u32[]{:S(2)}, u32[]{:S(2)}) collective-permute-start(bf16[256,512]{1,0:T(8,128)(2,1)S(1)} %pad_maximum_fusion.1), channel_id=1, source_target_pairs={{0,1},{1,0},{2,3},{3,2},{4,5},{5,4},{6,7},{7,6},{8,9},{9,8},{10,11... | collective-permute-start | bytes 786440 | tf_op jit(solution)/shard_map/ppermute | solution.py:379
  52.0 6.4 %collective-permute-start.17 = (bf16[128,512]{1,0:T(8,128)(2,1)S(1)}, bf16[128,512]{1,0:T(8,128)(2,1)S(1)}, u32[]{:S(2)}, u32[]{:S(2)}) collective-permute-start(bf16[128,512]{1,0:T(8,128)(2,1)S(1)} %get-tuple-element.148), channel_id=1, source_target_pairs={{0,32},{1,9},{2,34},{3,11},{4,36},{5,13},{6,38},{7,15},{8,40},{9,1... | collective-permute-start | bytes 393224 | tf_op jit(solution)/shard_map/ppermute | solution.py:402
  52.1 6.3 %collective-permute-start.18 = (bf16[128,512]{1,0:T(8,128)(2,1)S(1)}, bf16[128,512]{1,0:T(8,128)(2,1)S(1)}, u32[]{:S(2)}, u32[]{:S(2)}) collective-permute-start(bf16[128,512]{1,0:T(8,128)(2,1)S(1)} %get-tuple-element.149), channel_id=1, source_target_pairs={{0,96},{1,25},{2,98},{3,27},{4,100},{5,29},{6,102},{7,31},{8,104},... | collective-permute-start | bytes 393224 | tf_op jit(solution)/shard_map/ppermute | solution.py:403
  56.8 5.8 %collective-permute-start.20 = (bf16[128,512]{1,0:T(8,128)(2,1)S(1)}, bf16[128,512]{1,0:T(8,128)(2,1)S(1)}, u32[]{:S(2)}, u32[]{:S(2)}) collective-permute-start(bf16[128,512]{1,0:T(8,128)(2,1)S(1)} %get-tuple-element.153), channel_id=1, source_target_pairs={{0,2},{1,3},{2,4},{3,5},{4,6},{5,7},{6,0},{7,1},{8,10},{9,11},{10,... | collective-permute-start | bytes 393224 | tf_op jit(solution)/shard_map/ppermute | solution.py:385
  58.4 5.4 %collective-permute-start.19 = (bf16[128,512]{1,0:T(8,128)(2,1)S(1)}, bf16[128,512]{1,0:T(8,128)(2,1)S(1)}, u32[]{:S(2)}, u32[]{:S(2)}) collective-permute-start(bf16[128,512]{1,0:T(8,128)(2,1)S(1)} %add_convert_fusion), channel_id=1, source_target_pairs={{0,32},{1,9},{2,34},{3,11},{4,36},{5,13},{6,38},{7,15},{8,40},{9,1... | collective-permute-start | bytes 393224 | tf_op jit(solution)/shard_map/ppermute | solution.py:406
  63.9 5.7 %collective-permute-start.23 = (bf16[128,512]{1,0:T(8,128)(2,1)S(1)}, bf16[128,512]{1,0:T(8,128)(2,1)S(1)}, u32[]{:S(2)}, u32[]{:S(2)}) collective-permute-start(bf16[128,512]{1,0:T(8,128)(2,1)S(1)} %pad_maximum_fusion.5), channel_id=1, source_target_pairs={{0,8},{1,33},{2,10},{3,35},{4,12},{5,37},{6,14},{7,39},{8,16},{9,4... | collective-permute-start | bytes 393224 | tf_op jit(solution)/shard_map/ppermute | solution.py:396
  64.0 5.7 %collective-permute-start.21 = (bf16[128,512]{1,0:T(8,128)(2,1)S(1)}, bf16[128,512]{1,0:T(8,128)(2,1)S(1)}, u32[]{:S(2)}, u32[]{:S(2)}) collective-permute-start(bf16[128,512]{1,0:T(8,128)(2,1)S(1)} %get-tuple-element.155), channel_id=1, source_target_pairs={{0,4},{1,5},{2,6},{3,7},{4,0},{5,1},{6,2},{7,3},{8,12},{9,13},{10,... | collective-permute-start | bytes 393224 | tf_op jit(solution)/shard_map/ppermute | solution.py:385
  66.2 4.9 %collective-permute-start.22 = (bf16[128,512]{1,0:T(8,128)(2,1)S(1)}, bf16[128,512]{1,0:T(8,128)(2,1)S(1)}, u32[]{:S(2)}, u32[]{:S(2)}) collective-permute-start(bf16[128,512]{1,0:T(8,128)(2,1)S(1)} %get-tuple-element.156), channel_id=1, source_target_pairs={{0,6},{1,7},{2,0},{3,1},{4,2},{5,3},{6,4},{7,5},{8,14},{9,15},{10,... | collective-permute-start | bytes 393224 | tf_op jit(solution)/shard_map/ppermute | solution.py:385
  69.6 5.0 %collective-permute-start.24 = (bf16[128,512]{1,0:T(8,128)(2,1)S(1)}, bf16[128,512]{1,0:T(8,128)(2,1)S(1)}, u32[]{:S(2)}, u32[]{:S(2)}) collective-permute-start(bf16[128,512]{1,0:T(8,128)(2,1)S(1)} %collective-permute-done.23.g1), channel_id=1, source_target_pairs={{0,8},{1,33},{2,10},{3,35},{4,12},{5,37},{6,14},{7,39},{8,16},{9,4... | collective-permute-start | bytes 393224 | tf_op jit(solution)/shard_map/ppermute | solution.py:398
  74.7 5.1 %collective-permute-start.26 = (bf16[256,512]{1,0:T(8,128)(2,1)S(1)}, bf16[256,512]{1,0:T(8,128)(2,1)S(1)}, u32[]{:S(2)}, u32[]{:S(2)}) collective-permute-start(bf16[256,512]{1,0:T(8,128)(2,1)S(1)} %pad_maximum_fusion.2), channel_id=1, source_target_pairs={{0,1},{1,0},{2,3},{3,2},{4,5},{5,4},{6,7},{7,6},{8,9},{9,8},{10,11... | collective-permute-start | bytes 786440 | tf_op jit(solution)/shard_map/ppermute | solution.py:379
  78.8 5.9 %collective-permute-start.30 = (bf16[128,512]{1,0:T(8,128)(2,1)S(1)}, bf16[128,512]{1,0:T(8,128)(2,1)S(1)}, u32[]{:S(2)}, u32[]{:S(2)}) collective-permute-start(bf16[128,512]{1,0:T(8,128)(2,1)S(1)} %get-tuple-element.184.refs_1_.refs_0_), channel_id=1, source_target_pairs={{0,32},{1,9},{2,34},{3,11},{4,36},{5,13},{6,38},{7,15},{8,40},{9,1... | collective-permute-start | bytes 393224 | tf_op jit(solution)/shard_map/ppermute | solution.py:396
  80.5 6.2 %collective-permute-start.27 = (bf16[128,512]{1,0:T(8,128)(2,1)S(1)}, bf16[128,512]{1,0:T(8,128)(2,1)S(1)}, u32[]{:S(2)}, u32[]{:S(2)}) collective-permute-start(bf16[128,512]{1,0:T(8,128)(2,1)S(1)} %get-tuple-element.176), channel_id=1, source_target_pairs={{0,6},{1,7},{2,0},{3,1},{4,2},{5,3},{6,4},{7,5},{8,14},{9,15},{10,... | collective-permute-start | bytes 393224 | tf_op jit(solution)/shard_map/ppermute | solution.py:385
  81.4 5.9 %collective-permute-start.28 = (bf16[128,512]{1,0:T(8,128)(2,1)S(1)}, bf16[128,512]{1,0:T(8,128)(2,1)S(1)}, u32[]{:S(2)}, u32[]{:S(2)}) collective-permute-start(bf16[128,512]{1,0:T(8,128)(2,1)S(1)} %get-tuple-element.177), channel_id=1, source_target_pairs={{0,4},{1,5},{2,6},{3,7},{4,0},{5,1},{6,2},{7,3},{8,12},{9,13},{10,... | collective-permute-start | bytes 393224 | tf_op jit(solution)/shard_map/ppermute | solution.py:385
  82.9 7.8 %collective-permute-start.29 = (bf16[128,512]{1,0:T(8,128)(2,1)S(1)}, bf16[128,512]{1,0:T(8,128)(2,1)S(1)}, u32[]{:S(2)}, u32[]{:S(2)}) collective-permute-start(bf16[128,512]{1,0:T(8,128)(2,1)S(1)} %get-tuple-element.178), channel_id=1, source_target_pairs={{0,2},{1,3},{2,4},{3,5},{4,6},{5,7},{6,0},{7,1},{8,10},{9,11},{10,... | collective-permute-start | bytes 393224 | tf_op jit(solution)/shard_map/ppermute | solution.py:385
  82.9 7.8 %collective-permute-start.32 = (bf16[128,512]{1,0:T(8,128)(2,1)S(1)}, bf16[128,512]{1,0:T(8,128)(2,1)S(1)}, u32[]{:S(2)}, u32[]{:S(2)}) collective-permute-start(bf16[128,512]{1,0:T(8,128)(2,1)S(1)} %get-tuple-element.184.refs_1_.refs_0_), channel_id=1, source_target_pairs={{0,96},{1,25},{2,98},{3,27},{4,100},{5,29},{6,102},{7,31},{8,104},... | collective-permute-start | bytes 393224 | tf_op jit(solution)/shard_map/ppermute | solution.py:397
  84.6 6.1 %collective-permute-start.31 = (bf16[128,512]{1,0:T(8,128)(2,1)S(1)}, bf16[128,512]{1,0:T(8,128)(2,1)S(1)}, u32[]{:S(2)}, u32[]{:S(2)}) collective-permute-start(bf16[128,512]{1,0:T(8,128)(2,1)S(1)} %collective-permute-done.30.refs_1_), channel_id=1, source_target_pairs={{0,32},{1,9},{2,34},{3,11},{4,36},{5,13},{6,38},{7,15},{8,40},{9,1... | collective-permute-start | bytes 393224 | tf_op jit(solution)/shard_map/ppermute | solution.py:398
  95.6 14.3 %all-to-all-start = ((f32[128,1,128]{2,1,0:T(1,128)}), f32[128,1,128]{2,1,0:T(1,128)S(1)}, u32[]{:S(2)}, u32[]{:S(2)}) async-start(f32[128,1,128]{2,1,0:T(1,128)} %get-tuple-element.190), calls=%async_computation | async-start | bytes 131072 | tf_op jit(solution)/shard_map/all_to_all | solution.py:544
  (6 other events, 67.5 us)

commit v2 on v0

--- a/solution.py
+++ b/solution.py
@@ -67,7 +67,7 @@
     return [slice(i * TILE, (i + 1) * TILE) for i in range(NC // TILE)]
 
 
-def first(parent_of, section_of, y_far, linking_far, x_far, cost_far, *refs):
+def first(code, y_far, linking_far, x_far, cost_far, *refs):
     *outs, y, linking, ylow, nsend, nback, lsend, lback, scol, x_top, cost_top, state, sem = refs
     chunks = parts()
     copies = []
@@ -80,8 +80,9 @@
     copies = [pltpu.make_async_copy(a, b, sem.at[i]) for i, (a, b) in enumerate(copies)]
     for copy in copies:
         copy.start()
-    upper = section_of[...][:, ROWS] == 1
-    parent = parent_of[...][:, ROWS]
+    packed = code[...]
+    upper = (packed >> 16) == 1
+    parent = packed & 0xFFFF
     here = lax.axis_index("leaf") * N_NODE + lax.axis_index("node")
     owner = ((parent.astype(F32) + 0.5) * (1.0 / NODES)).astype(jnp.int32)
     local = parent - owner * NODES
@@ -392,6 +393,12 @@
     return got + [sibling(halves)], before
 
 
+def ring_gather(rows, ring):
+    one = lax.ppermute(rows, *ring(1))
+    three = lax.ppermute(rows, *ring(3))
+    return [rows, one, lax.ppermute(one, *ring(1)), three]
+
+
 def sum_leaf(blocks, own, state, before):
     got, before = lax.optimization_barrier((shifted(blocks, outer_ring), before))
     got = [block.astype(F32) for block in got]
@@ -411,6 +418,7 @@
 
 def shards(x_start, y_start, cost_vec, right_side, omega, coupling, linking, parent, section):
     unit = 2 * CHILD * NS * NC
+    code = (section * 65536 + parent)[ROOTS:].reshape(1, CHILD)
     rates = jnp.broadcast_to(jnp.stack([STEP / omega[0], STEP * omega[0]])[:, None], (2, 128))
     field = ((NODES, NC), F32)
     field_low = ((NODES, NC), BF16)
@@ -430,10 +438,10 @@
         first,
         [block_mark] * 4 + [block] * 4
         + [field, ((2, NC, NS), BF16), field_low, row, col, row, col, col, tops, tops, ((ROOTS, NS), BF16)],
-        [parent.reshape(1, NODES), section.reshape(1, NODES), y_start, linking, x_start, cost_vec],
+        [code, y_start, linking, x_start, cost_vec],
         2 * unit,
         [pltpu.SemaphoreType.DMA((3 * NC // TILE + 2,))],
-        (2, 3, 4, 5),
+        (1, 2, 3, 4),
     )
     chunk_sems = [pltpu.SemaphoreType.DMA((NC // TILE,))]
     own_root, coupling_root = call(
@@ -467,7 +475,7 @@
         ],
         2 * unit,
     )
-    back_leaf = shifted([extra_root] * 4, outer_ring)
+    back_leaf = ring_gather(extra_root, outer_ring)
     back_node, (back_leaf, base) = swap_node(out_node, -1, (back_leaf, base))
     later, *out_leaf = call(
         part_of(dual_leaf, False),
@@ -512,7 +520,7 @@
         [extra_child, extra_root, scol, coupling_root, coupling, y_next, right_side, rates, cost_top],
         2 * unit,
     )
-    back_leaf = shifted([extra_root] * 4, outer_ring)
+    back_leaf = ring_gather(extra_root, outer_ring)
     back_node, (back_leaf, base) = swap_node(out_node, -1, (back_leaf, base))
     (later,) = call(
         part_of(dual_leaf, True), [kids_field], back_leaf + [lback, linking, base, rates], unit

time: 107 us -> 105 us (0.981)
  waiting for transfers between devices: 26 us -> 22.6 us
  starting transfers between devices: 47.9 us -> 49.8 us
  local copies, waits for them, and re-layouts: 4.42 us -> 3.13 us
    ppermute x0 -> x6, starting transfers between devices: none -> 4.35 us  [the longest x2 4.19 us: ring_gather(): three = lax.ppermute(rows, *ring(3))]
    ppermute x30 -> x24, waiting for transfers between devices: 17.4 us -> 13 us  [shifted(): got[k] = lax.ppermute(blocks[k], *ring(sign * k % 4))]
    reshape x2 -> x0, local copies, waits for them, and re-layouts: 1.37 us -> none  [the longest x1 0.68 us: shards(): parent.reshape(1, NODES)]
    ppermute x0 -> x6, waiting for transfers between devices: none -> 1.18 us  [the longest x2 1.17 us: ring_gather(): return [rows, one, lax.ppermute(one, *ring(1)), three]]
    ppermute x4, starting transfers between devices: 12 us -> 10.9 us  [sibling(): return lax.ppermute(array, *pairs_of(lambda y, z, x, c: (y, z, x, 1 - c)))]
    ppermute x30 -> x24, starting transfers between devices: 30.6 us -> 30 us  [shifted(): got[k] = lax.ppermute(blocks[k], *ring(sign * k % 4))]
  transfers between devices with their start and end apart: 35 -> 35, of which waited for: 13 -> 13; matrix products, arithmetic and copies ran while one was open for 3% -> 3% of each run, Pallas kernels for 15% -> 17%
where the time goes in v2:
time: 105 us
  starting transfers between devices  49.8 us (47%)
  Pallas kernels  23.8 us (23%)
  waiting for transfers between devices  22.6 us (22%)
  between operations  4.3 us (4%)
  local copies, waits for them, and re-layouts  3.13 us (3%)
  other arithmetic  1.22 us (1%)
    ppermute x24, starting transfers between devices, shifted(): got[k] = lax.ppermute(blocks[k], *ring(sign * k % 4))  30 us
    pallas_call x15, Pallas kernels, call(): pl.pallas_call(kernel, out_shape=out_shapes, in_specs=[pl.BlockSpec(memor...  23.8 us
    ppermute x24, waiting for transfers between devices, shifted(): got[k] = lax.ppermute(blocks[k], *ring(sign * k % 4))  13 us
    ppermute x4, starting transfers between devices, sibling(): return lax.ppermute(array, *pairs_of(lambda y, z, x, c: (y, z, x, 1 - c)))  10.9 us
    all_to_all x1, waiting for transfers between devices, shards(): lax.all_to_all(load, ('leaf', 'node'), split_axis=0, concat_axis=0, tiled...  7.27 us
    all_to_all x1, starting transfers between devices, shards(): lax.all_to_all(load, ('leaf', 'node'), split_axis=0, concat_axis=0, tiled...  4.64 us
    ppermute x2, starting transfers between devices, ring_gather(): three = lax.ppermute(rows, *ring(3))  4.19 us
    unnamed x8, local copies, waits for them, and re-layouts  2.24 us
  transfers between devices with their start and end apart: 35, of which 13 were waited for; matrix products, arithmetic and copies ran while one was open for 3% of the time, Pallas kernels for 17%

profile of v2, /device:TPU:1, one launch (start us, length us, event | category | flops | bytes accessed | tf_op | source)
XLA Modules:
  0.0 105.0 jit_solution(9027234557689820870)
XLA Ops:
  1.4 4.2 %shard_map.112 = (bf16[128,640]{1,0:T(8,128)(2,1)S(1)}, bf16[128,640]{1,0:T(8,128)(2,1)S(1)}, bf16[128,640]{1,0:T(8,128)(2,1)S(1)}, bf16[128,640]{1,0:T(8,128)(2...) custom-call(s32[1,256]{1,0:T(1,128)S(1)} %bitcast.1, ...), custom_call_target="tpu_custom_call" | custom-call | flops 1073741824 | bytes 2150784 | tf_op jit(solution)/shard_map/pallas_call | solution.py:55
  5.7 2.5 %collective-permute-start.3 = (bf16[128,512]{1,0:T(8,128)(2,1)S(1)}, bf16[128,512]{1,0:T(8,128)(2,1)S(1)}, u32[]{:S(2)}, u32[]{:S(2)}) collective-permute-start(bf16[128,512]{1,0:T(8,128)(2,1)S(1)} %get-tuple-element.103), channel_id=1, source_target_pairs={{0,32},{1,9},{2,34},{3,11},{4,36},{5,13},{6,38},{7,15},{8,40},{9,1... | collective-permute-start | bytes 393224 | tf_op jit(solution)/shard_map/ppermute | solution.py:385
  8.2 3.3 %collective-permute-start.4 = (bf16[128,512]{1,0:T(8,128)(2,1)S(1)}, bf16[128,512]{1,0:T(8,128)(2,1)S(1)}, u32[]{:S(2)}, u32[]{:S(2)}) collective-permute-start(bf16[128,512]{1,0:T(8,128)(2,1)S(1)} %get-tuple-element.104), channel_id=1, source_target_pairs={{0,64},{1,17},{2,66},{3,19},{4,68},{5,21},{6,70},{7,23},{8,72},{9,... | collective-permute-start | bytes 393224 | tf_op jit(solution)/shard_map/ppermute | solution.py:385
  13.5 2.4 %collective-permute-start.1 = (bf16[128,640]{1,0:T(8,128)(2,1)S(1)}, bf16[128,640]{1,0:T(8,128)(2,1)S(1)}, u32[]{:S(2)}, u32[]{:S(2)}) collective-permute-start(bf16[128,640]{1,0:T(8,128)(2,1)S(1)} %get-tuple-element.100), channel_id=1, source_target_pairs={{0,4},{1,5},{2,6},{3,7},{4,0},{5,1},{6,2},{7,3},{8,12},{9,13},{10,... | collective-permute-start | bytes 491528 | tf_op jit(solution)/shard_map/ppermute | solution.py:385
  15.9 1.7 %shard_map.113 = (f32[32,512]{1,0:T(8,128)S(1)}, bf16[2048,512]{1,0:T(8,128)(2,1)S(1)}) custom-call(bf16[288,2048]{1,0:T(8,128)(2,1)S(1)} %get-tuple-element.106.ylow, f32[32,512]{1,0:T(8,128)S(1)} %get-tuple-element.107.cost_top.refs_8_, bf16[3,2048,512]{2,1,0:T(8,128)(2,1)} %coupling_far.3), custom_call_target="tpu_custom_call" | custom-call | flops 67108864 | bytes 1212416 | tf_op jit(solution)/shard_map/pallas_call | solution.py:55
  19.0 2.8 %collective-permute-start.8 = (bf16[160,512]{1,0:T(8,128)(2,1)S(1)}, bf16[160,512]{1,0:T(8,128)(2,1)S(1)}, u32[]{:S(2)}, u32[]{:S(2)}) collective-permute-start(bf16[160,512]{1,0:T(8,128)(2,1)S(1)} %pad_maximum_fusion.4), channel_id=1, source_target_pairs={{0,24},{1,97},{2,26},{3,99},{4,28},{5,101},{6,30},{7,103},{8,0},{9... | collective-permute-start | bytes 491528 | tf_op jit(solution)/shard_map/ppermute | solution.py:385
  22.9 2.9 %shard_map.114 = (f32[256,512]{1,0:T(8,128)S(1)}, bf16[2,2048,512]{2,1,0:T(8,128)(2,1)S(1)}) custom-call(bf16[288,2048]{1,0:T(8,128)(2,1)S(1)} %get-tuple-element.106.ylow, f32[256,128]{1,0:T(8,128)S(1)} %get-tuple-element.114.scol.refs_2_, bf16[3,2048,512]{2,1,0:T(8,128)(2,1)} %coupling_far.3), custom_call_target="tpu_custom_call" | custom-call | flops 1073741824 | bytes 1540096 | tf_op jit(solution)/shard_map/pallas_call | solution.py:55
  26.0 1.6 %collective-permute-done.7.g2 = bf16[160,512]{1,0:T(8,128)(2,1)S(1)} collective-permute-done((bf16[160,512]{1,0:T(8,128)(2,1)S(1)}, bf16[160,512]{1,0:T(8,128)(2,1)S(1)}, u32[]{:S(2)}, u32[]{:S(2)}) %collective-permute-start.7) | collective-permute-done | bytes 163872 | tf_op jit(solution)/shard_map/ppermute | solution.py:385
  27.6 1.9 %collective-permute-done.6.g1 = bf16[160,512]{1,0:T(8,128)(2,1)S(1)} collective-permute-done((bf16[160,512]{1,0:T(8,128)(2,1)S(1)}, bf16[160,512]{1,0:T(8,128)(2,1)S(1)}, u32[]{:S(2)}, u32[]{:S(2)}) %collective-permute-start.6) | collective-permute-done | bytes 163872 | tf_op jit(solution)/shard_map/ppermute | solution.py:385
  29.6 3.5 %collective-permute-start.9 = (bf16[256,640]{1,0:T(8,128)(2,1)S(1)}, bf16[256,640]{1,0:T(8,128)(2,1)S(1)}, u32[]{:S(2)}, u32[]{:S(2)}) collective-permute-start(bf16[256,640]{1,0:T(8,128)(2,1)S(1)} %pad_maximum_fusion), channel_id=1, source_target_pairs={{0,1},{1,0},{2,3},{3,2},{4,5},{5,4},{6,7},{7,6},{8,9},{9,8},{10,11... | collective-permute-start | bytes 983048 | tf_op jit(solution)/shard_map/ppermute | solution.py:379
  35.2 2.1 %collective-permute-start.11 = (bf16[128,512]{1,0:T(8,128)(2,1)S(1)}, bf16[128,512]{1,0:T(8,128)(2,1)S(1)}, u32[]{:S(2)}, u32[]{:S(2)}) collective-permute-start(bf16[128,512]{1,0:T(8,128)(2,1)S(1)} %get-tuple-element.128), channel_id=1, source_target_pairs={{0,4},{1,5},{2,6},{3,7},{4,0},{5,1},{6,2},{7,3},{8,12},{9,13},{10,... | collective-permute-start | bytes 393224 | tf_op jit(solution)/shard_map/ppermute | solution.py:385
  37.3 2.5 %collective-permute-start.15 = (bf16[128,512]{1,0:T(8,128)(2,1)S(1)}, bf16[128,512]{1,0:T(8,128)(2,1)S(1)}, u32[]{:S(2)}, u32[]{:S(2)}) collective-permute-start(bf16[128,512]{1,0:T(8,128)(2,1)S(1)} %get-tuple-element.140.refs_1_.refs_0_), channel_id=1, source_target_pairs={{0,96},{1,25},{2,98},{3,27},{4,100},{5,29},{6,102},{7,31},{8,104},... | collective-permute-start | bytes 393224 | tf_op jit(solution)/shard_map/ppermute | solution.py:398
  39.8 2.6 %shard_map.117 = (f32[288,2048]{1,0:T(8,128)S(1)}, f32[32,512]{1,0:T(8,128)S(1)}) custom-call(bf16[256,512]{1,0:T(8,128)(2,1)S(1)} %get-tuple-element.131.refs_0_, bf16[128,512]{1,0:T(8,128)(2,1)S(1)} %get-tuple-element.140.refs_1_.refs_0_, f32[256,128]{1,0:T(8,128)S(1)} %get-tuple-element.114.scol.refs_2_, ...), custom_call_target="tpu_custom_call" | custom-call | flops 1073741824 | bytes 1753216 | tf_op jit(solution)/shard_map/pallas_call | solution.py:55
  42.4 2.0 %collective-permute-done.12.g3 = bf16[128,512]{1,0:T(8,128)(2,1)S(1)} collective-permute-done((bf16[128,512]{1,0:T(8,128)(2,1)S(1)}, bf16[128,512]{1,0:T(8,128)(2,1)S(1)}, u32[]{:S(2)}, u32[]{:S(2)}) %collective-permute-start.12) | collective-permute-done | bytes 131104 | tf_op jit(solution)/shard_map/ppermute | solution.py:385
  45.1 2.0 %collective-permute-start.16 = (bf16[256,512]{1,0:T(8,128)(2,1)S(1)}, bf16[256,512]{1,0:T(8,128)(2,1)S(1)}, u32[]{:S(2)}, u32[]{:S(2)}) collective-permute-start(bf16[256,512]{1,0:T(8,128)(2,1)S(1)} %pad_maximum_fusion.1), channel_id=1, source_target_pairs={{0,1},{1,0},{2,3},{3,2},{4,5},{5,4},{6,7},{7,6},{8,9},{9,8},{10,11... | collective-permute-start | bytes 786440 | tf_op jit(solution)/shard_map/ppermute | solution.py:379
  47.1 2.1 %shard_map.118 = (f32[256,2048]{1,0:T(8,128)S(1)}, bf16[128,512]{1,0:T(8,128)(2,1)S(1)}, bf16[128,512]{1,0:T(8,128)(2,1)S(1)}, bf16[128,512]{1,0:T(8,128)(2,1)S(1)}, bf16[128,512]{1,0:T(8,128)(2,1)S(1)}) custom-call(bf16[128,512]{1,0:T(8,128)(2,1)S(1)} %get-tuple-element.140.refs_1_.refs_0_, bf16[128,512]{1,0:T(8,128)(2,1)S(1)} %collective-permute-done.13.refs_1_, ...), custom_call_target="tpu_custom_call" | custom-call | flops 1073741824 | bytes 1229056 | tf_op jit(solution)/shard_map/pallas_call | solution.py:55
  49.3 1.8 %collective-permute-start.21 = (bf16[128,512]{1,0:T(8,128)(2,1)S(1)}, bf16[128,512]{1,0:T(8,128)(2,1)S(1)}, u32[]{:S(2)}, u32[]{:S(2)}) collective-permute-start(bf16[128,512]{1,0:T(8,128)(2,1)S(1)} %get-tuple-element.154), channel_id=1, source_target_pairs={{0,64},{1,17},{2,66},{3,19},{4,68},{5,21},{6,70},{7,23},{8,72},{9,... | collective-permute-start | bytes 393224 | tf_op jit(solution)/shard_map/ppermute | solution.py:385
  51.9 2.0 %shard_map.119 = (f32[288,2048]{1,0:T(8,128)S(1)}, bf16[288,2048]{1,0:T(8,128)(2,1)S(1)}, bf16[128,512]{1,0:T(8,128)(2,1)S(1)}, bf16[128,512]{1,0:T(8,128)(2,1)S...) custom-call(bf16[128,512]{1,0:T(8,128)(2,1)S(1)} %get-tuple-element.126.g0, ...), custom_call_target="tpu_custom_call" | custom-call | flops 1073741824 | bytes 1704192 | tf_op jit(solution)/shard_map/pallas_call | solution.py:55
  54.7 3.5 %collective-permute-start.18 = (bf16[128,512]{1,0:T(8,128)(2,1)S(1)}, bf16[128,512]{1,0:T(8,128)(2,1)S(1)}, u32[]{:S(2)}, u32[]{:S(2)}) collective-permute-start(bf16[128,512]{1,0:T(8,128)(2,1)S(1)} %get-tuple-element.150), channel_id=1, source_target_pairs={{0,4},{1,5},{2,6},{3,7},{4,0},{5,1},{6,2},{7,3},{8,12},{9,13},{10,... | collective-permute-start | bytes 393224 | tf_op jit(solution)/shard_map/ppermute | solution.py:385
  61.0 1.2 %shard_map.120.own = f32[256,512]{1,0:T(8,128)S(1)} custom-call(bf16[288,2048]{1,0:T(8,128)(2,1)S(1)} %get-tuple-element.162.ylow, f32[256,128]{1,0:T(8,128)S(1)} %get-tuple-element.114.scol.refs_2_, bf16[2,2048,512]{2,1,0:T(8,128)(2,1)S(1)} %get-tuple-element.133.refs_4_.coupling), custom_call_target="tpu_custom_call" | custom-call | flops 1073741824 | bytes 753664 | tf_op jit(solution)/shard_map/pallas_call | solution.py:55
  62.3 1.7 %collective-permute-done.18.g2 = bf16[128,512]{1,0:T(8,128)(2,1)S(1)} collective-permute-done((bf16[128,512]{1,0:T(8,128)(2,1)S(1)}, bf16[128,512]{1,0:T(8,128)(2,1)S(1)}, u32[]{:S(2)}, u32[]{:S(2)}) %collective-permute-start.18) | collective-permute-done | bytes 131104 | tf_op jit(solution)/shard_map/ppermute | solution.py:385
  65.0 1.6 %collective-permute-done.23.g1 = bf16[128,512]{1,0:T(8,128)(2,1)S(1)} collective-permute-done((bf16[128,512]{1,0:T(8,128)(2,1)S(1)}, bf16[128,512]{1,0:T(8,128)(2,1)S(1)}, u32[]{:S(2)}, u32[]{:S(2)}) %collective-permute-start.23) | collective-permute-done | bytes 131104 | tf_op jit(solution)/shard_map/ppermute | solution.py:385
  66.6 3.1 %collective-permute-start.26 = (bf16[256,512]{1,0:T(8,128)(2,1)S(1)}, bf16[256,512]{1,0:T(8,128)(2,1)S(1)}, u32[]{:S(2)}, u32[]{:S(2)}) collective-permute-start(bf16[256,512]{1,0:T(8,128)(2,1)S(1)} %pad_maximum_fusion.2), channel_id=1, source_target_pairs={{0,1},{1,0},{2,3},{3,2},{4,5},{5,4},{6,7},{7,6},{8,9},{9,8},{10,11... | collective-permute-start | bytes 786440 | tf_op jit(solution)/shard_map/ppermute | solution.py:379
  72.0 2.1 %collective-permute-start.28 = (bf16[128,512]{1,0:T(8,128)(2,1)S(1)}, bf16[128,512]{1,0:T(8,128)(2,1)S(1)}, u32[]{:S(2)}, u32[]{:S(2)}) collective-permute-start(bf16[128,512]{1,0:T(8,128)(2,1)S(1)} %get-tuple-element.179), channel_id=1, source_target_pairs={{0,4},{1,5},{2,6},{3,7},{4,0},{5,1},{6,2},{7,3},{8,12},{9,13},{10,... | collective-permute-start | bytes 393224 | tf_op jit(solution)/shard_map/ppermute | solution.py:385
  74.9 1.7 %collective-permute-start.32 = (bf16[128,512]{1,0:T(8,128)(2,1)S(1)}, bf16[128,512]{1,0:T(8,128)(2,1)S(1)}, u32[]{:S(2)}, u32[]{:S(2)}) collective-permute-start(bf16[128,512]{1,0:T(8,128)(2,1)S(1)} %get-tuple-element.186.refs_1_.refs_0_), channel_id=1, source_target_pairs={{0,96},{1,25},{2,98},{3,27},{4,100},{5,29},{6,102},{7,31},{8,104},... | collective-permute-start | bytes 393224 | tf_op jit(solution)/shard_map/ppermute | solution.py:398
  76.6 2.0 %shard_map.124.refs_6_.base = f32[288,2048]{1,0:T(8,128)S(1)} custom-call(bf16[256,512]{1,0:T(8,128)(2,1)S(1)} %get-tuple-element.182.refs_0_, bf16[128,512]{1,0:T(8,128)(2,1)S(1)} %get-tuple-element.186.refs_1_.refs_0_, f32[256,128]{1,0:T(8,128)S(1)} %get-tuple-element.114.scol.refs_2_, bf16[2048,512]{1,0:T(8,128)(2,1)S(1)} %get-tuple-element.132.refs_3_, ...), custom_call_target="tpu_custom_call" | custom-call | flops 1073741824 | bytes 1745024 | tf_op jit(solution)/shard_map/pallas_call | solution.py:55
  78.7 2.6 %collective-permute-done.29.g3 = bf16[128,512]{1,0:T(8,128)(2,1)S(1)} collective-permute-done((bf16[128,512]{1,0:T(8,128)(2,1)S(1)}, bf16[128,512]{1,0:T(8,128)(2,1)S(1)}, u32[]{:S(2)}, u32[]{:S(2)}) %collective-permute-start.29) | collective-permute-done | bytes 131104 | tf_op jit(solution)/shard_map/ppermute | solution.py:385
  81.9 2.3 %collective-permute-start.33 = (bf16[256,512]{1,0:T(8,128)(2,1)S(1)}, bf16[256,512]{1,0:T(8,128)(2,1)S(1)}, u32[]{:S(2)}, u32[]{:S(2)}) collective-permute-start(bf16[256,512]{1,0:T(8,128)(2,1)S(1)} %pad_maximum_fusion.3), channel_id=1, source_target_pairs={{0,1},{1,0},{2,3},{3,2},{4,5},{5,4},{6,7},{7,6},{8,9},{9,8},{10,11... | collective-permute-start | bytes 786440 | tf_op jit(solution)/shard_map/ppermute | solution.py:379
  85.6 2.0 %shard_map.126 = (f32[288,2048]{1,0:T(8,128)S(1)}, f32[128,1,128]{2,1,0:T(1,128)}) custom-call(bf16[128,512]{1,0:T(8,128)(2,1)S(1)} %get-tuple-element.177.g0, bf16[128,512]{1,0:T(8,128)(2,1)S(1)} %collective-permute-done.27.g1, bf16[128,512]{1,0:T(8,128)(2,1)S(1)} %collective-permute-done.28.g2, bf16[128,512]{1,0:T(8,128)(2,1)S(1)} %collective-permute-done.29.g3, ...), custom_call_target="tpu_custom_call" | custom-call | flops 536870912 | bytes 2089600 | tf_op jit(solution)/shard_map/pallas_call | solution.py:55
  87.6 4.6 %all-to-all-start = ((f32[128,1,128]{2,1,0:T(1,128)}), f32[128,1,128]{2,1,0:T(1,128)S(1)}, u32[]{:S(2)}, u32[]{:S(2)}) async-start(f32[128,1,128]{2,1,0:T(1,128)} %get-tuple-element.192), calls=%async_computation | async-start | bytes 131072 | tf_op jit(solution)/shard_map/all_to_all | solution.py:535
  93.0 1.4 %copy.13 = f32[288,2048]{1,0:T(8,128)} copy(f32[288,2048]{1,0:T(8,128)S(1)} %get-tuple-element.200) | data formatting | bytes 4718592
  94.4 7.3 %all-to-all-done = f32[128,1,128]{2,1,0:T(1,128)S(1)} async-done(((f32[128,1,128]{2,1,0:T(1,128)}), f32[128,1,128]{2,1,0:T(1,128)S(1)}, u32[]{:S(2)}, u32[]{:S(2)}) %all-to-all-start) | async-done | bytes 65568 | tf_op jit(solution)/shard_map/all_to_all | solution.py:535
  (95 shorter events, 19.3 us)
Async XLA Ops:
  5.7 12.0 %collective-permute-start.3 = (bf16[128,512]{1,0:T(8,128)(2,1)S(1)}, bf16[128,512]{1,0:T(8,128)(2,1)S(1)}, u32[]{:S(2)}, u32[]{:S(2)}) collective-permute-start(bf16[128,512]{1,0:T(8,128)(2,1)S(1)} %get-tuple-element.103), channel_id=1, source_target_pairs={{0,32},{1,9},{2,34},{3,11},{4,36},{5,13},{6,38},{7,15},{8,40},{9,1... | collective-permute-start | bytes 393224 | tf_op jit(solution)/shard_map/ppermute | solution.py:385
  8.2 10.7 %collective-permute-start.4 = (bf16[128,512]{1,0:T(8,128)(2,1)S(1)}, bf16[128,512]{1,0:T(8,128)(2,1)S(1)}, u32[]{:S(2)}, u32[]{:S(2)}) collective-permute-start(bf16[128,512]{1,0:T(8,128)(2,1)S(1)} %get-tuple-element.104), channel_id=1, source_target_pairs={{0,64},{1,17},{2,66},{3,19},{4,68},{5,21},{6,70},{7,23},{8,72},{9,... | collective-permute-start | bytes 393224 | tf_op jit(solution)/shard_map/ppermute | solution.py:385
  11.5 7.4 %collective-permute-start.5 = (bf16[128,512]{1,0:T(8,128)(2,1)S(1)}, bf16[128,512]{1,0:T(8,128)(2,1)S(1)}, u32[]{:S(2)}, u32[]{:S(2)}) collective-permute-start(bf16[128,512]{1,0:T(8,128)(2,1)S(1)} %get-tuple-element.105), channel_id=1, source_target_pairs={{0,96},{1,25},{2,98},{3,27},{4,100},{5,29},{6,102},{7,31},{8,104},... | collective-permute-start | bytes 393224 | tf_op jit(solution)/shard_map/ppermute | solution.py:385
  12.2 10.0 %collective-permute-start = (bf16[128,640]{1,0:T(8,128)(2,1)S(1)}, bf16[128,640]{1,0:T(8,128)(2,1)S(1)}, u32[]{:S(2)}, u32[]{:S(2)}) collective-permute-start(bf16[128,640]{1,0:T(8,128)(2,1)S(1)} %get-tuple-element.99), channel_id=1, source_target_pairs={{0,2},{1,3},{2,4},{3,5},{4,6},{5,7},{6,0},{7,1},{8,10},{9,11},{10,... | collective-permute-start | bytes 491528 | tf_op jit(solution)/shard_map/ppermute | solution.py:385
  13.5 12.4 %collective-permute-start.1 = (bf16[128,640]{1,0:T(8,128)(2,1)S(1)}, bf16[128,640]{1,0:T(8,128)(2,1)S(1)}, u32[]{:S(2)}, u32[]{:S(2)}) collective-permute-start(bf16[128,640]{1,0:T(8,128)(2,1)S(1)} %get-tuple-element.100), channel_id=1, source_target_pairs={{0,4},{1,5},{2,6},{3,7},{4,0},{5,1},{6,2},{7,3},{8,12},{9,13},{10,... | collective-permute-start | bytes 491528 | tf_op jit(solution)/shard_map/ppermute | solution.py:385
  17.7 8.2 %collective-permute-start.2 = (bf16[128,640]{1,0:T(8,128)(2,1)S(1)}, bf16[128,640]{1,0:T(8,128)(2,1)S(1)}, u32[]{:S(2)}, u32[]{:S(2)}) collective-permute-start(bf16[128,640]{1,0:T(8,128)(2,1)S(1)} %get-tuple-element.101), channel_id=1, source_target_pairs={{0,6},{1,7},{2,0},{3,1},{4,2},{5,3},{6,4},{7,5},{8,14},{9,15},{10,... | collective-permute-start | bytes 491528 | tf_op jit(solution)/shard_map/ppermute | solution.py:385
  19.0 6.9 %collective-permute-start.8 = (bf16[160,512]{1,0:T(8,128)(2,1)S(1)}, bf16[160,512]{1,0:T(8,128)(2,1)S(1)}, u32[]{:S(2)}, u32[]{:S(2)}) collective-permute-start(bf16[160,512]{1,0:T(8,128)(2,1)S(1)} %pad_maximum_fusion.4), channel_id=1, source_target_pairs={{0,24},{1,97},{2,26},{3,99},{4,28},{5,101},{6,30},{7,103},{8,0},{9... | collective-permute-start | bytes 491528 | tf_op jit(solution)/shard_map/ppermute | solution.py:385
  21.8 5.8 %collective-permute-start.7 = (bf16[160,512]{1,0:T(8,128)(2,1)S(1)}, bf16[160,512]{1,0:T(8,128)(2,1)S(1)}, u32[]{:S(2)}, u32[]{:S(2)}) collective-permute-start(bf16[160,512]{1,0:T(8,128)(2,1)S(1)} %pad_maximum_fusion.4), channel_id=1, source_target_pairs={{0,16},{1,65},{2,18},{3,67},{4,20},{5,69},{6,22},{7,71},{8,24},{9,... | collective-permute-start | bytes 491528 | tf_op jit(solution)/shard_map/ppermute | solution.py:385
  22.2 7.4 %collective-permute-start.6 = (bf16[160,512]{1,0:T(8,128)(2,1)S(1)}, bf16[160,512]{1,0:T(8,128)(2,1)S(1)}, u32[]{:S(2)}, u32[]{:S(2)}) collective-permute-start(bf16[160,512]{1,0:T(8,128)(2,1)S(1)} %pad_maximum_fusion.4), channel_id=1, source_target_pairs={{0,8},{1,33},{2,10},{3,35},{4,12},{5,37},{6,14},{7,39},{8,16},{9,4... | collective-permute-start | bytes 491528 | tf_op jit(solution)/shard_map/ppermute | solution.py:385
  29.6 4.8 %collective-permute-start.9 = (bf16[256,640]{1,0:T(8,128)(2,1)S(1)}, bf16[256,640]{1,0:T(8,128)(2,1)S(1)}, u32[]{:S(2)}, u32[]{:S(2)}) collective-permute-start(bf16[256,640]{1,0:T(8,128)(2,1)S(1)} %pad_maximum_fusion), channel_id=1, source_target_pairs={{0,1},{1,0},{2,3},{3,2},{4,5},{5,4},{6,7},{7,6},{8,9},{9,8},{10,11... | collective-permute-start | bytes 983048 | tf_op jit(solution)/shard_map/ppermute | solution.py:379
  34.1 5.7 %collective-permute-start.13 = (bf16[128,512]{1,0:T(8,128)(2,1)S(1)}, bf16[128,512]{1,0:T(8,128)(2,1)S(1)}, u32[]{:S(2)}, u32[]{:S(2)}) collective-permute-start(bf16[128,512]{1,0:T(8,128)(2,1)S(1)} %get-tuple-element.140.refs_1_.refs_0_), channel_id=1, source_target_pairs={{0,32},{1,9},{2,34},{3,11},{4,36},{5,13},{6,38},{7,15},{8,40},{9,1... | collective-permute-start | bytes 393224 | tf_op jit(solution)/shard_map/ppermute | solution.py:397
  35.1 7.2 %collective-permute-start.10 = (bf16[128,512]{1,0:T(8,128)(2,1)S(1)}, bf16[128,512]{1,0:T(8,128)(2,1)S(1)}, u32[]{:S(2)}, u32[]{:S(2)}) collective-permute-start(bf16[128,512]{1,0:T(8,128)(2,1)S(1)} %get-tuple-element.127), channel_id=1, source_target_pairs={{0,6},{1,7},{2,0},{3,1},{4,2},{5,3},{6,4},{7,5},{8,14},{9,15},{10,... | collective-permute-start | bytes 393224 | tf_op jit(solution)/shard_map/ppermute | solution.py:385
  35.2 7.2 %collective-permute-start.11 = (bf16[128,512]{1,0:T(8,128)(2,1)S(1)}, bf16[128,512]{1,0:T(8,128)(2,1)S(1)}, u32[]{:S(2)}, u32[]{:S(2)}) collective-permute-start(bf16[128,512]{1,0:T(8,128)(2,1)S(1)} %get-tuple-element.128), channel_id=1, source_target_pairs={{0,4},{1,5},{2,6},{3,7},{4,0},{5,1},{6,2},{7,3},{8,12},{9,13},{10,... | collective-permute-start | bytes 393224 | tf_op jit(solution)/shard_map/ppermute | solution.py:385
  37.3 7.1 %collective-permute-start.12 = (bf16[128,512]{1,0:T(8,128)(2,1)S(1)}, bf16[128,512]{1,0:T(8,128)(2,1)S(1)}, u32[]{:S(2)}, u32[]{:S(2)}) collective-permute-start(bf16[128,512]{1,0:T(8,128)(2,1)S(1)} %get-tuple-element.129), channel_id=1, source_target_pairs={{0,2},{1,3},{2,4},{3,5},{4,6},{5,7},{6,0},{7,1},{8,10},{9,11},{10,... | collective-permute-start | bytes 393224 | tf_op jit(solution)/shard_map/ppermute | solution.py:385
  37.3 7.2 %collective-permute-start.15 = (bf16[128,512]{1,0:T(8,128)(2,1)S(1)}, bf16[128,512]{1,0:T(8,128)(2,1)S(1)}, u32[]{:S(2)}, u32[]{:S(2)}) collective-permute-start(bf16[128,512]{1,0:T(8,128)(2,1)S(1)} %get-tuple-element.140.refs_1_.refs_0_), channel_id=1, source_target_pairs={{0,96},{1,25},{2,98},{3,27},{4,100},{5,29},{6,102},{7,31},{8,104},... | collective-permute-start | bytes 393224 | tf_op jit(solution)/shard_map/ppermute | solution.py:398
  39.8 5.3 %collective-permute-start.14 = (bf16[128,512]{1,0:T(8,128)(2,1)S(1)}, bf16[128,512]{1,0:T(8,128)(2,1)S(1)}, u32[]{:S(2)}, u32[]{:S(2)}) collective-permute-start(bf16[128,512]{1,0:T(8,128)(2,1)S(1)} %collective-permute-done.13.refs_1_), channel_id=1, source_target_pairs={{0,32},{1,9},{2,34},{3,11},{4,36},{5,13},{6,38},{7,15},{8,40},{9,1... | collective-permute-start | bytes 393224 | tf_op jit(solution)/shard_map/ppermute | solution.py:399
  45.1 6.8 %collective-permute-start.16 = (bf16[256,512]{1,0:T(8,128)(2,1)S(1)}, bf16[256,512]{1,0:T(8,128)(2,1)S(1)}, u32[]{:S(2)}, u32[]{:S(2)}) collective-permute-start(bf16[256,512]{1,0:T(8,128)(2,1)S(1)} %pad_maximum_fusion.1), channel_id=1, source_target_pairs={{0,1},{1,0},{2,3},{3,2},{4,5},{5,4},{6,7},{7,6},{8,9},{9,8},{10,11... | collective-permute-start | bytes 786440 | tf_op jit(solution)/shard_map/ppermute | solution.py:379
  49.2 9.0 %collective-permute-start.20 = (bf16[128,512]{1,0:T(8,128)(2,1)S(1)}, bf16[128,512]{1,0:T(8,128)(2,1)S(1)}, u32[]{:S(2)}, u32[]{:S(2)}) collective-permute-start(bf16[128,512]{1,0:T(8,128)(2,1)S(1)} %get-tuple-element.153), channel_id=1, source_target_pairs={{0,32},{1,9},{2,34},{3,11},{4,36},{5,13},{6,38},{7,15},{8,40},{9,1... | collective-permute-start | bytes 393224 | tf_op jit(solution)/shard_map/ppermute | solution.py:385
  49.3 10.1 %collective-permute-start.21 = (bf16[128,512]{1,0:T(8,128)(2,1)S(1)}, bf16[128,512]{1,0:T(8,128)(2,1)S(1)}, u32[]{:S(2)}, u32[]{:S(2)}) collective-permute-start(bf16[128,512]{1,0:T(8,128)(2,1)S(1)} %get-tuple-element.154), channel_id=1, source_target_pairs={{0,64},{1,17},{2,66},{3,19},{4,68},{5,21},{6,70},{7,23},{8,72},{9,... | collective-permute-start | bytes 393224 | tf_op jit(solution)/shard_map/ppermute | solution.py:385
  51.0 8.3 %collective-permute-start.22 = (bf16[128,512]{1,0:T(8,128)(2,1)S(1)}, bf16[128,512]{1,0:T(8,128)(2,1)S(1)}, u32[]{:S(2)}, u32[]{:S(2)}) collective-permute-start(bf16[128,512]{1,0:T(8,128)(2,1)S(1)} %get-tuple-element.155), channel_id=1, source_target_pairs={{0,96},{1,25},{2,98},{3,27},{4,100},{5,29},{6,102},{7,31},{8,104},... | collective-permute-start | bytes 393224 | tf_op jit(solution)/shard_map/ppermute | solution.py:385
  54.0 6.4 %collective-permute-start.17 = (bf16[128,512]{1,0:T(8,128)(2,1)S(1)}, bf16[128,512]{1,0:T(8,128)(2,1)S(1)}, u32[]{:S(2)}, u32[]{:S(2)}) collective-permute-start(bf16[128,512]{1,0:T(8,128)(2,1)S(1)} %get-tuple-element.149), channel_id=1, source_target_pairs={{0,2},{1,3},{2,4},{3,5},{4,6},{5,7},{6,0},{7,1},{8,10},{9,11},{10,... | collective-permute-start | bytes 393224 | tf_op jit(solution)/shard_map/ppermute | solution.py:385
  54.7 9.3 %collective-permute-start.18 = (bf16[128,512]{1,0:T(8,128)(2,1)S(1)}, bf16[128,512]{1,0:T(8,128)(2,1)S(1)}, u32[]{:S(2)}, u32[]{:S(2)}) collective-permute-start(bf16[128,512]{1,0:T(8,128)(2,1)S(1)} %get-tuple-element.150), channel_id=1, source_target_pairs={{0,4},{1,5},{2,6},{3,7},{4,0},{5,1},{6,2},{7,3},{8,12},{9,13},{10,... | collective-permute-start | bytes 393224 | tf_op jit(solution)/shard_map/ppermute | solution.py:385
  58.2 5.8 %collective-permute-start.19 = (bf16[128,512]{1,0:T(8,128)(2,1)S(1)}, bf16[128,512]{1,0:T(8,128)(2,1)S(1)}, u32[]{:S(2)}, u32[]{:S(2)}) collective-permute-start(bf16[128,512]{1,0:T(8,128)(2,1)S(1)} %get-tuple-element.151), channel_id=1, source_target_pairs={{0,6},{1,7},{2,0},{3,1},{4,2},{5,3},{6,4},{7,5},{8,14},{9,15},{10,... | collective-permute-start | bytes 393224 | tf_op jit(solution)/shard_map/ppermute | solution.py:385
  59.5 5.5 %collective-permute-start.24 = (bf16[128,512]{1,0:T(8,128)(2,1)S(1)}, bf16[128,512]{1,0:T(8,128)(2,1)S(1)}, u32[]{:S(2)}, u32[]{:S(2)}) collective-permute-start(bf16[128,512]{1,0:T(8,128)(2,1)S(1)} %pad_maximum_fusion.5), channel_id=1, source_target_pairs={{0,16},{1,65},{2,18},{3,67},{4,20},{5,69},{6,22},{7,71},{8,24},{9,... | collective-permute-start | bytes 393224 | tf_op jit(solution)/shard_map/ppermute | solution.py:385
  60.3 6.3 %collective-permute-start.23 = (bf16[128,512]{1,0:T(8,128)(2,1)S(1)}, bf16[128,512]{1,0:T(8,128)(2,1)S(1)}, u32[]{:S(2)}, u32[]{:S(2)}) collective-permute-start(bf16[128,512]{1,0:T(8,128)(2,1)S(1)} %pad_maximum_fusion.5), channel_id=1, source_target_pairs={{0,8},{1,33},{2,10},{3,35},{4,12},{5,37},{6,14},{7,39},{8,16},{9,4... | collective-permute-start | bytes 393224 | tf_op jit(solution)/shard_map/ppermute | solution.py:385
  69.8 6.8 %collective-permute-start.30 = (bf16[128,512]{1,0:T(8,128)(2,1)S(1)}, bf16[128,512]{1,0:T(8,128)(2,1)S(1)}, u32[]{:S(2)}, u32[]{:S(2)}) collective-permute-start(bf16[128,512]{1,0:T(8,128)(2,1)S(1)} %get-tuple-element.186.refs_1_.refs_0_), channel_id=1, source_target_pairs={{0,32},{1,9},{2,34},{3,11},{4,36},{5,13},{6,38},{7,15},{8,40},{9,1... | collective-permute-start | bytes 393224 | tf_op jit(solution)/shard_map/ppermute | solution.py:397
  71.5 7.1 %collective-permute-start.27 = (bf16[128,512]{1,0:T(8,128)(2,1)S(1)}, bf16[128,512]{1,0:T(8,128)(2,1)S(1)}, u32[]{:S(2)}, u32[]{:S(2)}) collective-permute-start(bf16[128,512]{1,0:T(8,128)(2,1)S(1)} %get-tuple-element.178), channel_id=1, source_target_pairs={{0,6},{1,7},{2,0},{3,1},{4,2},{5,3},{6,4},{7,5},{8,14},{9,15},{10,... | collective-permute-start | bytes 393224 | tf_op jit(solution)/shard_map/ppermute | solution.py:385
  72.0 6.7 %collective-permute-start.28 = (bf16[128,512]{1,0:T(8,128)(2,1)S(1)}, bf16[128,512]{1,0:T(8,128)(2,1)S(1)}, u32[]{:S(2)}, u32[]{:S(2)}) collective-permute-start(bf16[128,512]{1,0:T(8,128)(2,1)S(1)} %get-tuple-element.179), channel_id=1, source_target_pairs={{0,4},{1,5},{2,6},{3,7},{4,0},{5,1},{6,2},{7,3},{8,12},{9,13},{10,... | collective-permute-start | bytes 393224 | tf_op jit(solution)/shard_map/ppermute | solution.py:385
  74.1 7.2 %collective-permute-start.29 = (bf16[128,512]{1,0:T(8,128)(2,1)S(1)}, bf16[128,512]{1,0:T(8,128)(2,1)S(1)}, u32[]{:S(2)}, u32[]{:S(2)}) collective-permute-start(bf16[128,512]{1,0:T(8,128)(2,1)S(1)} %get-tuple-element.180), channel_id=1, source_target_pairs={{0,2},{1,3},{2,4},{3,5},{4,6},{5,7},{6,0},{7,1},{8,10},{9,11},{10,... | collective-permute-start | bytes 393224 | tf_op jit(solution)/shard_map/ppermute | solution.py:385
  74.9 6.5 %collective-permute-start.32 = (bf16[128,512]{1,0:T(8,128)(2,1)S(1)}, bf16[128,512]{1,0:T(8,128)(2,1)S(1)}, u32[]{:S(2)}, u32[]{:S(2)}) collective-permute-start(bf16[128,512]{1,0:T(8,128)(2,1)S(1)} %get-tuple-element.186.refs_1_.refs_0_), channel_id=1, source_target_pairs={{0,96},{1,25},{2,98},{3,27},{4,100},{5,29},{6,102},{7,31},{8,104},... | collective-permute-start | bytes 393224 | tf_op jit(solution)/shard_map/ppermute | solution.py:398
  76.6 5.3 %collective-permute-start.31 = (bf16[128,512]{1,0:T(8,128)(2,1)S(1)}, bf16[128,512]{1,0:T(8,128)(2,1)S(1)}, u32[]{:S(2)}, u32[]{:S(2)}) collective-permute-start(bf16[128,512]{1,0:T(8,128)(2,1)S(1)} %collective-permute-done.30.refs_1_), channel_id=1, source_target_pairs={{0,32},{1,9},{2,34},{3,11},{4,36},{5,13},{6,38},{7,15},{8,40},{9,1... | collective-permute-start | bytes 393224 | tf_op jit(solution)/shard_map/ppermute | solution.py:399
  87.6 14.1 %all-to-all-start = ((f32[128,1,128]{2,1,0:T(1,128)}), f32[128,1,128]{2,1,0:T(1,128)S(1)}, u32[]{:S(2)}, u32[]{:S(2)}) async-start(f32[128,1,128]{2,1,0:T(1,128)} %get-tuple-element.192), calls=%async_computation | async-start | bytes 131072 | tf_op jit(solution)/shard_map/all_to_all | solution.py:535
  (6 other events, 43.5 us)

commit v3 on v2

--- a/solution.py
+++ b/solution.py
@@ -67,8 +67,8 @@
     return [slice(i * TILE, (i + 1) * TILE) for i in range(NC // TILE)]
 
 
-def first(code, y_far, linking_far, x_far, cost_far, *refs):
-    *outs, y, linking, ylow, nsend, nback, lsend, lback, scol, x_top, cost_top, state, sem = refs
+def first(parent_far, section_far, y_far, linking_far, x_far, cost_far, *refs):
+    *outs, y, linking, ylow, nsend, nback, lsend, lback, scol, x_top, cost_top, state, parent_of, section_of, sem = refs
     chunks = parts()
     copies = []
     for cols in chunks:
@@ -77,12 +77,15 @@
     for cols in chunks:
         copies.append((linking_far.at[0, cols], linking.at[0, cols]))
     copies += [(x_far.at[:ROOTS], x_top), (cost_far.at[:ROOTS], cost_top)]
+    copies = [(parent_far, parent_of), (section_far, section_of)] + copies
     copies = [pltpu.make_async_copy(a, b, sem.at[i]) for i, (a, b) in enumerate(copies)]
     for copy in copies:
         copy.start()
-    packed = code[...]
-    upper = (packed >> 16) == 1
-    parent = packed & 0xFFFF
+    copies[0].wait()
+    copies[1].wait()
+    copies = copies[2:]
+    upper = section_of[...].reshape(1, NODES)[:, ROWS] == 1
+    parent = parent_of[...].reshape(1, NODES)[:, ROWS]
     here = lax.axis_index("leaf") * N_NODE + lax.axis_index("node")
     owner = ((parent.astype(F32) + 0.5) * (1.0 / NODES)).astype(jnp.int32)
     local = parent - owner * NODES
@@ -141,39 +144,11 @@
 def own_adjoint(ylow, scol, coupling, own):
     upper = jnp.concatenate([scol[...]] * (NS // 128), axis=1) == 1.0
     low = ylow[ROWS]
-    own[...] = jnp.where(upper, times(low, coupling[0]), times(low, coupling[1]))
-
-
-def own_root_first(ylow, cost_top, coupling_far, own_root, coupling_root, sem):
-    copies = [
-        pltpu.make_async_copy(coupling_far.at[0, cols], coupling_root.at[cols], sem.at[i])
-        for i, cols in enumerate(parts())
-    ]
-    for copy in copies:
-        copy.start()
-    total = -cost_top[...]
-    for copy, cols in zip(copies, parts()):
-        copy.wait()
-        total = total + times(ylow[:ROOTS, cols], coupling_root[cols])
-    own_root[...] = total
-
-
-def own_first(ylow, scol, coupling_far, own, coupling, sem):
-    copies = [
-        pltpu.make_async_copy(coupling_far.at[pl.ds(1, 2), cols], coupling.at[:, cols], sem.at[i])
-        for i, cols in enumerate(parts())
-    ]
-    for copy in copies:
-        copy.start()
-    first_total, second_total = None, None
-    for copy, cols in zip(copies, parts()):
-        copy.wait()
-        low = ylow[ROWS, cols]
-        one, two = times(low, coupling[0, cols]), times(low, coupling[1, cols])
-        first_total = one if first_total is None else first_total + one
-        second_total = two if second_total is None else second_total + two
-    upper = jnp.concatenate([scol[...]] * (NS // 128), axis=1) == 1.0
-    own[...] = jnp.where(upper, first_total, second_total)
+    own[...] = jnp.where(upper, times(low, coupling[1]), times(low, coupling[2]))
+
+
+def own_root_first(ylow, cost_top, coupling, own_root):
+    own_root[...] = times(ylow[:ROOTS], coupling[0]) - cost_top[...]
 
 
 def join(blocks, swapped, held):
@@ -260,7 +235,7 @@
 
 
 def own_image(
-    last, extra_child, extra_root, scol, coupling_root, coupling, y, right, rates, cost_top, base, *refs
+    last, extra_child, extra_root, scol, coupling, y, right, rates, cost_top, base, *refs
 ):
     sigma = rates[1:2, :1]
     upper = jnp.concatenate([scol[...]] * (TILE // 128), axis=1) == 1.0
@@ -269,9 +244,9 @@
     total = -cost_top[...]
     for cols in parts():
         image = jnp.where(
-            upper, times_t(child, coupling[0, cols]), times_t(child, coupling[1, cols])
+            upper, times_t(child, coupling[1, cols]), times_t(child, coupling[2, cols])
         )
-        weights = coupling_root[cols]
+        weights = coupling[0, cols]
         base_root = y[:ROOTS, cols] + sigma * (right[:ROOTS, cols] - times_t(root, weights))
         base[:ROOTS, cols] = base_root
         if not last:
@@ -418,7 +393,6 @@
 
 def shards(x_start, y_start, cost_vec, right_side, omega, coupling, linking, parent, section):
     unit = 2 * CHILD * NS * NC
-    code = (section * 65536 + parent)[ROOTS:].reshape(1, CHILD)
     rates = jnp.broadcast_to(jnp.stack([STEP / omega[0], STEP * omega[0]])[:, None], (2, 128))
     field = ((NODES, NC), F32)
     field_low = ((NODES, NC), BF16)
@@ -438,18 +412,17 @@
         first,
         [block_mark] * 4 + [block] * 4
         + [field, ((2, NC, NS), BF16), field_low, row, col, row, col, col, tops, tops, ((ROOTS, NS), BF16)],
-        [code, y_start, linking, x_start, cost_vec],
+        [parent, section, y_start, linking, x_start, cost_vec],
         2 * unit,
-        [pltpu.SemaphoreType.DMA((3 * NC // TILE + 2,))],
-        (1, 2, 3, 4),
-    )
-    chunk_sems = [pltpu.SemaphoreType.DMA((NC // TILE,))]
-    own_root, coupling_root = call(
-        own_root_first, [tops, ((NC, NS), BF16)], [ylow, cost_top, coupling], unit // 8, chunk_sems, (2,)
-    )
-    own, coupling = call(
-        own_first, [kids, ((2, NC, NS), BF16)], [ylow, scol, coupling], 2 * unit, chunk_sems, (2,)
-    )
+        [
+            pltpu.VMEM((NODES,), jnp.int32),
+            pltpu.VMEM((NODES,), jnp.int32),
+            pltpu.SemaphoreType.DMA((3 * NC // TILE + 4,)),
+        ],
+        (0, 1, 2, 3, 4, 5),
+    )
+    (own_root,) = call(own_root_first, [tops], [ylow, cost_top, coupling], unit // 8)
+    (own,) = call(own_adjoint, [kids], [ylow, scol, coupling], 2 * unit)
     got_leaf, _ = sum_leaf(sent[4:], own_root, state, own_root)
     got_node, (got_leaf, own) = swap_node(sent[:4], 1, (got_leaf, own))
 
@@ -471,7 +444,7 @@
         part_of(own_image, False),
         [field, tops],
         [
-            extra_child, extra_root, scol, coupling_root, coupling, y_start, right_side, rates, cost_top
+            extra_child, extra_root, scol, coupling, y_start, right_side, rates, cost_top
         ],
         2 * unit,
     )
@@ -517,7 +490,7 @@
     (base,) = call(
         part_of(own_image, True),
         [field],
-        [extra_child, extra_root, scol, coupling_root, coupling, y_next, right_side, rates, cost_top],
+        [extra_child, extra_root, scol, coupling, y_next, right_side, rates, cost_top],
         2 * unit,
     )
     back_leaf = ring_gather(extra_root, outer_ring)

time: 105 us -> 103 us (0.981)
  Pallas kernels: 23.8 us -> 21.2 us
  waiting for transfers between devices: 22.6 us -> 25.2 us
    pallas_call x15, Pallas kernels: 23.8 us -> 21.2 us  [call(): pl.pallas_call(kernel, out_shape=out_shapes, in_specs=[pl.BlockSpec(memor...]
    ppermute x24, waiting for transfers between devices: 13 us -> 15.6 us  [shifted(): got[k] = lax.ppermute(blocks[k], *ring(sign * k % 4))]
    ppermute x4, starting transfers between devices: 10.9 us -> 9.6 us  [sibling(): return lax.ppermute(array, *pairs_of(lambda y, z, x, c: (y, z, x, 1 - c)))]
    unnamed x8 -> x10, local copies, waits for them, and re-layouts: 2.24 us -> 2.25 us
  transfers between devices with their start and end apart: 35 -> 35, of which waited for: 13 -> 14; matrix products, arithmetic and copies ran while one was open for 3% -> 3% of each run, Pallas kernels for 17% -> 14%
where the time goes in v3:
time: 103 us
  starting transfers between devices  48.8 us (47%)
  waiting for transfers between devices  25.2 us (24%)
  Pallas kernels  21.2 us (21%)
  between operations  4.28 us (4%)
  local copies, waits for them, and re-layouts  3.1 us (3%)
    ppermute x24, starting transfers between devices, shifted(): got[k] = lax.ppermute(blocks[k], *ring(sign * k % 4))  30.3 us
    pallas_call x15, Pallas kernels, call(): pl.pallas_call(kernel, out_shape=out_shapes, in_specs=[pl.BlockSpec(memor...  21.2 us
    ppermute x24, waiting for transfers between devices, shifted(): got[k] = lax.ppermute(blocks[k], *ring(sign * k % 4))  15.6 us
    ppermute x4, starting transfers between devices, sibling(): return lax.ppermute(array, *pairs_of(lambda y, z, x, c: (y, z, x, 1 - c)))  9.6 us
    all_to_all x1, waiting for transfers between devices, shards(): lax.all_to_all(load, ('leaf', 'node'), split_axis=0, concat_axis=0, tiled...  7.23 us
    all_to_all x1, starting transfers between devices, shards(): lax.all_to_all(load, ('leaf', 'node'), split_axis=0, concat_axis=0, tiled...  4.59 us
    ppermute x2, starting transfers between devices, ring_gather(): three = lax.ppermute(rows, *ring(3))  4.19 us
    unnamed x10, local copies, waits for them, and re-layouts  2.25 us
  transfers between devices with their start and end apart: 35, of which 14 were waited for; matrix products, arithmetic and copies ran while one was open for 3% of the time, Pallas kernels for 14%

profile of v3, /device:TPU:1, one launch (start us, length us, event | category | flops | bytes accessed | tf_op | source)
XLA Modules:
  0.0 103.1 jit_solution(14530219529138818051)
XLA Ops:
  0.6 4.4 %shard_map.112 = (bf16[128,640]{1,0:T(8,128)(2,1)S(1)}, bf16[128,640]{1,0:T(8,128)(2,1)S(1)}, bf16[128,640]{1,0:T(8,128)(2,1)S(1)}, bf16[128,640]{1,0:T(8,128)(2...) custom-call(s32[288]{0:T(512)} %parent_far.1, ...), custom_call_target="tpu_custom_call" | custom-call | flops 1073741824 | bytes 2150944 | tf_op jit(solution)/shard_map/pallas_call | solution.py:55
  5.1 2.5 %collective-permute-start.3 = (bf16[128,512]{1,0:T(8,128)(2,1)S(1)}, bf16[128,512]{1,0:T(8,128)(2,1)S(1)}, u32[]{:S(2)}, u32[]{:S(2)}) collective-permute-start(bf16[128,512]{1,0:T(8,128)(2,1)S(1)} %get-tuple-element.99), channel_id=1, source_target_pairs={{0,32},{1,9},{2,34},{3,11},{4,36},{5,13},{6,38},{7,15},{8,40},{9,1... | collective-permute-start | bytes 393224 | tf_op jit(solution)/shard_map/ppermute | solution.py:360
  7.6 3.3 %collective-permute-start.4 = (bf16[128,512]{1,0:T(8,128)(2,1)S(1)}, bf16[128,512]{1,0:T(8,128)(2,1)S(1)}, u32[]{:S(2)}, u32[]{:S(2)}) collective-permute-start(bf16[128,512]{1,0:T(8,128)(2,1)S(1)} %get-tuple-element.100), channel_id=1, source_target_pairs={{0,64},{1,17},{2,66},{3,19},{4,68},{5,21},{6,70},{7,23},{8,72},{9,... | collective-permute-start | bytes 393224 | tf_op jit(solution)/shard_map/ppermute | solution.py:360
  12.9 2.4 %collective-permute-start.1 = (bf16[128,640]{1,0:T(8,128)(2,1)S(1)}, bf16[128,640]{1,0:T(8,128)(2,1)S(1)}, u32[]{:S(2)}, u32[]{:S(2)}) collective-permute-start(bf16[128,640]{1,0:T(8,128)(2,1)S(1)} %get-tuple-element.96), channel_id=1, source_target_pairs={{0,4},{1,5},{2,6},{3,7},{4,0},{5,1},{6,2},{7,3},{8,12},{9,13},{10,... | collective-permute-start | bytes 491528 | tf_op jit(solution)/shard_map/ppermute | solution.py:360
  17.1 2.8 %collective-permute-start.8 = (bf16[160,512]{1,0:T(8,128)(2,1)S(1)}, bf16[160,512]{1,0:T(8,128)(2,1)S(1)}, u32[]{:S(2)}, u32[]{:S(2)}) collective-permute-start(bf16[160,512]{1,0:T(8,128)(2,1)S(1)} %pad_maximum_fusion.4), channel_id=1, source_target_pairs={{0,24},{1,97},{2,26},{3,99},{4,28},{5,101},{6,30},{7,103},{8,0},{9... | collective-permute-start | bytes 491528 | tf_op jit(solution)/shard_map/ppermute | solution.py:360
  21.0 1.3 %shard_map.114.own = f32[256,512]{1,0:T(8,128)S(1)} custom-call(bf16[288,2048]{1,0:T(8,128)(2,1)S(1)} %get-tuple-element.102.ylow, f32[256,128]{1,0:T(8,128)S(1)} %get-tuple-element.109.scol.refs_2_, bf16[3,2048,512]{2,1,0:T(8,128)(2,1)S(1)} %copy-done), custom_call_target="tpu_custom_call" | custom-call | flops 1073741824 | bytes 1015808 | tf_op jit(solution)/shard_map/pallas_call | solution.py:55
  22.4 1.5 %collective-permute-done.8.g3 = bf16[160,512]{1,0:T(8,128)(2,1)S(1)} collective-permute-done((bf16[160,512]{1,0:T(8,128)(2,1)S(1)}, bf16[160,512]{1,0:T(8,128)(2,1)S(1)}, u32[]{:S(2)}, u32[]{:S(2)}) %collective-permute-start.8) | collective-permute-done | bytes 163872 | tf_op jit(solution)/shard_map/ppermute | solution.py:360
  24.0 1.8 %collective-permute-done.7.g2 = bf16[160,512]{1,0:T(8,128)(2,1)S(1)} collective-permute-done((bf16[160,512]{1,0:T(8,128)(2,1)S(1)}, bf16[160,512]{1,0:T(8,128)(2,1)S(1)}, u32[]{:S(2)}, u32[]{:S(2)}) %collective-permute-start.7) | collective-permute-done | bytes 163872 | tf_op jit(solution)/shard_map/ppermute | solution.py:360
  25.7 1.9 %collective-permute-done.6.g1 = bf16[160,512]{1,0:T(8,128)(2,1)S(1)} collective-permute-done((bf16[160,512]{1,0:T(8,128)(2,1)S(1)}, bf16[160,512]{1,0:T(8,128)(2,1)S(1)}, u32[]{:S(2)}, u32[]{:S(2)}) %collective-permute-start.6) | collective-permute-done | bytes 163872 | tf_op jit(solution)/shard_map/ppermute | solution.py:360
  27.7 3.5 %collective-permute-start.9 = (bf16[256,640]{1,0:T(8,128)(2,1)S(1)}, bf16[256,640]{1,0:T(8,128)(2,1)S(1)}, u32[]{:S(2)}, u32[]{:S(2)}) collective-permute-start(bf16[256,640]{1,0:T(8,128)(2,1)S(1)} %pad_maximum_fusion), channel_id=1, source_target_pairs={{0,1},{1,0},{2,3},{3,2},{4,5},{5,4},{6,7},{7,6},{8,9},{9,8},{10,11... | collective-permute-start | bytes 983048 | tf_op jit(solution)/shard_map/ppermute | solution.py:354
  33.3 2.1 %collective-permute-start.11 = (bf16[128,512]{1,0:T(8,128)(2,1)S(1)}, bf16[128,512]{1,0:T(8,128)(2,1)S(1)}, u32[]{:S(2)}, u32[]{:S(2)}) collective-permute-start(bf16[128,512]{1,0:T(8,128)(2,1)S(1)} %get-tuple-element.122), channel_id=1, source_target_pairs={{0,4},{1,5},{2,6},{3,7},{4,0},{5,1},{6,2},{7,3},{8,12},{9,13},{10,... | collective-permute-start | bytes 393224 | tf_op jit(solution)/shard_map/ppermute | solution.py:360
  35.4 2.5 %collective-permute-start.15 = (bf16[128,512]{1,0:T(8,128)(2,1)S(1)}, bf16[128,512]{1,0:T(8,128)(2,1)S(1)}, u32[]{:S(2)}, u32[]{:S(2)}) collective-permute-start(bf16[128,512]{1,0:T(8,128)(2,1)S(1)} %get-tuple-element.132.refs_1_.refs_0_), channel_id=1, source_target_pairs={{0,96},{1,25},{2,98},{3,27},{4,100},{5,29},{6,102},{7,31},{8,104},... | collective-permute-start | bytes 393224 | tf_op jit(solution)/shard_map/ppermute | solution.py:373
  37.9 2.6 %shard_map.117 = (f32[288,2048]{1,0:T(8,128)S(1)}, f32[32,512]{1,0:T(8,128)S(1)}) custom-call(bf16[256,512]{1,0:T(8,128)(2,1)S(1)} %get-tuple-element.125.refs_0_, bf16[128,512]{1,0:T(8,128)(2,1)S(1)} %get-tuple-element.132.refs_1_.refs_0_, f32[256,128]{1,0:T(8,128)S(1)} %get-tuple-element.109.scol.refs_2_, bf16[3,2048,512]{2,1,0:T(8,128)(2,1)S(1)} %copy-done, ...), custom_call_target="tpu_custom_call" | custom-call | flops 1073741824 | bytes 1753216 | tf_op jit(solution)/shard_map/pallas_call | solution.py:55
  40.5 2.0 %collective-permute-done.12.g3 = bf16[128,512]{1,0:T(8,128)(2,1)S(1)} collective-permute-done((bf16[128,512]{1,0:T(8,128)(2,1)S(1)}, bf16[128,512]{1,0:T(8,128)(2,1)S(1)}, u32[]{:S(2)}, u32[]{:S(2)}) %collective-permute-start.12) | collective-permute-done | bytes 131104 | tf_op jit(solution)/shard_map/ppermute | solution.py:360
  43.2 2.0 %collective-permute-start.16 = (bf16[256,512]{1,0:T(8,128)(2,1)S(1)}, bf16[256,512]{1,0:T(8,128)(2,1)S(1)}, u32[]{:S(2)}, u32[]{:S(2)}) collective-permute-start(bf16[256,512]{1,0:T(8,128)(2,1)S(1)} %pad_maximum_fusion.1), channel_id=1, source_target_pairs={{0,1},{1,0},{2,3},{3,2},{4,5},{5,4},{6,7},{7,6},{8,9},{9,8},{10,11... | collective-permute-start | bytes 786440 | tf_op jit(solution)/shard_map/ppermute | solution.py:354
  45.2 2.1 %shard_map.118 = (f32[256,2048]{1,0:T(8,128)S(1)}, bf16[128,512]{1,0:T(8,128)(2,1)S(1)}, bf16[128,512]{1,0:T(8,128)(2,1)S(1)}, bf16[128,512]{1,0:T(8,128)(2,1)S(1)}, bf16[128,512]{1,0:T(8,128)(2,1)S(1)}) custom-call(bf16[128,512]{1,0:T(8,128)(2,1)S(1)} %get-tuple-element.132.refs_1_.refs_0_, bf16[128,512]{1,0:T(8,128)(2,1)S(1)} %collective-permute-done.13.refs_1_, ...), custom_call_target="tpu_custom_call" | custom-call | flops 1073741824 | bytes 1229056 | tf_op jit(solution)/shard_map/pallas_call | solution.py:55
  47.4 1.8 %collective-permute-start.21 = (bf16[128,512]{1,0:T(8,128)(2,1)S(1)}, bf16[128,512]{1,0:T(8,128)(2,1)S(1)}, u32[]{:S(2)}, u32[]{:S(2)}) collective-permute-start(bf16[128,512]{1,0:T(8,128)(2,1)S(1)} %get-tuple-element.146), channel_id=1, source_target_pairs={{0,64},{1,17},{2,66},{3,19},{4,68},{5,21},{6,70},{7,23},{8,72},{9,... | collective-permute-start | bytes 393224 | tf_op jit(solution)/shard_map/ppermute | solution.py:360
  50.1 2.1 %shard_map.119 = (f32[288,2048]{1,0:T(8,128)S(1)}, bf16[288,2048]{1,0:T(8,128)(2,1)S(1)}, bf16[128,512]{1,0:T(8,128)(2,1)S(1)}, bf16[128,512]{1,0:T(8,128)(2,1)S...) custom-call(bf16[128,512]{1,0:T(8,128)(2,1)S(1)} %get-tuple-element.120.g0, ...), custom_call_target="tpu_custom_call" | custom-call | flops 1073741824 | bytes 1704192 | tf_op jit(solution)/shard_map/pallas_call | solution.py:55
  52.9 3.4 %collective-permute-start.18 = (bf16[128,512]{1,0:T(8,128)(2,1)S(1)}, bf16[128,512]{1,0:T(8,128)(2,1)S(1)}, u32[]{:S(2)}, u32[]{:S(2)}) collective-permute-start(bf16[128,512]{1,0:T(8,128)(2,1)S(1)} %get-tuple-element.142), channel_id=1, source_target_pairs={{0,4},{1,5},{2,6},{3,7},{4,0},{5,1},{6,2},{7,3},{8,12},{9,13},{10,... | collective-permute-start | bytes 393224 | tf_op jit(solution)/shard_map/ppermute | solution.py:360
  59.3 1.3 %shard_map.120.own = f32[256,512]{1,0:T(8,128)S(1)} custom-call(bf16[288,2048]{1,0:T(8,128)(2,1)S(1)} %get-tuple-element.154.ylow, f32[256,128]{1,0:T(8,128)S(1)} %get-tuple-element.109.scol.refs_2_, bf16[3,2048,512]{2,1,0:T(8,128)(2,1)S(1)} %copy-done), custom_call_target="tpu_custom_call" | custom-call | flops 1073741824 | bytes 1015808 | tf_op jit(solution)/shard_map/pallas_call | solution.py:55
  60.6 1.6 %collective-permute-done.18.g2 = bf16[128,512]{1,0:T(8,128)(2,1)S(1)} collective-permute-done((bf16[128,512]{1,0:T(8,128)(2,1)S(1)}, bf16[128,512]{1,0:T(8,128)(2,1)S(1)}, u32[]{:S(2)}, u32[]{:S(2)}) %collective-permute-start.18) | collective-permute-done | bytes 131104 | tf_op jit(solution)/shard_map/ppermute | solution.py:360
  63.2 2.9 %collective-permute-done.23.g1 = bf16[128,512]{1,0:T(8,128)(2,1)S(1)} collective-permute-done((bf16[128,512]{1,0:T(8,128)(2,1)S(1)}, bf16[128,512]{1,0:T(8,128)(2,1)S(1)}, u32[]{:S(2)}, u32[]{:S(2)}) %collective-permute-start.23) | collective-permute-done | bytes 131104 | tf_op jit(solution)/shard_map/ppermute | solution.py:360
  66.1 1.8 %collective-permute-start.26 = (bf16[256,512]{1,0:T(8,128)(2,1)S(1)}, bf16[256,512]{1,0:T(8,128)(2,1)S(1)}, u32[]{:S(2)}, u32[]{:S(2)}) collective-permute-start(bf16[256,512]{1,0:T(8,128)(2,1)S(1)} %pad_maximum_fusion.2), channel_id=1, source_target_pairs={{0,1},{1,0},{2,3},{3,2},{4,5},{5,4},{6,7},{7,6},{8,9},{9,8},{10,11... | collective-permute-start | bytes 786440 | tf_op jit(solution)/shard_map/ppermute | solution.py:354
  70.2 2.1 %collective-permute-start.28 = (bf16[128,512]{1,0:T(8,128)(2,1)S(1)}, bf16[128,512]{1,0:T(8,128)(2,1)S(1)}, u32[]{:S(2)}, u32[]{:S(2)}) collective-permute-start(bf16[128,512]{1,0:T(8,128)(2,1)S(1)} %get-tuple-element.171), channel_id=1, source_target_pairs={{0,4},{1,5},{2,6},{3,7},{4,0},{5,1},{6,2},{7,3},{8,12},{9,13},{10,... | collective-permute-start | bytes 393224 | tf_op jit(solution)/shard_map/ppermute | solution.py:360
  73.1 1.7 %collective-permute-start.32 = (bf16[128,512]{1,0:T(8,128)(2,1)S(1)}, bf16[128,512]{1,0:T(8,128)(2,1)S(1)}, u32[]{:S(2)}, u32[]{:S(2)}) collective-permute-start(bf16[128,512]{1,0:T(8,128)(2,1)S(1)} %get-tuple-element.178.refs_1_.refs_0_), channel_id=1, source_target_pairs={{0,96},{1,25},{2,98},{3,27},{4,100},{5,29},{6,102},{7,31},{8,104},... | collective-permute-start | bytes 393224 | tf_op jit(solution)/shard_map/ppermute | solution.py:373
  74.8 2.0 %shard_map.124.refs_6_.base = f32[288,2048]{1,0:T(8,128)S(1)} custom-call(bf16[256,512]{1,0:T(8,128)(2,1)S(1)} %get-tuple-element.174.refs_0_, bf16[128,512]{1,0:T(8,128)(2,1)S(1)} %get-tuple-element.178.refs_1_.refs_0_, f32[256,128]{1,0:T(8,128)S(1)} %get-tuple-element.109.scol.refs_2_, bf16[3,2048,512]{2,1,0:T(8,128)(2,1)S(1)} %copy-done, ...), custom_call_target="tpu_custom_call" | custom-call | flops 1073741824 | bytes 1745024 | tf_op jit(solution)/shard_map/pallas_call | solution.py:55
  76.9 2.6 %collective-permute-done.29.g3 = bf16[128,512]{1,0:T(8,128)(2,1)S(1)} collective-permute-done((bf16[128,512]{1,0:T(8,128)(2,1)S(1)}, bf16[128,512]{1,0:T(8,128)(2,1)S(1)}, u32[]{:S(2)}, u32[]{:S(2)}) %collective-permute-start.29) | collective-permute-done | bytes 131104 | tf_op jit(solution)/shard_map/ppermute | solution.py:360
  80.1 2.3 %collective-permute-start.33 = (bf16[256,512]{1,0:T(8,128)(2,1)S(1)}, bf16[256,512]{1,0:T(8,128)(2,1)S(1)}, u32[]{:S(2)}, u32[]{:S(2)}) collective-permute-start(bf16[256,512]{1,0:T(8,128)(2,1)S(1)} %pad_maximum_fusion.3), channel_id=1, source_target_pairs={{0,1},{1,0},{2,3},{3,2},{4,5},{5,4},{6,7},{7,6},{8,9},{9,8},{10,11... | collective-permute-start | bytes 786440 | tf_op jit(solution)/shard_map/ppermute | solution.py:354
  83.8 2.0 %shard_map.126 = (f32[288,2048]{1,0:T(8,128)S(1)}, f32[128,1,128]{2,1,0:T(1,128)}) custom-call(bf16[128,512]{1,0:T(8,128)(2,1)S(1)} %get-tuple-element.169.g0, bf16[128,512]{1,0:T(8,128)(2,1)S(1)} %collective-permute-done.27.g1, bf16[128,512]{1,0:T(8,128)(2,1)S(1)} %collective-permute-done.28.g2, bf16[128,512]{1,0:T(8,128)(2,1)S(1)} %collective-permute-done.29.g3, ...), custom_call_target="tpu_custom_call" | custom-call | flops 536870912 | bytes 2089600 | tf_op jit(solution)/shard_map/pallas_call | solution.py:55
  85.8 4.6 %all-to-all-start = ((f32[128,1,128]{2,1,0:T(1,128)}), f32[128,1,128]{2,1,0:T(1,128)S(1)}, u32[]{:S(2)}, u32[]{:S(2)}) async-start(f32[128,1,128]{2,1,0:T(1,128)} %get-tuple-element.184), calls=%async_computation | async-start | bytes 131072 | tf_op jit(solution)/shard_map/all_to_all | solution.py:508
  91.2 1.4 %copy.13 = f32[288,2048]{1,0:T(8,128)} copy(f32[288,2048]{1,0:T(8,128)S(1)} %get-tuple-element.192) | data formatting | bytes 4718592
  92.6 7.2 %all-to-all-done = f32[128,1,128]{2,1,0:T(1,128)S(1)} async-done(((f32[128,1,128]{2,1,0:T(1,128)}), f32[128,1,128]{2,1,0:T(1,128)S(1)}, u32[]{:S(2)}, u32[]{:S(2)}) %all-to-all-start) | async-done | bytes 65568 | tf_op jit(solution)/shard_map/all_to_all | solution.py:508
  (95 shorter events, 19.3 us)
Async XLA Ops:
  5.1 10.7 %collective-permute-start.3 = (bf16[128,512]{1,0:T(8,128)(2,1)S(1)}, bf16[128,512]{1,0:T(8,128)(2,1)S(1)}, u32[]{:S(2)}, u32[]{:S(2)}) collective-permute-start(bf16[128,512]{1,0:T(8,128)(2,1)S(1)} %get-tuple-element.99), channel_id=1, source_target_pairs={{0,32},{1,9},{2,34},{3,11},{4,36},{5,13},{6,38},{7,15},{8,40},{9,1... | collective-permute-start | bytes 393224 | tf_op jit(solution)/shard_map/ppermute | solution.py:360
  7.6 9.4 %collective-permute-start.4 = (bf16[128,512]{1,0:T(8,128)(2,1)S(1)}, bf16[128,512]{1,0:T(8,128)(2,1)S(1)}, u32[]{:S(2)}, u32[]{:S(2)}) collective-permute-start(bf16[128,512]{1,0:T(8,128)(2,1)S(1)} %get-tuple-element.100), channel_id=1, source_target_pairs={{0,64},{1,17},{2,66},{3,19},{4,68},{5,21},{6,70},{7,23},{8,72},{9,... | collective-permute-start | bytes 393224 | tf_op jit(solution)/shard_map/ppermute | solution.py:360
  10.9 6.1 %collective-permute-start.5 = (bf16[128,512]{1,0:T(8,128)(2,1)S(1)}, bf16[128,512]{1,0:T(8,128)(2,1)S(1)}, u32[]{:S(2)}, u32[]{:S(2)}) collective-permute-start(bf16[128,512]{1,0:T(8,128)(2,1)S(1)} %get-tuple-element.101), channel_id=1, source_target_pairs={{0,96},{1,25},{2,98},{3,27},{4,100},{5,29},{6,102},{7,31},{8,104},... | collective-permute-start | bytes 393224 | tf_op jit(solution)/shard_map/ppermute | solution.py:360
  11.6 8.6 %collective-permute-start = (bf16[128,640]{1,0:T(8,128)(2,1)S(1)}, bf16[128,640]{1,0:T(8,128)(2,1)S(1)}, u32[]{:S(2)}, u32[]{:S(2)}) collective-permute-start(bf16[128,640]{1,0:T(8,128)(2,1)S(1)} %get-tuple-element.95), channel_id=1, source_target_pairs={{0,2},{1,3},{2,4},{3,5},{4,6},{5,7},{6,0},{7,1},{8,10},{9,11},{10,... | collective-permute-start | bytes 491528 | tf_op jit(solution)/shard_map/ppermute | solution.py:360
  12.9 9.5 %collective-permute-start.1 = (bf16[128,640]{1,0:T(8,128)(2,1)S(1)}, bf16[128,640]{1,0:T(8,128)(2,1)S(1)}, u32[]{:S(2)}, u32[]{:S(2)}) collective-permute-start(bf16[128,640]{1,0:T(8,128)(2,1)S(1)} %get-tuple-element.96), channel_id=1, source_target_pairs={{0,4},{1,5},{2,6},{3,7},{4,0},{5,1},{6,2},{7,3},{8,12},{9,13},{10,... | collective-permute-start | bytes 491528 | tf_op jit(solution)/shard_map/ppermute | solution.py:360
  15.8 6.6 %collective-permute-start.2 = (bf16[128,640]{1,0:T(8,128)(2,1)S(1)}, bf16[128,640]{1,0:T(8,128)(2,1)S(1)}, u32[]{:S(2)}, u32[]{:S(2)}) collective-permute-start(bf16[128,640]{1,0:T(8,128)(2,1)S(1)} %get-tuple-element.97), channel_id=1, source_target_pairs={{0,6},{1,7},{2,0},{3,1},{4,2},{5,3},{6,4},{7,5},{8,14},{9,15},{10,... | collective-permute-start | bytes 491528 | tf_op jit(solution)/shard_map/ppermute | solution.py:360
  17.1 6.8 %collective-permute-start.8 = (bf16[160,512]{1,0:T(8,128)(2,1)S(1)}, bf16[160,512]{1,0:T(8,128)(2,1)S(1)}, u32[]{:S(2)}, u32[]{:S(2)}) collective-permute-start(bf16[160,512]{1,0:T(8,128)(2,1)S(1)} %pad_maximum_fusion.4), channel_id=1, source_target_pairs={{0,24},{1,97},{2,26},{3,99},{4,28},{5,101},{6,30},{7,103},{8,0},{9... | collective-permute-start | bytes 491528 | tf_op jit(solution)/shard_map/ppermute | solution.py:360
  20.0 5.8 %collective-permute-start.7 = (bf16[160,512]{1,0:T(8,128)(2,1)S(1)}, bf16[160,512]{1,0:T(8,128)(2,1)S(1)}, u32[]{:S(2)}, u32[]{:S(2)}) collective-permute-start(bf16[160,512]{1,0:T(8,128)(2,1)S(1)} %pad_maximum_fusion.4), channel_id=1, source_target_pairs={{0,16},{1,65},{2,18},{3,67},{4,20},{5,69},{6,22},{7,71},{8,24},{9,... | collective-permute-start | bytes 491528 | tf_op jit(solution)/shard_map/ppermute | solution.py:360
  20.3 7.4 %collective-permute-start.6 = (bf16[160,512]{1,0:T(8,128)(2,1)S(1)}, bf16[160,512]{1,0:T(8,128)(2,1)S(1)}, u32[]{:S(2)}, u32[]{:S(2)}) collective-permute-start(bf16[160,512]{1,0:T(8,128)(2,1)S(1)} %pad_maximum_fusion.4), channel_id=1, source_target_pairs={{0,8},{1,33},{2,10},{3,35},{4,12},{5,37},{6,14},{7,39},{8,16},{9,4... | collective-permute-start | bytes 491528 | tf_op jit(solution)/shard_map/ppermute | solution.py:360
  27.7 4.8 %collective-permute-start.9 = (bf16[256,640]{1,0:T(8,128)(2,1)S(1)}, bf16[256,640]{1,0:T(8,128)(2,1)S(1)}, u32[]{:S(2)}, u32[]{:S(2)}) collective-permute-start(bf16[256,640]{1,0:T(8,128)(2,1)S(1)} %pad_maximum_fusion), channel_id=1, source_target_pairs={{0,1},{1,0},{2,3},{3,2},{4,5},{5,4},{6,7},{7,6},{8,9},{9,8},{10,11... | collective-permute-start | bytes 983048 | tf_op jit(solution)/shard_map/ppermute | solution.py:354
  32.2 5.7 %collective-permute-start.13 = (bf16[128,512]{1,0:T(8,128)(2,1)S(1)}, bf16[128,512]{1,0:T(8,128)(2,1)S(1)}, u32[]{:S(2)}, u32[]{:S(2)}) collective-permute-start(bf16[128,512]{1,0:T(8,128)(2,1)S(1)} %get-tuple-element.132.refs_1_.refs_0_), channel_id=1, source_target_pairs={{0,32},{1,9},{2,34},{3,11},{4,36},{5,13},{6,38},{7,15},{8,40},{9,1... | collective-permute-start | bytes 393224 | tf_op jit(solution)/shard_map/ppermute | solution.py:372
  33.2 7.3 %collective-permute-start.10 = (bf16[128,512]{1,0:T(8,128)(2,1)S(1)}, bf16[128,512]{1,0:T(8,128)(2,1)S(1)}, u32[]{:S(2)}, u32[]{:S(2)}) collective-permute-start(bf16[128,512]{1,0:T(8,128)(2,1)S(1)} %get-tuple-element.121), channel_id=1, source_target_pairs={{0,6},{1,7},{2,0},{3,1},{4,2},{5,3},{6,4},{7,5},{8,14},{9,15},{10,... | collective-permute-start | bytes 393224 | tf_op jit(solution)/shard_map/ppermute | solution.py:360
  33.3 7.2 %collective-permute-start.11 = (bf16[128,512]{1,0:T(8,128)(2,1)S(1)}, bf16[128,512]{1,0:T(8,128)(2,1)S(1)}, u32[]{:S(2)}, u32[]{:S(2)}) collective-permute-start(bf16[128,512]{1,0:T(8,128)(2,1)S(1)} %get-tuple-element.122), channel_id=1, source_target_pairs={{0,4},{1,5},{2,6},{3,7},{4,0},{5,1},{6,2},{7,3},{8,12},{9,13},{10,... | collective-permute-start | bytes 393224 | tf_op jit(solution)/shard_map/ppermute | solution.py:360
  35.4 7.1 %collective-permute-start.12 = (bf16[128,512]{1,0:T(8,128)(2,1)S(1)}, bf16[128,512]{1,0:T(8,128)(2,1)S(1)}, u32[]{:S(2)}, u32[]{:S(2)}) collective-permute-start(bf16[128,512]{1,0:T(8,128)(2,1)S(1)} %get-tuple-element.123), channel_id=1, source_target_pairs={{0,2},{1,3},{2,4},{3,5},{4,6},{5,7},{6,0},{7,1},{8,10},{9,11},{10,... | collective-permute-start | bytes 393224 | tf_op jit(solution)/shard_map/ppermute | solution.py:360
  35.4 7.1 %collective-permute-start.15 = (bf16[128,512]{1,0:T(8,128)(2,1)S(1)}, bf16[128,512]{1,0:T(8,128)(2,1)S(1)}, u32[]{:S(2)}, u32[]{:S(2)}) collective-permute-start(bf16[128,512]{1,0:T(8,128)(2,1)S(1)} %get-tuple-element.132.refs_1_.refs_0_), channel_id=1, source_target_pairs={{0,96},{1,25},{2,98},{3,27},{4,100},{5,29},{6,102},{7,31},{8,104},... | collective-permute-start | bytes 393224 | tf_op jit(solution)/shard_map/ppermute | solution.py:373
  37.9 5.3 %collective-permute-start.14 = (bf16[128,512]{1,0:T(8,128)(2,1)S(1)}, bf16[128,512]{1,0:T(8,128)(2,1)S(1)}, u32[]{:S(2)}, u32[]{:S(2)}) collective-permute-start(bf16[128,512]{1,0:T(8,128)(2,1)S(1)} %collective-permute-done.13.refs_1_), channel_id=1, source_target_pairs={{0,32},{1,9},{2,34},{3,11},{4,36},{5,13},{6,38},{7,15},{8,40},{9,1... | collective-permute-start | bytes 393224 | tf_op jit(solution)/shard_map/ppermute | solution.py:374
  43.2 6.9 %collective-permute-start.16 = (bf16[256,512]{1,0:T(8,128)(2,1)S(1)}, bf16[256,512]{1,0:T(8,128)(2,1)S(1)}, u32[]{:S(2)}, u32[]{:S(2)}) collective-permute-start(bf16[256,512]{1,0:T(8,128)(2,1)S(1)} %pad_maximum_fusion.1), channel_id=1, source_target_pairs={{0,1},{1,0},{2,3},{3,2},{4,5},{5,4},{6,7},{7,6},{8,9},{9,8},{10,11... | collective-permute-start | bytes 786440 | tf_op jit(solution)/shard_map/ppermute | solution.py:354
  47.3 9.0 %collective-permute-start.20 = (bf16[128,512]{1,0:T(8,128)(2,1)S(1)}, bf16[128,512]{1,0:T(8,128)(2,1)S(1)}, u32[]{:S(2)}, u32[]{:S(2)}) collective-permute-start(bf16[128,512]{1,0:T(8,128)(2,1)S(1)} %get-tuple-element.145), channel_id=1, source_target_pairs={{0,32},{1,9},{2,34},{3,11},{4,36},{5,13},{6,38},{7,15},{8,40},{9,1... | collective-permute-start | bytes 393224 | tf_op jit(solution)/shard_map/ppermute | solution.py:360
  47.4 10.1 %collective-permute-start.21 = (bf16[128,512]{1,0:T(8,128)(2,1)S(1)}, bf16[128,512]{1,0:T(8,128)(2,1)S(1)}, u32[]{:S(2)}, u32[]{:S(2)}) collective-permute-start(bf16[128,512]{1,0:T(8,128)(2,1)S(1)} %get-tuple-element.146), channel_id=1, source_target_pairs={{0,64},{1,17},{2,66},{3,19},{4,68},{5,21},{6,70},{7,23},{8,72},{9,... | collective-permute-start | bytes 393224 | tf_op jit(solution)/shard_map/ppermute | solution.py:360
  49.2 8.2 %collective-permute-start.22 = (bf16[128,512]{1,0:T(8,128)(2,1)S(1)}, bf16[128,512]{1,0:T(8,128)(2,1)S(1)}, u32[]{:S(2)}, u32[]{:S(2)}) collective-permute-start(bf16[128,512]{1,0:T(8,128)(2,1)S(1)} %get-tuple-element.147), channel_id=1, source_target_pairs={{0,96},{1,25},{2,98},{3,27},{4,100},{5,29},{6,102},{7,31},{8,104},... | collective-permute-start | bytes 393224 | tf_op jit(solution)/shard_map/ppermute | solution.py:360
  52.1 6.2 %collective-permute-start.17 = (bf16[128,512]{1,0:T(8,128)(2,1)S(1)}, bf16[128,512]{1,0:T(8,128)(2,1)S(1)}, u32[]{:S(2)}, u32[]{:S(2)}) collective-permute-start(bf16[128,512]{1,0:T(8,128)(2,1)S(1)} %get-tuple-element.141), channel_id=1, source_target_pairs={{0,2},{1,3},{2,4},{3,5},{4,6},{5,7},{6,0},{7,1},{8,10},{9,11},{10,... | collective-permute-start | bytes 393224 | tf_op jit(solution)/shard_map/ppermute | solution.py:360
  52.9 9.2 %collective-permute-start.18 = (bf16[128,512]{1,0:T(8,128)(2,1)S(1)}, bf16[128,512]{1,0:T(8,128)(2,1)S(1)}, u32[]{:S(2)}, u32[]{:S(2)}) collective-permute-start(bf16[128,512]{1,0:T(8,128)(2,1)S(1)} %get-tuple-element.142), channel_id=1, source_target_pairs={{0,4},{1,5},{2,6},{3,7},{4,0},{5,1},{6,2},{7,3},{8,12},{9,13},{10,... | collective-permute-start | bytes 393224 | tf_op jit(solution)/shard_map/ppermute | solution.py:360
  56.3 5.8 %collective-permute-start.19 = (bf16[128,512]{1,0:T(8,128)(2,1)S(1)}, bf16[128,512]{1,0:T(8,128)(2,1)S(1)}, u32[]{:S(2)}, u32[]{:S(2)}) collective-permute-start(bf16[128,512]{1,0:T(8,128)(2,1)S(1)} %get-tuple-element.143), channel_id=1, source_target_pairs={{0,6},{1,7},{2,0},{3,1},{4,2},{5,3},{6,4},{7,5},{8,14},{9,15},{10,... | collective-permute-start | bytes 393224 | tf_op jit(solution)/shard_map/ppermute | solution.py:360
  57.7 5.5 %collective-permute-start.24 = (bf16[128,512]{1,0:T(8,128)(2,1)S(1)}, bf16[128,512]{1,0:T(8,128)(2,1)S(1)}, u32[]{:S(2)}, u32[]{:S(2)}) collective-permute-start(bf16[128,512]{1,0:T(8,128)(2,1)S(1)} %pad_maximum_fusion.5), channel_id=1, source_target_pairs={{0,16},{1,65},{2,18},{3,67},{4,20},{5,69},{6,22},{7,71},{8,24},{9,... | collective-permute-start | bytes 393224 | tf_op jit(solution)/shard_map/ppermute | solution.py:360
  58.3 7.8 %collective-permute-start.23 = (bf16[128,512]{1,0:T(8,128)(2,1)S(1)}, bf16[128,512]{1,0:T(8,128)(2,1)S(1)}, u32[]{:S(2)}, u32[]{:S(2)}) collective-permute-start(bf16[128,512]{1,0:T(8,128)(2,1)S(1)} %pad_maximum_fusion.5), channel_id=1, source_target_pairs={{0,8},{1,33},{2,10},{3,35},{4,12},{5,37},{6,14},{7,39},{8,16},{9,4... | collective-permute-start | bytes 393224 | tf_op jit(solution)/shard_map/ppermute | solution.py:360
  68.0 6.8 %collective-permute-start.30 = (bf16[128,512]{1,0:T(8,128)(2,1)S(1)}, bf16[128,512]{1,0:T(8,128)(2,1)S(1)}, u32[]{:S(2)}, u32[]{:S(2)}) collective-permute-start(bf16[128,512]{1,0:T(8,128)(2,1)S(1)} %get-tuple-element.178.refs_1_.refs_0_), channel_id=1, source_target_pairs={{0,32},{1,9},{2,34},{3,11},{4,36},{5,13},{6,38},{7,15},{8,40},{9,1... | collective-permute-start | bytes 393224 | tf_op jit(solution)/shard_map/ppermute | solution.py:372
  69.7 7.1 %collective-permute-start.27 = (bf16[128,512]{1,0:T(8,128)(2,1)S(1)}, bf16[128,512]{1,0:T(8,128)(2,1)S(1)}, u32[]{:S(2)}, u32[]{:S(2)}) collective-permute-start(bf16[128,512]{1,0:T(8,128)(2,1)S(1)} %get-tuple-element.170), channel_id=1, source_target_pairs={{0,6},{1,7},{2,0},{3,1},{4,2},{5,3},{6,4},{7,5},{8,14},{9,15},{10,... | collective-permute-start | bytes 393224 | tf_op jit(solution)/shard_map/ppermute | solution.py:360
  70.2 6.7 %collective-permute-start.28 = (bf16[128,512]{1,0:T(8,128)(2,1)S(1)}, bf16[128,512]{1,0:T(8,128)(2,1)S(1)}, u32[]{:S(2)}, u32[]{:S(2)}) collective-permute-start(bf16[128,512]{1,0:T(8,128)(2,1)S(1)} %get-tuple-element.171), channel_id=1, source_target_pairs={{0,4},{1,5},{2,6},{3,7},{4,0},{5,1},{6,2},{7,3},{8,12},{9,13},{10,... | collective-permute-start | bytes 393224 | tf_op jit(solution)/shard_map/ppermute | solution.py:360
  72.3 7.2 %collective-permute-start.29 = (bf16[128,512]{1,0:T(8,128)(2,1)S(1)}, bf16[128,512]{1,0:T(8,128)(2,1)S(1)}, u32[]{:S(2)}, u32[]{:S(2)}) collective-permute-start(bf16[128,512]{1,0:T(8,128)(2,1)S(1)} %get-tuple-element.172), channel_id=1, source_target_pairs={{0,2},{1,3},{2,4},{3,5},{4,6},{5,7},{6,0},{7,1},{8,10},{9,11},{10,... | collective-permute-start | bytes 393224 | tf_op jit(solution)/shard_map/ppermute | solution.py:360
  73.1 6.5 %collective-permute-start.32 = (bf16[128,512]{1,0:T(8,128)(2,1)S(1)}, bf16[128,512]{1,0:T(8,128)(2,1)S(1)}, u32[]{:S(2)}, u32[]{:S(2)}) collective-permute-start(bf16[128,512]{1,0:T(8,128)(2,1)S(1)} %get-tuple-element.178.refs_1_.refs_0_), channel_id=1, source_target_pairs={{0,96},{1,25},{2,98},{3,27},{4,100},{5,29},{6,102},{7,31},{8,104},... | collective-permute-start | bytes 393224 | tf_op jit(solution)/shard_map/ppermute | solution.py:373
  74.8 5.3 %collective-permute-start.31 = (bf16[128,512]{1,0:T(8,128)(2,1)S(1)}, bf16[128,512]{1,0:T(8,128)(2,1)S(1)}, u32[]{:S(2)}, u32[]{:S(2)}) collective-permute-start(bf16[128,512]{1,0:T(8,128)(2,1)S(1)} %collective-permute-done.30.refs_1_), channel_id=1, source_target_pairs={{0,32},{1,9},{2,34},{3,11},{4,36},{5,13},{6,38},{7,15},{8,40},{9,1... | collective-permute-start | bytes 393224 | tf_op jit(solution)/shard_map/ppermute | solution.py:374
  85.8 14.1 %all-to-all-start = ((f32[128,1,128]{2,1,0:T(1,128)}), f32[128,1,128]{2,1,0:T(1,128)S(1)}, u32[]{:S(2)}, u32[]{:S(2)}) async-start(f32[128,1,128]{2,1,0:T(1,128)} %get-tuple-element.184), calls=%async_computation | async-start | bytes 131072 | tf_op jit(solution)/shard_map/all_to_all | solution.py:508
  (7 other events, 61.8 us)

commit v4 on v3

--- a/solution.py
+++ b/solution.py
@@ -45,10 +45,12 @@
     return jnp.broadcast_to(row, (128, row.shape[1])).T
 
 
-def call(kernel, outs, arrays, flops, scratch=(), far=()):
+def call(kernel, outs, arrays, flops, scratch=(), far=(), final=()):
     out_shapes = [jax.ShapeDtypeStruct(shape, dtype) for shape, dtype in outs]
     moved = sum(a.size * a.dtype.itemsize for a in list(arrays) + out_shapes)
-    out_shapes = [pltpu.VMEM(shape, dtype) for shape, dtype in outs]
+    out_shapes = [
+        (pltpu.HBM if i in final else pltpu.VMEM)(shape, dtype) for i, (shape, dtype) in enumerate(outs)
+    ]
     arrays = [
         pltpu.with_memory_space_constraint(a, pltpu.HBM) if i in far else a for i, a in enumerate(arrays)
     ]
@@ -486,6 +488,7 @@
         [states, ((8, 128), F32)],
         [x_start, x_root, x_top, x_child, x_child_next],
         0,
+        final=(0,),
     )
     (base,) = call(
         part_of(own_image, True),
@@ -494,7 +497,9 @@
         2 * unit,
     )
     back_leaf = ring_gather(extra_root, outer_ring)
-    back_node, (back_leaf, base) = swap_node(out_node, -1, (back_leaf, base))
+    back_node, (back_leaf, base, primal_move) = swap_node(
+        out_node, -1, (back_leaf, base, primal_move)
+    )
     (later,) = call(
         part_of(dual_leaf, True), [kids_field], back_leaf + [lback, linking, base, rates], unit
     )

time: 103 us -> 103 us (level)
    unnamed x10 -> x9, local copies, waits for them, and re-layouts: 2.25 us -> 1.43 us
  transfers between devices with their start and end apart: 35 -> 35, of which waited for: 14 -> 15; matrix products, arithmetic and copies ran while one was open for 3% -> 2% of each run, Pallas kernels for 14% -> 15%
where the time goes in v4:
time: 103 us
  starting transfers between devices  49.1 us (48%)
  waiting for transfers between devices  25.1 us (24%)
  Pallas kernels  21.9 us (21%)
  between operations  4.25 us (4%)
  local copies, waits for them, and re-layouts  2.28 us (2%)
    ppermute x24, starting transfers between devices, shifted(): got[k] = lax.ppermute(blocks[k], *ring(sign * k % 4))  30.3 us
    pallas_call x15, Pallas kernels, call(): pl.pallas_call(kernel, out_shape=out_shapes, in_specs=[pl.BlockSpec(memor...  21.9 us
    ppermute x24, waiting for transfers between devices, shifted(): got[k] = lax.ppermute(blocks[k], *ring(sign * k % 4))  14.6 us
    ppermute x4, starting transfers between devices, sibling(): return lax.ppermute(array, *pairs_of(lambda y, z, x, c: (y, z, x, 1 - c)))  9.6 us
    all_to_all x1, waiting for transfers between devices, shards(): lax.all_to_all(load, ('leaf', 'node'), split_axis=0, concat_axis=0, tiled...  8.04 us
    all_to_all x1, starting transfers between devices, shards(): lax.all_to_all(load, ('leaf', 'node'), split_axis=0, concat_axis=0, tiled...  4.82 us
    ppermute x2, starting transfers between devices, ring_gather(): three = lax.ppermute(rows, *ring(3))  4.19 us
  transfers between devices with their start and end apart: 35, of which 15 were waited for; matrix products, arithmetic and copies ran while one was open for 2% of the time, Pallas kernels for 15%

profile of v4, /device:TPU:1, one launch (start us, length us, event | category | flops | bytes accessed | tf_op | source)
XLA Modules:
  0.0 103.1 jit_solution(7394526765396863069)
XLA Ops:
  0.6 4.4 %shard_map.112 = (bf16[128,640]{1,0:T(8,128)(2,1)S(1)}, bf16[128,640]{1,0:T(8,128)(2,1)S(1)}, bf16[128,640]{1,0:T(8,128)(2,1)S(1)}, bf16[128,640]{1,0:T(8,128)(2...) custom-call(s32[288]{0:T(512)} %parent_far.1, ...), custom_call_target="tpu_custom_call" | custom-call | flops 1073741824 | bytes 2150944 | tf_op jit(solution)/shard_map/pallas_call | solution.py:57
  5.1 2.5 %collective-permute-start.3 = (bf16[128,512]{1,0:T(8,128)(2,1)S(1)}, bf16[128,512]{1,0:T(8,128)(2,1)S(1)}, u32[]{:S(2)}, u32[]{:S(2)}) collective-permute-start(bf16[128,512]{1,0:T(8,128)(2,1)S(1)} %get-tuple-element.100), channel_id=1, source_target_pairs={{0,32},{1,9},{2,34},{3,11},{4,36},{5,13},{6,38},{7,15},{8,40},{9,1... | collective-permute-start | bytes 393224 | tf_op jit(solution)/shard_map/ppermute | solution.py:362
  7.6 3.3 %collective-permute-start.4 = (bf16[128,512]{1,0:T(8,128)(2,1)S(1)}, bf16[128,512]{1,0:T(8,128)(2,1)S(1)}, u32[]{:S(2)}, u32[]{:S(2)}) collective-permute-start(bf16[128,512]{1,0:T(8,128)(2,1)S(1)} %get-tuple-element.101), channel_id=1, source_target_pairs={{0,64},{1,17},{2,66},{3,19},{4,68},{5,21},{6,70},{7,23},{8,72},{9,... | collective-permute-start | bytes 393224 | tf_op jit(solution)/shard_map/ppermute | solution.py:362
  12.9 2.4 %collective-permute-start.1 = (bf16[128,640]{1,0:T(8,128)(2,1)S(1)}, bf16[128,640]{1,0:T(8,128)(2,1)S(1)}, u32[]{:S(2)}, u32[]{:S(2)}) collective-permute-start(bf16[128,640]{1,0:T(8,128)(2,1)S(1)} %get-tuple-element.97), channel_id=1, source_target_pairs={{0,4},{1,5},{2,6},{3,7},{4,0},{5,1},{6,2},{7,3},{8,12},{9,13},{10,... | collective-permute-start | bytes 491528 | tf_op jit(solution)/shard_map/ppermute | solution.py:362
  17.1 2.8 %collective-permute-start.8 = (bf16[160,512]{1,0:T(8,128)(2,1)S(1)}, bf16[160,512]{1,0:T(8,128)(2,1)S(1)}, u32[]{:S(2)}, u32[]{:S(2)}) collective-permute-start(bf16[160,512]{1,0:T(8,128)(2,1)S(1)} %pad_maximum_fusion.4), channel_id=1, source_target_pairs={{0,24},{1,97},{2,26},{3,99},{4,28},{5,101},{6,30},{7,103},{8,0},{9... | collective-permute-start | bytes 491528 | tf_op jit(solution)/shard_map/ppermute | solution.py:362
  21.0 1.3 %shard_map.114.own = f32[256,512]{1,0:T(8,128)S(1)} custom-call(bf16[288,2048]{1,0:T(8,128)(2,1)S(1)} %get-tuple-element.103.ylow, f32[256,128]{1,0:T(8,128)S(1)} %get-tuple-element.110.scol.refs_2_, bf16[3,2048,512]{2,1,0:T(8,128)(2,1)S(1)} %copy-done), custom_call_target="tpu_custom_call" | custom-call | flops 1073741824 | bytes 1015808 | tf_op jit(solution)/shard_map/pallas_call | solution.py:57
  22.4 1.5 %collective-permute-done.8.g3 = bf16[160,512]{1,0:T(8,128)(2,1)S(1)} collective-permute-done((bf16[160,512]{1,0:T(8,128)(2,1)S(1)}, bf16[160,512]{1,0:T(8,128)(2,1)S(1)}, u32[]{:S(2)}, u32[]{:S(2)}) %collective-permute-start.8) | collective-permute-done | bytes 163872 | tf_op jit(solution)/shard_map/ppermute | solution.py:362
  24.0 1.8 %collective-permute-done.7.g2 = bf16[160,512]{1,0:T(8,128)(2,1)S(1)} collective-permute-done((bf16[160,512]{1,0:T(8,128)(2,1)S(1)}, bf16[160,512]{1,0:T(8,128)(2,1)S(1)}, u32[]{:S(2)}, u32[]{:S(2)}) %collective-permute-start.7) | collective-permute-done | bytes 163872 | tf_op jit(solution)/shard_map/ppermute | solution.py:362
  25.7 1.9 %collective-permute-done.6.g1 = bf16[160,512]{1,0:T(8,128)(2,1)S(1)} collective-permute-done((bf16[160,512]{1,0:T(8,128)(2,1)S(1)}, bf16[160,512]{1,0:T(8,128)(2,1)S(1)}, u32[]{:S(2)}, u32[]{:S(2)}) %collective-permute-start.6) | collective-permute-done | bytes 163872 | tf_op jit(solution)/shard_map/ppermute | solution.py:362
  27.7 3.5 %collective-permute-start.9 = (bf16[256,640]{1,0:T(8,128)(2,1)S(1)}, bf16[256,640]{1,0:T(8,128)(2,1)S(1)}, u32[]{:S(2)}, u32[]{:S(2)}) collective-permute-start(bf16[256,640]{1,0:T(8,128)(2,1)S(1)} %pad_maximum_fusion), channel_id=1, source_target_pairs={{0,1},{1,0},{2,3},{3,2},{4,5},{5,4},{6,7},{7,6},{8,9},{9,8},{10,11... | collective-permute-start | bytes 983048 | tf_op jit(solution)/shard_map/ppermute | solution.py:356
  33.3 2.1 %collective-permute-start.11 = (bf16[128,512]{1,0:T(8,128)(2,1)S(1)}, bf16[128,512]{1,0:T(8,128)(2,1)S(1)}, u32[]{:S(2)}, u32[]{:S(2)}) collective-permute-start(bf16[128,512]{1,0:T(8,128)(2,1)S(1)} %get-tuple-element.123), channel_id=1, source_target_pairs={{0,4},{1,5},{2,6},{3,7},{4,0},{5,1},{6,2},{7,3},{8,12},{9,13},{10,... | collective-permute-start | bytes 393224 | tf_op jit(solution)/shard_map/ppermute | solution.py:362
  35.4 2.5 %collective-permute-start.15 = (bf16[128,512]{1,0:T(8,128)(2,1)S(1)}, bf16[128,512]{1,0:T(8,128)(2,1)S(1)}, u32[]{:S(2)}, u32[]{:S(2)}) collective-permute-start(bf16[128,512]{1,0:T(8,128)(2,1)S(1)} %get-tuple-element.133.refs_1_.refs_0_), channel_id=1, source_target_pairs={{0,96},{1,25},{2,98},{3,27},{4,100},{5,29},{6,102},{7,31},{8,104},... | collective-permute-start | bytes 393224 | tf_op jit(solution)/shard_map/ppermute | solution.py:375
  37.9 2.6 %shard_map.117 = (f32[288,2048]{1,0:T(8,128)S(1)}, f32[32,512]{1,0:T(8,128)S(1)}) custom-call(bf16[256,512]{1,0:T(8,128)(2,1)S(1)} %get-tuple-element.126.refs_0_, bf16[128,512]{1,0:T(8,128)(2,1)S(1)} %get-tuple-element.133.refs_1_.refs_0_, f32[256,128]{1,0:T(8,128)S(1)} %get-tuple-element.110.scol.refs_2_, bf16[3,2048,512]{2,1,0:T(8,128)(2,1)S(1)} %copy-done, ...), custom_call_target="tpu_custom_call" | custom-call | flops 1073741824 | bytes 1753216 | tf_op jit(solution)/shard_map/pallas_call | solution.py:57
  40.5 2.0 %collective-permute-done.12.g3 = bf16[128,512]{1,0:T(8,128)(2,1)S(1)} collective-permute-done((bf16[128,512]{1,0:T(8,128)(2,1)S(1)}, bf16[128,512]{1,0:T(8,128)(2,1)S(1)}, u32[]{:S(2)}, u32[]{:S(2)}) %collective-permute-start.12) | collective-permute-done | bytes 131104 | tf_op jit(solution)/shard_map/ppermute | solution.py:362
  43.2 2.0 %collective-permute-start.16 = (bf16[256,512]{1,0:T(8,128)(2,1)S(1)}, bf16[256,512]{1,0:T(8,128)(2,1)S(1)}, u32[]{:S(2)}, u32[]{:S(2)}) collective-permute-start(bf16[256,512]{1,0:T(8,128)(2,1)S(1)} %pad_maximum_fusion.1), channel_id=1, source_target_pairs={{0,1},{1,0},{2,3},{3,2},{4,5},{5,4},{6,7},{7,6},{8,9},{9,8},{10,11... | collective-permute-start | bytes 786440 | tf_op jit(solution)/shard_map/ppermute | solution.py:356
  45.2 2.1 %shard_map.118 = (f32[256,2048]{1,0:T(8,128)S(1)}, bf16[128,512]{1,0:T(8,128)(2,1)S(1)}, bf16[128,512]{1,0:T(8,128)(2,1)S(1)}, bf16[128,512]{1,0:T(8,128)(2,1)S(1)}, bf16[128,512]{1,0:T(8,128)(2,1)S(1)}) custom-call(bf16[128,512]{1,0:T(8,128)(2,1)S(1)} %get-tuple-element.133.refs_1_.refs_0_, bf16[128,512]{1,0:T(8,128)(2,1)S(1)} %collective-permute-done.13.refs_1_, ...), custom_call_target="tpu_custom_call" | custom-call | flops 1073741824 | bytes 1229056 | tf_op jit(solution)/shard_map/pallas_call | solution.py:57
  47.4 1.8 %collective-permute-start.21 = (bf16[128,512]{1,0:T(8,128)(2,1)S(1)}, bf16[128,512]{1,0:T(8,128)(2,1)S(1)}, u32[]{:S(2)}, u32[]{:S(2)}) collective-permute-start(bf16[128,512]{1,0:T(8,128)(2,1)S(1)} %get-tuple-element.147), channel_id=1, source_target_pairs={{0,64},{1,17},{2,66},{3,19},{4,68},{5,21},{6,70},{7,23},{8,72},{9,... | collective-permute-start | bytes 393224 | tf_op jit(solution)/shard_map/ppermute | solution.py:362
  50.1 2.1 %shard_map.119 = (f32[288,2048]{1,0:T(8,128)S(1)}, bf16[288,2048]{1,0:T(8,128)(2,1)S(1)}, bf16[128,512]{1,0:T(8,128)(2,1)S(1)}, bf16[128,512]{1,0:T(8,128)(2,1)S...) custom-call(bf16[128,512]{1,0:T(8,128)(2,1)S(1)} %get-tuple-element.121.g0, ...), custom_call_target="tpu_custom_call" | custom-call | flops 1073741824 | bytes 1704192 | tf_op jit(solution)/shard_map/pallas_call | solution.py:57
  52.9 3.4 %collective-permute-start.18 = (bf16[128,512]{1,0:T(8,128)(2,1)S(1)}, bf16[128,512]{1,0:T(8,128)(2,1)S(1)}, u32[]{:S(2)}, u32[]{:S(2)}) collective-permute-start(bf16[128,512]{1,0:T(8,128)(2,1)S(1)} %get-tuple-element.143), channel_id=1, source_target_pairs={{0,4},{1,5},{2,6},{3,7},{4,0},{5,1},{6,2},{7,3},{8,12},{9,13},{10,... | collective-permute-start | bytes 393224 | tf_op jit(solution)/shard_map/ppermute | solution.py:362
  59.3 1.3 %shard_map.120.own = f32[256,512]{1,0:T(8,128)S(1)} custom-call(bf16[288,2048]{1,0:T(8,128)(2,1)S(1)} %get-tuple-element.155.ylow, f32[256,128]{1,0:T(8,128)S(1)} %get-tuple-element.110.scol.refs_2_, bf16[3,2048,512]{2,1,0:T(8,128)(2,1)S(1)} %copy-done), custom_call_target="tpu_custom_call" | custom-call | flops 1073741824 | bytes 1015808 | tf_op jit(solution)/shard_map/pallas_call | solution.py:57
  60.6 1.6 %collective-permute-done.18.g2 = bf16[128,512]{1,0:T(8,128)(2,1)S(1)} collective-permute-done((bf16[128,512]{1,0:T(8,128)(2,1)S(1)}, bf16[128,512]{1,0:T(8,128)(2,1)S(1)}, u32[]{:S(2)}, u32[]{:S(2)}) %collective-permute-start.18) | collective-permute-done | bytes 131104 | tf_op jit(solution)/shard_map/ppermute | solution.py:362
  63.2 2.9 %collective-permute-done.23.g1 = bf16[128,512]{1,0:T(8,128)(2,1)S(1)} collective-permute-done((bf16[128,512]{1,0:T(8,128)(2,1)S(1)}, bf16[128,512]{1,0:T(8,128)(2,1)S(1)}, u32[]{:S(2)}, u32[]{:S(2)}) %collective-permute-start.23) | collective-permute-done | bytes 131104 | tf_op jit(solution)/shard_map/ppermute | solution.py:362
  66.1 1.8 %collective-permute-start.26 = (bf16[256,512]{1,0:T(8,128)(2,1)S(1)}, bf16[256,512]{1,0:T(8,128)(2,1)S(1)}, u32[]{:S(2)}, u32[]{:S(2)}) collective-permute-start(bf16[256,512]{1,0:T(8,128)(2,1)S(1)} %pad_maximum_fusion.2), channel_id=1, source_target_pairs={{0,1},{1,0},{2,3},{3,2},{4,5},{5,4},{6,7},{7,6},{8,9},{9,8},{10,11... | collective-permute-start | bytes 786440 | tf_op jit(solution)/shard_map/ppermute | solution.py:356
  70.2 2.1 %collective-permute-start.28 = (bf16[128,512]{1,0:T(8,128)(2,1)S(1)}, bf16[128,512]{1,0:T(8,128)(2,1)S(1)}, u32[]{:S(2)}, u32[]{:S(2)}) collective-permute-start(bf16[128,512]{1,0:T(8,128)(2,1)S(1)} %get-tuple-element.172), channel_id=1, source_target_pairs={{0,4},{1,5},{2,6},{3,7},{4,0},{5,1},{6,2},{7,3},{8,12},{9,13},{10,... | collective-permute-start | bytes 393224 | tf_op jit(solution)/shard_map/ppermute | solution.py:362
  73.1 1.7 %collective-permute-start.32 = (bf16[128,512]{1,0:T(8,128)(2,1)S(1)}, bf16[128,512]{1,0:T(8,128)(2,1)S(1)}, u32[]{:S(2)}, u32[]{:S(2)}) collective-permute-start(bf16[128,512]{1,0:T(8,128)(2,1)S(1)} %get-tuple-element.180.refs_1_.refs_0_), channel_id=1, source_target_pairs={{0,96},{1,25},{2,98},{3,27},{4,100},{5,29},{6,102},{7,31},{8,104},... | collective-permute-start | bytes 393224 | tf_op jit(solution)/shard_map/ppermute | solution.py:375
  74.8 2.0 %shard_map.124.refs_6_.base = f32[288,2048]{1,0:T(8,128)S(1)} custom-call(bf16[256,512]{1,0:T(8,128)(2,1)S(1)} %get-tuple-element.175.refs_0_, bf16[128,512]{1,0:T(8,128)(2,1)S(1)} %get-tuple-element.180.refs_1_.refs_0_, f32[256,128]{1,0:T(8,128)S(1)} %get-tuple-element.110.scol.refs_2_, bf16[3,2048,512]{2,1,0:T(8,128)(2,1)S(1)} %copy-done, ...), custom_call_target="tpu_custom_call" | custom-call | flops 1073741824 | bytes 1745024 | tf_op jit(solution)/shard_map/pallas_call | solution.py:57
  77.9 1.6 %collective-permute-done.29.g3 = bf16[128,512]{1,0:T(8,128)(2,1)S(1)} collective-permute-done((bf16[128,512]{1,0:T(8,128)(2,1)S(1)}, bf16[128,512]{1,0:T(8,128)(2,1)S(1)}, u32[]{:S(2)}, u32[]{:S(2)}) %collective-permute-start.29) | collective-permute-done | bytes 131104 | tf_op jit(solution)/shard_map/ppermute | solution.py:362
  80.1 2.3 %collective-permute-start.33 = (bf16[256,512]{1,0:T(8,128)(2,1)S(1)}, bf16[256,512]{1,0:T(8,128)(2,1)S(1)}, u32[]{:S(2)}, u32[]{:S(2)}) collective-permute-start(bf16[256,512]{1,0:T(8,128)(2,1)S(1)} %pad_maximum_fusion.3), channel_id=1, source_target_pairs={{0,1},{1,0},{2,3},{3,2},{4,5},{5,4},{6,7},{7,6},{8,9},{9,8},{10,11... | collective-permute-start | bytes 786440 | tf_op jit(solution)/shard_map/ppermute | solution.py:356
  83.5 2.0 %shard_map.126 = (f32[288,2048]{1,0:T(8,128)S(1)}, f32[128,1,128]{2,1,0:T(1,128)}) custom-call(bf16[128,512]{1,0:T(8,128)(2,1)S(1)} %get-tuple-element.170.g0, bf16[128,512]{1,0:T(8,128)(2,1)S(1)} %collective-permute-done.27.g1, bf16[128,512]{1,0:T(8,128)(2,1)S(1)} %collective-permute-done.28.g2, bf16[128,512]{1,0:T(8,128)(2,1)S(1)} %collective-permute-done.29.g3, ...), custom_call_target="tpu_custom_call" | custom-call | flops 536870912 | bytes 2089600 | tf_op jit(solution)/shard_map/pallas_call | solution.py:57
  85.5 4.8 %all-to-all-start = ((f32[128,1,128]{2,1,0:T(1,128)}), f32[128,1,128]{2,1,0:T(1,128)S(1)}, u32[]{:S(2)}, u32[]{:S(2)}) async-start(f32[128,1,128]{2,1,0:T(1,128)} %get-tuple-element.186), calls=%async_computation | async-start | bytes 131072 | tf_op jit(solution)/shard_map/all_to_all | solution.py:513
  90.3 1.4 %copy.12 = f32[288,2048]{1,0:T(8,128)} copy(f32[288,2048]{1,0:T(8,128)S(1)} %get-tuple-element.194) | data formatting | bytes 4718592
  91.7 8.0 %all-to-all-done = f32[128,1,128]{2,1,0:T(1,128)S(1)} async-done(((f32[128,1,128]{2,1,0:T(1,128)}), f32[128,1,128]{2,1,0:T(1,128)S(1)}, u32[]{:S(2)}, u32[]{:S(2)}) %all-to-all-start) | async-done | bytes 65568 | tf_op jit(solution)/shard_map/all_to_all | solution.py:513
  (94 shorter events, 19.2 us)
Async XLA Ops:
  5.1 10.7 %collective-permute-start.3 = (bf16[128,512]{1,0:T(8,128)(2,1)S(1)}, bf16[128,512]{1,0:T(8,128)(2,1)S(1)}, u32[]{:S(2)}, u32[]{:S(2)}) collective-permute-start(bf16[128,512]{1,0:T(8,128)(2,1)S(1)} %get-tuple-element.100), channel_id=1, source_target_pairs={{0,32},{1,9},{2,34},{3,11},{4,36},{5,13},{6,38},{7,15},{8,40},{9,1... | collective-permute-start | bytes 393224 | tf_op jit(solution)/shard_map/ppermute | solution.py:362
  7.6 9.4 %collective-permute-start.4 = (bf16[128,512]{1,0:T(8,128)(2,1)S(1)}, bf16[128,512]{1,0:T(8,128)(2,1)S(1)}, u32[]{:S(2)}, u32[]{:S(2)}) collective-permute-start(bf16[128,512]{1,0:T(8,128)(2,1)S(1)} %get-tuple-element.101), channel_id=1, source_target_pairs={{0,64},{1,17},{2,66},{3,19},{4,68},{5,21},{6,70},{7,23},{8,72},{9,... | collective-permute-start | bytes 393224 | tf_op jit(solution)/shard_map/ppermute | solution.py:362
  10.9 6.1 %collective-permute-start.5 = (bf16[128,512]{1,0:T(8,128)(2,1)S(1)}, bf16[128,512]{1,0:T(8,128)(2,1)S(1)}, u32[]{:S(2)}, u32[]{:S(2)}) collective-permute-start(bf16[128,512]{1,0:T(8,128)(2,1)S(1)} %get-tuple-element.102), channel_id=1, source_target_pairs={{0,96},{1,25},{2,98},{3,27},{4,100},{5,29},{6,102},{7,31},{8,104},... | collective-permute-start | bytes 393224 | tf_op jit(solution)/shard_map/ppermute | solution.py:362
  11.6 8.6 %collective-permute-start = (bf16[128,640]{1,0:T(8,128)(2,1)S(1)}, bf16[128,640]{1,0:T(8,128)(2,1)S(1)}, u32[]{:S(2)}, u32[]{:S(2)}) collective-permute-start(bf16[128,640]{1,0:T(8,128)(2,1)S(1)} %get-tuple-element.96), channel_id=1, source_target_pairs={{0,2},{1,3},{2,4},{3,5},{4,6},{5,7},{6,0},{7,1},{8,10},{9,11},{10,... | collective-permute-start | bytes 491528 | tf_op jit(solution)/shard_map/ppermute | solution.py:362
  12.9 9.5 %collective-permute-start.1 = (bf16[128,640]{1,0:T(8,128)(2,1)S(1)}, bf16[128,640]{1,0:T(8,128)(2,1)S(1)}, u32[]{:S(2)}, u32[]{:S(2)}) collective-permute-start(bf16[128,640]{1,0:T(8,128)(2,1)S(1)} %get-tuple-element.97), channel_id=1, source_target_pairs={{0,4},{1,5},{2,6},{3,7},{4,0},{5,1},{6,2},{7,3},{8,12},{9,13},{10,... | collective-permute-start | bytes 491528 | tf_op jit(solution)/shard_map/ppermute | solution.py:362
  15.8 6.6 %collective-permute-start.2 = (bf16[128,640]{1,0:T(8,128)(2,1)S(1)}, bf16[128,640]{1,0:T(8,128)(2,1)S(1)}, u32[]{:S(2)}, u32[]{:S(2)}) collective-permute-start(bf16[128,640]{1,0:T(8,128)(2,1)S(1)} %get-tuple-element.98), channel_id=1, source_target_pairs={{0,6},{1,7},{2,0},{3,1},{4,2},{5,3},{6,4},{7,5},{8,14},{9,15},{10,... | collective-permute-start | bytes 491528 | tf_op jit(solution)/shard_map/ppermute | solution.py:362
  17.1 6.8 %collective-permute-start.8 = (bf16[160,512]{1,0:T(8,128)(2,1)S(1)}, bf16[160,512]{1,0:T(8,128)(2,1)S(1)}, u32[]{:S(2)}, u32[]{:S(2)}) collective-permute-start(bf16[160,512]{1,0:T(8,128)(2,1)S(1)} %pad_maximum_fusion.4), channel_id=1, source_target_pairs={{0,24},{1,97},{2,26},{3,99},{4,28},{5,101},{6,30},{7,103},{8,0},{9... | collective-permute-start | bytes 491528 | tf_op jit(solution)/shard_map/ppermute | solution.py:362
  20.0 5.8 %collective-permute-start.7 = (bf16[160,512]{1,0:T(8,128)(2,1)S(1)}, bf16[160,512]{1,0:T(8,128)(2,1)S(1)}, u32[]{:S(2)}, u32[]{:S(2)}) collective-permute-start(bf16[160,512]{1,0:T(8,128)(2,1)S(1)} %pad_maximum_fusion.4), channel_id=1, source_target_pairs={{0,16},{1,65},{2,18},{3,67},{4,20},{5,69},{6,22},{7,71},{8,24},{9,... | collective-permute-start | bytes 491528 | tf_op jit(solution)/shard_map/ppermute | solution.py:362
  20.3 7.4 %collective-permute-start.6 = (bf16[160,512]{1,0:T(8,128)(2,1)S(1)}, bf16[160,512]{1,0:T(8,128)(2,1)S(1)}, u32[]{:S(2)}, u32[]{:S(2)}) collective-permute-start(bf16[160,512]{1,0:T(8,128)(2,1)S(1)} %pad_maximum_fusion.4), channel_id=1, source_target_pairs={{0,8},{1,33},{2,10},{3,35},{4,12},{5,37},{6,14},{7,39},{8,16},{9,4... | collective-permute-start | bytes 491528 | tf_op jit(solution)/shard_map/ppermute | solution.py:362
  27.7 4.8 %collective-permute-start.9 = (bf16[256,640]{1,0:T(8,128)(2,1)S(1)}, bf16[256,640]{1,0:T(8,128)(2,1)S(1)}, u32[]{:S(2)}, u32[]{:S(2)}) collective-permute-start(bf16[256,640]{1,0:T(8,128)(2,1)S(1)} %pad_maximum_fusion), channel_id=1, source_target_pairs={{0,1},{1,0},{2,3},{3,2},{4,5},{5,4},{6,7},{7,6},{8,9},{9,8},{10,11... | collective-permute-start | bytes 983048 | tf_op jit(solution)/shard_map/ppermute | solution.py:356
  32.2 5.7 %collective-permute-start.13 = (bf16[128,512]{1,0:T(8,128)(2,1)S(1)}, bf16[128,512]{1,0:T(8,128)(2,1)S(1)}, u32[]{:S(2)}, u32[]{:S(2)}) collective-permute-start(bf16[128,512]{1,0:T(8,128)(2,1)S(1)} %get-tuple-element.133.refs_1_.refs_0_), channel_id=1, source_target_pairs={{0,32},{1,9},{2,34},{3,11},{4,36},{5,13},{6,38},{7,15},{8,40},{9,1... | collective-permute-start | bytes 393224 | tf_op jit(solution)/shard_map/ppermute | solution.py:374
  33.2 7.3 %collective-permute-start.10 = (bf16[128,512]{1,0:T(8,128)(2,1)S(1)}, bf16[128,512]{1,0:T(8,128)(2,1)S(1)}, u32[]{:S(2)}, u32[]{:S(2)}) collective-permute-start(bf16[128,512]{1,0:T(8,128)(2,1)S(1)} %get-tuple-element.122), channel_id=1, source_target_pairs={{0,6},{1,7},{2,0},{3,1},{4,2},{5,3},{6,4},{7,5},{8,14},{9,15},{10,... | collective-permute-start | bytes 393224 | tf_op jit(solution)/shard_map/ppermute | solution.py:362
  33.3 7.2 %collective-permute-start.11 = (bf16[128,512]{1,0:T(8,128)(2,1)S(1)}, bf16[128,512]{1,0:T(8,128)(2,1)S(1)}, u32[]{:S(2)}, u32[]{:S(2)}) collective-permute-start(bf16[128,512]{1,0:T(8,128)(2,1)S(1)} %get-tuple-element.123), channel_id=1, source_target_pairs={{0,4},{1,5},{2,6},{3,7},{4,0},{5,1},{6,2},{7,3},{8,12},{9,13},{10,... | collective-permute-start | bytes 393224 | tf_op jit(solution)/shard_map/ppermute | solution.py:362
  35.4 7.1 %collective-permute-start.12 = (bf16[128,512]{1,0:T(8,128)(2,1)S(1)}, bf16[128,512]{1,0:T(8,128)(2,1)S(1)}, u32[]{:S(2)}, u32[]{:S(2)}) collective-permute-start(bf16[128,512]{1,0:T(8,128)(2,1)S(1)} %get-tuple-element.124), channel_id=1, source_target_pairs={{0,2},{1,3},{2,4},{3,5},{4,6},{5,7},{6,0},{7,1},{8,10},{9,11},{10,... | collective-permute-start | bytes 393224 | tf_op jit(solution)/shard_map/ppermute | solution.py:362
  35.4 7.1 %collective-permute-start.15 = (bf16[128,512]{1,0:T(8,128)(2,1)S(1)}, bf16[128,512]{1,0:T(8,128)(2,1)S(1)}, u32[]{:S(2)}, u32[]{:S(2)}) collective-permute-start(bf16[128,512]{1,0:T(8,128)(2,1)S(1)} %get-tuple-element.133.refs_1_.refs_0_), channel_id=1, source_target_pairs={{0,96},{1,25},{2,98},{3,27},{4,100},{5,29},{6,102},{7,31},{8,104},... | collective-permute-start | bytes 393224 | tf_op jit(solution)/shard_map/ppermute | solution.py:375
  37.9 5.3 %collective-permute-start.14 = (bf16[128,512]{1,0:T(8,128)(2,1)S(1)}, bf16[128,512]{1,0:T(8,128)(2,1)S(1)}, u32[]{:S(2)}, u32[]{:S(2)}) collective-permute-start(bf16[128,512]{1,0:T(8,128)(2,1)S(1)} %collective-permute-done.13.refs_1_), channel_id=1, source_target_pairs={{0,32},{1,9},{2,34},{3,11},{4,36},{5,13},{6,38},{7,15},{8,40},{9,1... | collective-permute-start | bytes 393224 | tf_op jit(solution)/shard_map/ppermute | solution.py:376
  43.2 6.9 %collective-permute-start.16 = (bf16[256,512]{1,0:T(8,128)(2,1)S(1)}, bf16[256,512]{1,0:T(8,128)(2,1)S(1)}, u32[]{:S(2)}, u32[]{:S(2)}) collective-permute-start(bf16[256,512]{1,0:T(8,128)(2,1)S(1)} %pad_maximum_fusion.1), channel_id=1, source_target_pairs={{0,1},{1,0},{2,3},{3,2},{4,5},{5,4},{6,7},{7,6},{8,9},{9,8},{10,11... | collective-permute-start | bytes 786440 | tf_op jit(solution)/shard_map/ppermute | solution.py:356
  47.3 9.0 %collective-permute-start.20 = (bf16[128,512]{1,0:T(8,128)(2,1)S(1)}, bf16[128,512]{1,0:T(8,128)(2,1)S(1)}, u32[]{:S(2)}, u32[]{:S(2)}) collective-permute-start(bf16[128,512]{1,0:T(8,128)(2,1)S(1)} %get-tuple-element.146), channel_id=1, source_target_pairs={{0,32},{1,9},{2,34},{3,11},{4,36},{5,13},{6,38},{7,15},{8,40},{9,1... | collective-permute-start | bytes 393224 | tf_op jit(solution)/shard_map/ppermute | solution.py:362
  47.4 10.1 %collective-permute-start.21 = (bf16[128,512]{1,0:T(8,128)(2,1)S(1)}, bf16[128,512]{1,0:T(8,128)(2,1)S(1)}, u32[]{:S(2)}, u32[]{:S(2)}) collective-permute-start(bf16[128,512]{1,0:T(8,128)(2,1)S(1)} %get-tuple-element.147), channel_id=1, source_target_pairs={{0,64},{1,17},{2,66},{3,19},{4,68},{5,21},{6,70},{7,23},{8,72},{9,... | collective-permute-start | bytes 393224 | tf_op jit(solution)/shard_map/ppermute | solution.py:362
  49.2 8.2 %collective-permute-start.22 = (bf16[128,512]{1,0:T(8,128)(2,1)S(1)}, bf16[128,512]{1,0:T(8,128)(2,1)S(1)}, u32[]{:S(2)}, u32[]{:S(2)}) collective-permute-start(bf16[128,512]{1,0:T(8,128)(2,1)S(1)} %get-tuple-element.148), channel_id=1, source_target_pairs={{0,96},{1,25},{2,98},{3,27},{4,100},{5,29},{6,102},{7,31},{8,104},... | collective-permute-start | bytes 393224 | tf_op jit(solution)/shard_map/ppermute | solution.py:362
  52.1 6.2 %collective-permute-start.17 = (bf16[128,512]{1,0:T(8,128)(2,1)S(1)}, bf16[128,512]{1,0:T(8,128)(2,1)S(1)}, u32[]{:S(2)}, u32[]{:S(2)}) collective-permute-start(bf16[128,512]{1,0:T(8,128)(2,1)S(1)} %get-tuple-element.142), channel_id=1, source_target_pairs={{0,2},{1,3},{2,4},{3,5},{4,6},{5,7},{6,0},{7,1},{8,10},{9,11},{10,... | collective-permute-start | bytes 393224 | tf_op jit(solution)/shard_map/ppermute | solution.py:362
  52.9 9.2 %collective-permute-start.18 = (bf16[128,512]{1,0:T(8,128)(2,1)S(1)}, bf16[128,512]{1,0:T(8,128)(2,1)S(1)}, u32[]{:S(2)}, u32[]{:S(2)}) collective-permute-start(bf16[128,512]{1,0:T(8,128)(2,1)S(1)} %get-tuple-element.143), channel_id=1, source_target_pairs={{0,4},{1,5},{2,6},{3,7},{4,0},{5,1},{6,2},{7,3},{8,12},{9,13},{10,... | collective-permute-start | bytes 393224 | tf_op jit(solution)/shard_map/ppermute | solution.py:362
  56.3 5.8 %collective-permute-start.19 = (bf16[128,512]{1,0:T(8,128)(2,1)S(1)}, bf16[128,512]{1,0:T(8,128)(2,1)S(1)}, u32[]{:S(2)}, u32[]{:S(2)}) collective-permute-start(bf16[128,512]{1,0:T(8,128)(2,1)S(1)} %get-tuple-element.144), channel_id=1, source_target_pairs={{0,6},{1,7},{2,0},{3,1},{4,2},{5,3},{6,4},{7,5},{8,14},{9,15},{10,... | collective-permute-start | bytes 393224 | tf_op jit(solution)/shard_map/ppermute | solution.py:362
  57.7 5.5 %collective-permute-start.24 = (bf16[128,512]{1,0:T(8,128)(2,1)S(1)}, bf16[128,512]{1,0:T(8,128)(2,1)S(1)}, u32[]{:S(2)}, u32[]{:S(2)}) collective-permute-start(bf16[128,512]{1,0:T(8,128)(2,1)S(1)} %pad_maximum_fusion.5), channel_id=1, source_target_pairs={{0,16},{1,65},{2,18},{3,67},{4,20},{5,69},{6,22},{7,71},{8,24},{9,... | collective-permute-start | bytes 393224 | tf_op jit(solution)/shard_map/ppermute | solution.py:362
  58.3 7.8 %collective-permute-start.23 = (bf16[128,512]{1,0:T(8,128)(2,1)S(1)}, bf16[128,512]{1,0:T(8,128)(2,1)S(1)}, u32[]{:S(2)}, u32[]{:S(2)}) collective-permute-start(bf16[128,512]{1,0:T(8,128)(2,1)S(1)} %pad_maximum_fusion.5), channel_id=1, source_target_pairs={{0,8},{1,33},{2,10},{3,35},{4,12},{5,37},{6,14},{7,39},{8,16},{9,4... | collective-permute-start | bytes 393224 | tf_op jit(solution)/shard_map/ppermute | solution.py:362
  68.0 6.8 %collective-permute-start.30 = (bf16[128,512]{1,0:T(8,128)(2,1)S(1)}, bf16[128,512]{1,0:T(8,128)(2,1)S(1)}, u32[]{:S(2)}, u32[]{:S(2)}) collective-permute-start(bf16[128,512]{1,0:T(8,128)(2,1)S(1)} %get-tuple-element.180.refs_1_.refs_0_), channel_id=1, source_target_pairs={{0,32},{1,9},{2,34},{3,11},{4,36},{5,13},{6,38},{7,15},{8,40},{9,1... | collective-permute-start | bytes 393224 | tf_op jit(solution)/shard_map/ppermute | solution.py:374
  69.7 8.2 %collective-permute-start.27 = (bf16[128,512]{1,0:T(8,128)(2,1)S(1)}, bf16[128,512]{1,0:T(8,128)(2,1)S(1)}, u32[]{:S(2)}, u32[]{:S(2)}) collective-permute-start(bf16[128,512]{1,0:T(8,128)(2,1)S(1)} %get-tuple-element.171), channel_id=1, source_target_pairs={{0,6},{1,7},{2,0},{3,1},{4,2},{5,3},{6,4},{7,5},{8,14},{9,15},{10,... | collective-permute-start | bytes 393224 | tf_op jit(solution)/shard_map/ppermute | solution.py:362
  70.2 7.7 %collective-permute-start.28 = (bf16[128,512]{1,0:T(8,128)(2,1)S(1)}, bf16[128,512]{1,0:T(8,128)(2,1)S(1)}, u32[]{:S(2)}, u32[]{:S(2)}) collective-permute-start(bf16[128,512]{1,0:T(8,128)(2,1)S(1)} %get-tuple-element.172), channel_id=1, source_target_pairs={{0,4},{1,5},{2,6},{3,7},{4,0},{5,1},{6,2},{7,3},{8,12},{9,13},{10,... | collective-permute-start | bytes 393224 | tf_op jit(solution)/shard_map/ppermute | solution.py:362
  72.3 7.2 %collective-permute-start.29 = (bf16[128,512]{1,0:T(8,128)(2,1)S(1)}, bf16[128,512]{1,0:T(8,128)(2,1)S(1)}, u32[]{:S(2)}, u32[]{:S(2)}) collective-permute-start(bf16[128,512]{1,0:T(8,128)(2,1)S(1)} %get-tuple-element.173), channel_id=1, source_target_pairs={{0,2},{1,3},{2,4},{3,5},{4,6},{5,7},{6,0},{7,1},{8,10},{9,11},{10,... | collective-permute-start | bytes 393224 | tf_op jit(solution)/shard_map/ppermute | solution.py:362
  73.1 6.5 %collective-permute-start.32 = (bf16[128,512]{1,0:T(8,128)(2,1)S(1)}, bf16[128,512]{1,0:T(8,128)(2,1)S(1)}, u32[]{:S(2)}, u32[]{:S(2)}) collective-permute-start(bf16[128,512]{1,0:T(8,128)(2,1)S(1)} %get-tuple-element.180.refs_1_.refs_0_), channel_id=1, source_target_pairs={{0,96},{1,25},{2,98},{3,27},{4,100},{5,29},{6,102},{7,31},{8,104},... | collective-permute-start | bytes 393224 | tf_op jit(solution)/shard_map/ppermute | solution.py:375
  74.8 5.3 %collective-permute-start.31 = (bf16[128,512]{1,0:T(8,128)(2,1)S(1)}, bf16[128,512]{1,0:T(8,128)(2,1)S(1)}, u32[]{:S(2)}, u32[]{:S(2)}) collective-permute-start(bf16[128,512]{1,0:T(8,128)(2,1)S(1)} %collective-permute-done.30.refs_1_), channel_id=1, source_target_pairs={{0,32},{1,9},{2,34},{3,11},{4,36},{5,13},{6,38},{7,15},{8,40},{9,1... | collective-permute-start | bytes 393224 | tf_op jit(solution)/shard_map/ppermute | solution.py:376
  85.5 14.3 %all-to-all-start = ((f32[128,1,128]{2,1,0:T(1,128)}), f32[128,1,128]{2,1,0:T(1,128)S(1)}, u32[]{:S(2)}, u32[]{:S(2)}) async-start(f32[128,1,128]{2,1,0:T(1,128)} %get-tuple-element.186), calls=%async_computation | async-start | bytes 131072 | tf_op jit(solution)/shard_map/all_to_all | solution.py:513
  (7 other events, 61.6 us)

commit v5 on v4

--- a/solution.py
+++ b/solution.py
@@ -14,7 +14,8 @@
 N_NODE = 8
 CAP_NODE = 64
 SLOTS = 512
-TILE = 512
+TILE = 1024
+CHUNK = 512
 VMEM_LIMIT = 24 * 2**20
 STEP = 0.3
 F32 = jnp.float32
@@ -65,13 +66,13 @@
     )(*arrays)
 
 
-def parts():
-    return [slice(i * TILE, (i + 1) * TILE) for i in range(NC // TILE)]
+def parts(size=TILE):
+    return [slice(i * size, (i + 1) * size) for i in range(NC // size)]
 
 
 def first(parent_far, section_far, y_far, linking_far, x_far, cost_far, *refs):
     *outs, y, linking, ylow, nsend, nback, lsend, lback, scol, x_top, cost_top, state, parent_of, section_of, sem = refs
-    chunks = parts()
+    chunks = parts(CHUNK)
     copies = []
     for cols in chunks:
         copies.append((y_far.at[:, cols], y.at[:, cols]))
@@ -419,7 +420,7 @@
         [
             pltpu.VMEM((NODES,), jnp.int32),
             pltpu.VMEM((NODES,), jnp.int32),
-            pltpu.SemaphoreType.DMA((3 * NC // TILE + 4,)),
+            pltpu.SemaphoreType.DMA((3 * NC // CHUNK + 4,)),
         ],
         (0, 1, 2, 3, 4, 5),
     )

time: 103 us -> 103 us (level)
  no operation moved by 1% of the time
where the time goes in v5:
time: 103 us
  starting transfers between devices  49.1 us (48%)
  waiting for transfers between devices  25.1 us (24%)
  Pallas kernels  21.5 us (21%)
  between operations  4.25 us (4%)
  local copies, waits for them, and re-layouts  2.28 us (2%)
    ppermute x24, starting transfers between devices, shifted(): got[k] = lax.ppermute(blocks[k], *ring(sign * k % 4))  30.3 us
    pallas_call x15, Pallas kernels, call(): pl.pallas_call(kernel, out_shape=out_shapes, in_specs=[pl.BlockSpec(memor...  21.5 us
    ppermute x24, waiting for transfers between devices, shifted(): got[k] = lax.ppermute(blocks[k], *ring(sign * k % 4))  14.6 us
    ppermute x4, starting transfers between devices, sibling(): return lax.ppermute(array, *pairs_of(lambda y, z, x, c: (y, z, x, 1 - c)))  9.59 us
    all_to_all x1, waiting for transfers between devices, shards(): lax.all_to_all(load, ('leaf', 'node'), split_axis=0, concat_axis=0, tiled...  8.04 us
    all_to_all x1, starting transfers between devices, shards(): lax.all_to_all(load, ('leaf', 'node'), split_axis=0, concat_axis=0, tiled...  4.83 us
    ppermute x2, starting transfers between devices, ring_gather(): three = lax.ppermute(rows, *ring(3))  4.18 us
  transfers between devices with their start and end apart: 35, of which 15 were waited for; matrix products, arithmetic and copies ran while one was open for 2% of the time, Pallas kernels for 15%

profile of v5, /device:TPU:1, one launch (start us, length us, event | category | flops | bytes accessed | tf_op | source)
XLA Modules:
  0.0 102.7 jit_solution(16595235730586041845)
XLA Ops:
  0.6 4.4 %shard_map.112 = (bf16[128,640]{1,0:T(8,128)(2,1)S(1)}, bf16[128,640]{1,0:T(8,128)(2,1)S(1)}, bf16[128,640]{1,0:T(8,128)(2,1)S(1)}, bf16[128,640]{1,0:T(8,128)(2...) custom-call(s32[288]{0:T(512)} %parent_far.1, ...), custom_call_target="tpu_custom_call" | custom-call | flops 1073741824 | bytes 2150944 | tf_op jit(solution)/shard_map/pallas_call | solution.py:58
  5.1 2.5 %collective-permute-start.3 = (bf16[128,512]{1,0:T(8,128)(2,1)S(1)}, bf16[128,512]{1,0:T(8,128)(2,1)S(1)}, u32[]{:S(2)}, u32[]{:S(2)}) collective-permute-start(bf16[128,512]{1,0:T(8,128)(2,1)S(1)} %get-tuple-element.100), channel_id=1, source_target_pairs={{0,32},{1,9},{2,34},{3,11},{4,36},{5,13},{6,38},{7,15},{8,40},{9,1... | collective-permute-start | bytes 393224 | tf_op jit(solution)/shard_map/ppermute | solution.py:363
  7.6 3.3 %collective-permute-start.4 = (bf16[128,512]{1,0:T(8,128)(2,1)S(1)}, bf16[128,512]{1,0:T(8,128)(2,1)S(1)}, u32[]{:S(2)}, u32[]{:S(2)}) collective-permute-start(bf16[128,512]{1,0:T(8,128)(2,1)S(1)} %get-tuple-element.101), channel_id=1, source_target_pairs={{0,64},{1,17},{2,66},{3,19},{4,68},{5,21},{6,70},{7,23},{8,72},{9,... | collective-permute-start | bytes 393224 | tf_op jit(solution)/shard_map/ppermute | solution.py:363
  12.9 2.4 %collective-permute-start.1 = (bf16[128,640]{1,0:T(8,128)(2,1)S(1)}, bf16[128,640]{1,0:T(8,128)(2,1)S(1)}, u32[]{:S(2)}, u32[]{:S(2)}) collective-permute-start(bf16[128,640]{1,0:T(8,128)(2,1)S(1)} %get-tuple-element.97), channel_id=1, source_target_pairs={{0,4},{1,5},{2,6},{3,7},{4,0},{5,1},{6,2},{7,3},{8,12},{9,13},{10,... | collective-permute-start | bytes 491528 | tf_op jit(solution)/shard_map/ppermute | solution.py:363
  17.1 2.8 %collective-permute-start.8 = (bf16[160,512]{1,0:T(8,128)(2,1)S(1)}, bf16[160,512]{1,0:T(8,128)(2,1)S(1)}, u32[]{:S(2)}, u32[]{:S(2)}) collective-permute-start(bf16[160,512]{1,0:T(8,128)(2,1)S(1)} %pad_maximum_fusion.4), channel_id=1, source_target_pairs={{0,24},{1,97},{2,26},{3,99},{4,28},{5,101},{6,30},{7,103},{8,0},{9... | collective-permute-start | bytes 491528 | tf_op jit(solution)/shard_map/ppermute | solution.py:363
  21.0 1.3 %shard_map.114.own = f32[256,512]{1,0:T(8,128)S(1)} custom-call(bf16[288,2048]{1,0:T(8,128)(2,1)S(1)} %get-tuple-element.103.ylow, f32[256,128]{1,0:T(8,128)S(1)} %get-tuple-element.110.scol.refs_2_, bf16[3,2048,512]{2,1,0:T(8,128)(2,1)S(1)} %copy-done), custom_call_target="tpu_custom_call" | custom-call | flops 1073741824 | bytes 1015808 | tf_op jit(solution)/shard_map/pallas_call | solution.py:58
  22.4 1.5 %collective-permute-done.8.g3 = bf16[160,512]{1,0:T(8,128)(2,1)S(1)} collective-permute-done((bf16[160,512]{1,0:T(8,128)(2,1)S(1)}, bf16[160,512]{1,0:T(8,128)(2,1)S(1)}, u32[]{:S(2)}, u32[]{:S(2)}) %collective-permute-start.8) | collective-permute-done | bytes 163872 | tf_op jit(solution)/shard_map/ppermute | solution.py:363
  24.0 1.8 %collective-permute-done.7.g2 = bf16[160,512]{1,0:T(8,128)(2,1)S(1)} collective-permute-done((bf16[160,512]{1,0:T(8,128)(2,1)S(1)}, bf16[160,512]{1,0:T(8,128)(2,1)S(1)}, u32[]{:S(2)}, u32[]{:S(2)}) %collective-permute-start.7) | collective-permute-done | bytes 163872 | tf_op jit(solution)/shard_map/ppermute | solution.py:363
  25.7 1.9 %collective-permute-done.6.g1 = bf16[160,512]{1,0:T(8,128)(2,1)S(1)} collective-permute-done((bf16[160,512]{1,0:T(8,128)(2,1)S(1)}, bf16[160,512]{1,0:T(8,128)(2,1)S(1)}, u32[]{:S(2)}, u32[]{:S(2)}) %collective-permute-start.6) | collective-permute-done | bytes 163872 | tf_op jit(solution)/shard_map/ppermute | solution.py:363
  27.7 3.5 %collective-permute-start.9 = (bf16[256,640]{1,0:T(8,128)(2,1)S(1)}, bf16[256,640]{1,0:T(8,128)(2,1)S(1)}, u32[]{:S(2)}, u32[]{:S(2)}) collective-permute-start(bf16[256,640]{1,0:T(8,128)(2,1)S(1)} %pad_maximum_fusion), channel_id=1, source_target_pairs={{0,1},{1,0},{2,3},{3,2},{4,5},{5,4},{6,7},{7,6},{8,9},{9,8},{10,11... | collective-permute-start | bytes 983048 | tf_op jit(solution)/shard_map/ppermute | solution.py:357
  33.3 2.1 %collective-permute-start.11 = (bf16[128,512]{1,0:T(8,128)(2,1)S(1)}, bf16[128,512]{1,0:T(8,128)(2,1)S(1)}, u32[]{:S(2)}, u32[]{:S(2)}) collective-permute-start(bf16[128,512]{1,0:T(8,128)(2,1)S(1)} %get-tuple-element.123), channel_id=1, source_target_pairs={{0,4},{1,5},{2,6},{3,7},{4,0},{5,1},{6,2},{7,3},{8,12},{9,13},{10,... | collective-permute-start | bytes 393224 | tf_op jit(solution)/shard_map/ppermute | solution.py:363
  35.4 2.5 %collective-permute-start.15 = (bf16[128,512]{1,0:T(8,128)(2,1)S(1)}, bf16[128,512]{1,0:T(8,128)(2,1)S(1)}, u32[]{:S(2)}, u32[]{:S(2)}) collective-permute-start(bf16[128,512]{1,0:T(8,128)(2,1)S(1)} %get-tuple-element.133.refs_1_.refs_0_), channel_id=1, source_target_pairs={{0,96},{1,25},{2,98},{3,27},{4,100},{5,29},{6,102},{7,31},{8,104},... | collective-permute-start | bytes 393224 | tf_op jit(solution)/shard_map/ppermute | solution.py:376
  37.9 2.5 %shard_map.117 = (f32[288,2048]{1,0:T(8,128)S(1)}, f32[32,512]{1,0:T(8,128)S(1)}) custom-call(bf16[256,512]{1,0:T(8,128)(2,1)S(1)} %get-tuple-element.126.refs_0_, bf16[128,512]{1,0:T(8,128)(2,1)S(1)} %get-tuple-element.133.refs_1_.refs_0_, f32[256,128]{1,0:T(8,128)S(1)} %get-tuple-element.110.scol.refs_2_, bf16[3,2048,512]{2,1,0:T(8,128)(2,1)S(1)} %copy-done, ...), custom_call_target="tpu_custom_call" | custom-call | flops 1073741824 | bytes 1753216 | tf_op jit(solution)/shard_map/pallas_call | solution.py:58
  40.4 2.1 %collective-permute-done.12.g3 = bf16[128,512]{1,0:T(8,128)(2,1)S(1)} collective-permute-done((bf16[128,512]{1,0:T(8,128)(2,1)S(1)}, bf16[128,512]{1,0:T(8,128)(2,1)S(1)}, u32[]{:S(2)}, u32[]{:S(2)}) %collective-permute-start.12) | collective-permute-done | bytes 131104 | tf_op jit(solution)/shard_map/ppermute | solution.py:363
  43.2 2.0 %collective-permute-start.16 = (bf16[256,512]{1,0:T(8,128)(2,1)S(1)}, bf16[256,512]{1,0:T(8,128)(2,1)S(1)}, u32[]{:S(2)}, u32[]{:S(2)}) collective-permute-start(bf16[256,512]{1,0:T(8,128)(2,1)S(1)} %pad_maximum_fusion.1), channel_id=1, source_target_pairs={{0,1},{1,0},{2,3},{3,2},{4,5},{5,4},{6,7},{7,6},{8,9},{9,8},{10,11... | collective-permute-start | bytes 786440 | tf_op jit(solution)/shard_map/ppermute | solution.py:357
  45.2 1.9 %shard_map.118 = (f32[256,2048]{1,0:T(8,128)S(1)}, bf16[128,512]{1,0:T(8,128)(2,1)S(1)}, bf16[128,512]{1,0:T(8,128)(2,1)S(1)}, bf16[128,512]{1,0:T(8,128)(2,1)S(1)}, bf16[128,512]{1,0:T(8,128)(2,1)S(1)}) custom-call(bf16[128,512]{1,0:T(8,128)(2,1)S(1)} %get-tuple-element.133.refs_1_.refs_0_, bf16[128,512]{1,0:T(8,128)(2,1)S(1)} %collective-permute-done.13.refs_1_, ...), custom_call_target="tpu_custom_call" | custom-call | flops 1073741824 | bytes 1229056 | tf_op jit(solution)/shard_map/pallas_call | solution.py:58
  47.2 1.8 %collective-permute-start.21 = (bf16[128,512]{1,0:T(8,128)(2,1)S(1)}, bf16[128,512]{1,0:T(8,128)(2,1)S(1)}, u32[]{:S(2)}, u32[]{:S(2)}) collective-permute-start(bf16[128,512]{1,0:T(8,128)(2,1)S(1)} %get-tuple-element.147), channel_id=1, source_target_pairs={{0,64},{1,17},{2,66},{3,19},{4,68},{5,21},{6,70},{7,23},{8,72},{9,... | collective-permute-start | bytes 393224 | tf_op jit(solution)/shard_map/ppermute | solution.py:363
  49.9 1.9 %shard_map.119 = (f32[288,2048]{1,0:T(8,128)S(1)}, bf16[288,2048]{1,0:T(8,128)(2,1)S(1)}, bf16[128,512]{1,0:T(8,128)(2,1)S(1)}, bf16[128,512]{1,0:T(8,128)(2,1)S...) custom-call(bf16[128,512]{1,0:T(8,128)(2,1)S(1)} %get-tuple-element.121.g0, ...), custom_call_target="tpu_custom_call" | custom-call | flops 1073741824 | bytes 1704192 | tf_op jit(solution)/shard_map/pallas_call | solution.py:58
  52.5 3.4 %collective-permute-start.18 = (bf16[128,512]{1,0:T(8,128)(2,1)S(1)}, bf16[128,512]{1,0:T(8,128)(2,1)S(1)}, u32[]{:S(2)}, u32[]{:S(2)}) collective-permute-start(bf16[128,512]{1,0:T(8,128)(2,1)S(1)} %get-tuple-element.143), channel_id=1, source_target_pairs={{0,4},{1,5},{2,6},{3,7},{4,0},{5,1},{6,2},{7,3},{8,12},{9,13},{10,... | collective-permute-start | bytes 393224 | tf_op jit(solution)/shard_map/ppermute | solution.py:363
  58.9 1.3 %shard_map.120.own = f32[256,512]{1,0:T(8,128)S(1)} custom-call(bf16[288,2048]{1,0:T(8,128)(2,1)S(1)} %get-tuple-element.155.ylow, f32[256,128]{1,0:T(8,128)S(1)} %get-tuple-element.110.scol.refs_2_, bf16[3,2048,512]{2,1,0:T(8,128)(2,1)S(1)} %copy-done), custom_call_target="tpu_custom_call" | custom-call | flops 1073741824 | bytes 1015808 | tf_op jit(solution)/shard_map/pallas_call | solution.py:58
  60.2 1.6 %collective-permute-done.18.g2 = bf16[128,512]{1,0:T(8,128)(2,1)S(1)} collective-permute-done((bf16[128,512]{1,0:T(8,128)(2,1)S(1)}, bf16[128,512]{1,0:T(8,128)(2,1)S(1)}, u32[]{:S(2)}, u32[]{:S(2)}) %collective-permute-start.18) | collective-permute-done | bytes 131104 | tf_op jit(solution)/shard_map/ppermute | solution.py:363
  62.8 2.9 %collective-permute-done.23.g1 = bf16[128,512]{1,0:T(8,128)(2,1)S(1)} collective-permute-done((bf16[128,512]{1,0:T(8,128)(2,1)S(1)}, bf16[128,512]{1,0:T(8,128)(2,1)S(1)}, u32[]{:S(2)}, u32[]{:S(2)}) %collective-permute-start.23) | collective-permute-done | bytes 131104 | tf_op jit(solution)/shard_map/ppermute | solution.py:363
  65.7 1.8 %collective-permute-start.26 = (bf16[256,512]{1,0:T(8,128)(2,1)S(1)}, bf16[256,512]{1,0:T(8,128)(2,1)S(1)}, u32[]{:S(2)}, u32[]{:S(2)}) collective-permute-start(bf16[256,512]{1,0:T(8,128)(2,1)S(1)} %pad_maximum_fusion.2), channel_id=1, source_target_pairs={{0,1},{1,0},{2,3},{3,2},{4,5},{5,4},{6,7},{7,6},{8,9},{9,8},{10,11... | collective-permute-start | bytes 786440 | tf_op jit(solution)/shard_map/ppermute | solution.py:357
  69.8 2.1 %collective-permute-start.28 = (bf16[128,512]{1,0:T(8,128)(2,1)S(1)}, bf16[128,512]{1,0:T(8,128)(2,1)S(1)}, u32[]{:S(2)}, u32[]{:S(2)}) collective-permute-start(bf16[128,512]{1,0:T(8,128)(2,1)S(1)} %get-tuple-element.172), channel_id=1, source_target_pairs={{0,4},{1,5},{2,6},{3,7},{4,0},{5,1},{6,2},{7,3},{8,12},{9,13},{10,... | collective-permute-start | bytes 393224 | tf_op jit(solution)/shard_map/ppermute | solution.py:363
  72.7 1.7 %collective-permute-start.32 = (bf16[128,512]{1,0:T(8,128)(2,1)S(1)}, bf16[128,512]{1,0:T(8,128)(2,1)S(1)}, u32[]{:S(2)}, u32[]{:S(2)}) collective-permute-start(bf16[128,512]{1,0:T(8,128)(2,1)S(1)} %get-tuple-element.180.refs_1_.refs_0_), channel_id=1, source_target_pairs={{0,96},{1,25},{2,98},{3,27},{4,100},{5,29},{6,102},{7,31},{8,104},... | collective-permute-start | bytes 393224 | tf_op jit(solution)/shard_map/ppermute | solution.py:376
  74.4 2.1 %shard_map.124.refs_6_.base = f32[288,2048]{1,0:T(8,128)S(1)} custom-call(bf16[256,512]{1,0:T(8,128)(2,1)S(1)} %get-tuple-element.175.refs_0_, bf16[128,512]{1,0:T(8,128)(2,1)S(1)} %get-tuple-element.180.refs_1_.refs_0_, f32[256,128]{1,0:T(8,128)S(1)} %get-tuple-element.110.scol.refs_2_, bf16[3,2048,512]{2,1,0:T(8,128)(2,1)S(1)} %copy-done, ...), custom_call_target="tpu_custom_call" | custom-call | flops 1073741824 | bytes 1745024 | tf_op jit(solution)/shard_map/pallas_call | solution.py:58
  77.6 1.5 %collective-permute-done.29.g3 = bf16[128,512]{1,0:T(8,128)(2,1)S(1)} collective-permute-done((bf16[128,512]{1,0:T(8,128)(2,1)S(1)}, bf16[128,512]{1,0:T(8,128)(2,1)S(1)}, u32[]{:S(2)}, u32[]{:S(2)}) %collective-permute-start.29) | collective-permute-done | bytes 131104 | tf_op jit(solution)/shard_map/ppermute | solution.py:363
  79.7 2.3 %collective-permute-start.33 = (bf16[256,512]{1,0:T(8,128)(2,1)S(1)}, bf16[256,512]{1,0:T(8,128)(2,1)S(1)}, u32[]{:S(2)}, u32[]{:S(2)}) collective-permute-start(bf16[256,512]{1,0:T(8,128)(2,1)S(1)} %pad_maximum_fusion.3), channel_id=1, source_target_pairs={{0,1},{1,0},{2,3},{3,2},{4,5},{5,4},{6,7},{7,6},{8,9},{9,8},{10,11... | collective-permute-start | bytes 786440 | tf_op jit(solution)/shard_map/ppermute | solution.py:357
  83.1 2.0 %shard_map.126 = (f32[288,2048]{1,0:T(8,128)S(1)}, f32[128,1,128]{2,1,0:T(1,128)}) custom-call(bf16[128,512]{1,0:T(8,128)(2,1)S(1)} %get-tuple-element.170.g0, bf16[128,512]{1,0:T(8,128)(2,1)S(1)} %collective-permute-done.27.g1, bf16[128,512]{1,0:T(8,128)(2,1)S(1)} %collective-permute-done.28.g2, bf16[128,512]{1,0:T(8,128)(2,1)S(1)} %collective-permute-done.29.g3, ...), custom_call_target="tpu_custom_call" | custom-call | flops 536870912 | bytes 2089600 | tf_op jit(solution)/shard_map/pallas_call | solution.py:58
  85.1 4.8 %all-to-all-start = ((f32[128,1,128]{2,1,0:T(1,128)}), f32[128,1,128]{2,1,0:T(1,128)S(1)}, u32[]{:S(2)}, u32[]{:S(2)}) async-start(f32[128,1,128]{2,1,0:T(1,128)} %get-tuple-element.186), calls=%async_computation | async-start | bytes 131072 | tf_op jit(solution)/shard_map/all_to_all | solution.py:514
  90.0 1.4 %copy.12 = f32[288,2048]{1,0:T(8,128)} copy(f32[288,2048]{1,0:T(8,128)S(1)} %get-tuple-element.194) | data formatting | bytes 4718592
  91.4 8.0 %all-to-all-done = f32[128,1,128]{2,1,0:T(1,128)S(1)} async-done(((f32[128,1,128]{2,1,0:T(1,128)}), f32[128,1,128]{2,1,0:T(1,128)S(1)}, u32[]{:S(2)}, u32[]{:S(2)}) %all-to-all-start) | async-done | bytes 65568 | tf_op jit(solution)/shard_map/all_to_all | solution.py:514
  (94 shorter events, 19.2 us)
Async XLA Ops:
  5.1 10.7 %collective-permute-start.3 = (bf16[128,512]{1,0:T(8,128)(2,1)S(1)}, bf16[128,512]{1,0:T(8,128)(2,1)S(1)}, u32[]{:S(2)}, u32[]{:S(2)}) collective-permute-start(bf16[128,512]{1,0:T(8,128)(2,1)S(1)} %get-tuple-element.100), channel_id=1, source_target_pairs={{0,32},{1,9},{2,34},{3,11},{4,36},{5,13},{6,38},{7,15},{8,40},{9,1... | collective-permute-start | bytes 393224 | tf_op jit(solution)/shard_map/ppermute | solution.py:363
  7.6 9.4 %collective-permute-start.4 = (bf16[128,512]{1,0:T(8,128)(2,1)S(1)}, bf16[128,512]{1,0:T(8,128)(2,1)S(1)}, u32[]{:S(2)}, u32[]{:S(2)}) collective-permute-start(bf16[128,512]{1,0:T(8,128)(2,1)S(1)} %get-tuple-element.101), channel_id=1, source_target_pairs={{0,64},{1,17},{2,66},{3,19},{4,68},{5,21},{6,70},{7,23},{8,72},{9,... | collective-permute-start | bytes 393224 | tf_op jit(solution)/shard_map/ppermute | solution.py:363
  10.9 6.1 %collective-permute-start.5 = (bf16[128,512]{1,0:T(8,128)(2,1)S(1)}, bf16[128,512]{1,0:T(8,128)(2,1)S(1)}, u32[]{:S(2)}, u32[]{:S(2)}) collective-permute-start(bf16[128,512]{1,0:T(8,128)(2,1)S(1)} %get-tuple-element.102), channel_id=1, source_target_pairs={{0,96},{1,25},{2,98},{3,27},{4,100},{5,29},{6,102},{7,31},{8,104},... | collective-permute-start | bytes 393224 | tf_op jit(solution)/shard_map/ppermute | solution.py:363
  11.6 8.6 %collective-permute-start = (bf16[128,640]{1,0:T(8,128)(2,1)S(1)}, bf16[128,640]{1,0:T(8,128)(2,1)S(1)}, u32[]{:S(2)}, u32[]{:S(2)}) collective-permute-start(bf16[128,640]{1,0:T(8,128)(2,1)S(1)} %get-tuple-element.96), channel_id=1, source_target_pairs={{0,2},{1,3},{2,4},{3,5},{4,6},{5,7},{6,0},{7,1},{8,10},{9,11},{10,... | collective-permute-start | bytes 491528 | tf_op jit(solution)/shard_map/ppermute | solution.py:363
  12.9 9.5 %collective-permute-start.1 = (bf16[128,640]{1,0:T(8,128)(2,1)S(1)}, bf16[128,640]{1,0:T(8,128)(2,1)S(1)}, u32[]{:S(2)}, u32[]{:S(2)}) collective-permute-start(bf16[128,640]{1,0:T(8,128)(2,1)S(1)} %get-tuple-element.97), channel_id=1, source_target_pairs={{0,4},{1,5},{2,6},{3,7},{4,0},{5,1},{6,2},{7,3},{8,12},{9,13},{10,... | collective-permute-start | bytes 491528 | tf_op jit(solution)/shard_map/ppermute | solution.py:363
  15.8 6.6 %collective-permute-start.2 = (bf16[128,640]{1,0:T(8,128)(2,1)S(1)}, bf16[128,640]{1,0:T(8,128)(2,1)S(1)}, u32[]{:S(2)}, u32[]{:S(2)}) collective-permute-start(bf16[128,640]{1,0:T(8,128)(2,1)S(1)} %get-tuple-element.98), channel_id=1, source_target_pairs={{0,6},{1,7},{2,0},{3,1},{4,2},{5,3},{6,4},{7,5},{8,14},{9,15},{10,... | collective-permute-start | bytes 491528 | tf_op jit(solution)/shard_map/ppermute | solution.py:363
  17.1 6.8 %collective-permute-start.8 = (bf16[160,512]{1,0:T(8,128)(2,1)S(1)}, bf16[160,512]{1,0:T(8,128)(2,1)S(1)}, u32[]{:S(2)}, u32[]{:S(2)}) collective-permute-start(bf16[160,512]{1,0:T(8,128)(2,1)S(1)} %pad_maximum_fusion.4), channel_id=1, source_target_pairs={{0,24},{1,97},{2,26},{3,99},{4,28},{5,101},{6,30},{7,103},{8,0},{9... | collective-permute-start | bytes 491528 | tf_op jit(solution)/shard_map/ppermute | solution.py:363
  20.0 5.8 %collective-permute-start.7 = (bf16[160,512]{1,0:T(8,128)(2,1)S(1)}, bf16[160,512]{1,0:T(8,128)(2,1)S(1)}, u32[]{:S(2)}, u32[]{:S(2)}) collective-permute-start(bf16[160,512]{1,0:T(8,128)(2,1)S(1)} %pad_maximum_fusion.4), channel_id=1, source_target_pairs={{0,16},{1,65},{2,18},{3,67},{4,20},{5,69},{6,22},{7,71},{8,24},{9,... | collective-permute-start | bytes 491528 | tf_op jit(solution)/shard_map/ppermute | solution.py:363
  20.3 7.4 %collective-permute-start.6 = (bf16[160,512]{1,0:T(8,128)(2,1)S(1)}, bf16[160,512]{1,0:T(8,128)(2,1)S(1)}, u32[]{:S(2)}, u32[]{:S(2)}) collective-permute-start(bf16[160,512]{1,0:T(8,128)(2,1)S(1)} %pad_maximum_fusion.4), channel_id=1, source_target_pairs={{0,8},{1,33},{2,10},{3,35},{4,12},{5,37},{6,14},{7,39},{8,16},{9,4... | collective-permute-start | bytes 491528 | tf_op jit(solution)/shard_map/ppermute | solution.py:363
  27.7 4.8 %collective-permute-start.9 = (bf16[256,640]{1,0:T(8,128)(2,1)S(1)}, bf16[256,640]{1,0:T(8,128)(2,1)S(1)}, u32[]{:S(2)}, u32[]{:S(2)}) collective-permute-start(bf16[256,640]{1,0:T(8,128)(2,1)S(1)} %pad_maximum_fusion), channel_id=1, source_target_pairs={{0,1},{1,0},{2,3},{3,2},{4,5},{5,4},{6,7},{7,6},{8,9},{9,8},{10,11... | collective-permute-start | bytes 983048 | tf_op jit(solution)/shard_map/ppermute | solution.py:357
  32.2 5.7 %collective-permute-start.13 = (bf16[128,512]{1,0:T(8,128)(2,1)S(1)}, bf16[128,512]{1,0:T(8,128)(2,1)S(1)}, u32[]{:S(2)}, u32[]{:S(2)}) collective-permute-start(bf16[128,512]{1,0:T(8,128)(2,1)S(1)} %get-tuple-element.133.refs_1_.refs_0_), channel_id=1, source_target_pairs={{0,32},{1,9},{2,34},{3,11},{4,36},{5,13},{6,38},{7,15},{8,40},{9,1... | collective-permute-start | bytes 393224 | tf_op jit(solution)/shard_map/ppermute | solution.py:375
  33.2 7.2 %collective-permute-start.10 = (bf16[128,512]{1,0:T(8,128)(2,1)S(1)}, bf16[128,512]{1,0:T(8,128)(2,1)S(1)}, u32[]{:S(2)}, u32[]{:S(2)}) collective-permute-start(bf16[128,512]{1,0:T(8,128)(2,1)S(1)} %get-tuple-element.122), channel_id=1, source_target_pairs={{0,6},{1,7},{2,0},{3,1},{4,2},{5,3},{6,4},{7,5},{8,14},{9,15},{10,... | collective-permute-start | bytes 393224 | tf_op jit(solution)/shard_map/ppermute | solution.py:363
  33.3 7.1 %collective-permute-start.11 = (bf16[128,512]{1,0:T(8,128)(2,1)S(1)}, bf16[128,512]{1,0:T(8,128)(2,1)S(1)}, u32[]{:S(2)}, u32[]{:S(2)}) collective-permute-start(bf16[128,512]{1,0:T(8,128)(2,1)S(1)} %get-tuple-element.123), channel_id=1, source_target_pairs={{0,4},{1,5},{2,6},{3,7},{4,0},{5,1},{6,2},{7,3},{8,12},{9,13},{10,... | collective-permute-start | bytes 393224 | tf_op jit(solution)/shard_map/ppermute | solution.py:363
  35.4 7.1 %collective-permute-start.12 = (bf16[128,512]{1,0:T(8,128)(2,1)S(1)}, bf16[128,512]{1,0:T(8,128)(2,1)S(1)}, u32[]{:S(2)}, u32[]{:S(2)}) collective-permute-start(bf16[128,512]{1,0:T(8,128)(2,1)S(1)} %get-tuple-element.124), channel_id=1, source_target_pairs={{0,2},{1,3},{2,4},{3,5},{4,6},{5,7},{6,0},{7,1},{8,10},{9,11},{10,... | collective-permute-start | bytes 393224 | tf_op jit(solution)/shard_map/ppermute | solution.py:363
  35.4 7.1 %collective-permute-start.15 = (bf16[128,512]{1,0:T(8,128)(2,1)S(1)}, bf16[128,512]{1,0:T(8,128)(2,1)S(1)}, u32[]{:S(2)}, u32[]{:S(2)}) collective-permute-start(bf16[128,512]{1,0:T(8,128)(2,1)S(1)} %get-tuple-element.133.refs_1_.refs_0_), channel_id=1, source_target_pairs={{0,96},{1,25},{2,98},{3,27},{4,100},{5,29},{6,102},{7,31},{8,104},... | collective-permute-start | bytes 393224 | tf_op jit(solution)/shard_map/ppermute | solution.py:376
  37.9 5.3 %collective-permute-start.14 = (bf16[128,512]{1,0:T(8,128)(2,1)S(1)}, bf16[128,512]{1,0:T(8,128)(2,1)S(1)}, u32[]{:S(2)}, u32[]{:S(2)}) collective-permute-start(bf16[128,512]{1,0:T(8,128)(2,1)S(1)} %collective-permute-done.13.refs_1_), channel_id=1, source_target_pairs={{0,32},{1,9},{2,34},{3,11},{4,36},{5,13},{6,38},{7,15},{8,40},{9,1... | collective-permute-start | bytes 393224 | tf_op jit(solution)/shard_map/ppermute | solution.py:377
  43.2 6.7 %collective-permute-start.16 = (bf16[256,512]{1,0:T(8,128)(2,1)S(1)}, bf16[256,512]{1,0:T(8,128)(2,1)S(1)}, u32[]{:S(2)}, u32[]{:S(2)}) collective-permute-start(bf16[256,512]{1,0:T(8,128)(2,1)S(1)} %pad_maximum_fusion.1), channel_id=1, source_target_pairs={{0,1},{1,0},{2,3},{3,2},{4,5},{5,4},{6,7},{7,6},{8,9},{9,8},{10,11... | collective-permute-start | bytes 786440 | tf_op jit(solution)/shard_map/ppermute | solution.py:357
  47.1 8.8 %collective-permute-start.20 = (bf16[128,512]{1,0:T(8,128)(2,1)S(1)}, bf16[128,512]{1,0:T(8,128)(2,1)S(1)}, u32[]{:S(2)}, u32[]{:S(2)}) collective-permute-start(bf16[128,512]{1,0:T(8,128)(2,1)S(1)} %get-tuple-element.146), channel_id=1, source_target_pairs={{0,32},{1,9},{2,34},{3,11},{4,36},{5,13},{6,38},{7,15},{8,40},{9,1... | collective-permute-start | bytes 393224 | tf_op jit(solution)/shard_map/ppermute | solution.py:363
  47.2 9.9 %collective-permute-start.21 = (bf16[128,512]{1,0:T(8,128)(2,1)S(1)}, bf16[128,512]{1,0:T(8,128)(2,1)S(1)}, u32[]{:S(2)}, u32[]{:S(2)}) collective-permute-start(bf16[128,512]{1,0:T(8,128)(2,1)S(1)} %get-tuple-element.147), channel_id=1, source_target_pairs={{0,64},{1,17},{2,66},{3,19},{4,68},{5,21},{6,70},{7,23},{8,72},{9,... | collective-permute-start | bytes 393224 | tf_op jit(solution)/shard_map/ppermute | solution.py:363
  49.0 8.1 %collective-permute-start.22 = (bf16[128,512]{1,0:T(8,128)(2,1)S(1)}, bf16[128,512]{1,0:T(8,128)(2,1)S(1)}, u32[]{:S(2)}, u32[]{:S(2)}) collective-permute-start(bf16[128,512]{1,0:T(8,128)(2,1)S(1)} %get-tuple-element.148), channel_id=1, source_target_pairs={{0,96},{1,25},{2,98},{3,27},{4,100},{5,29},{6,102},{7,31},{8,104},... | collective-permute-start | bytes 393224 | tf_op jit(solution)/shard_map/ppermute | solution.py:363
  51.7 6.2 %collective-permute-start.17 = (bf16[128,512]{1,0:T(8,128)(2,1)S(1)}, bf16[128,512]{1,0:T(8,128)(2,1)S(1)}, u32[]{:S(2)}, u32[]{:S(2)}) collective-permute-start(bf16[128,512]{1,0:T(8,128)(2,1)S(1)} %get-tuple-element.142), channel_id=1, source_target_pairs={{0,2},{1,3},{2,4},{3,5},{4,6},{5,7},{6,0},{7,1},{8,10},{9,11},{10,... | collective-permute-start | bytes 393224 | tf_op jit(solution)/shard_map/ppermute | solution.py:363
  52.5 9.3 %collective-permute-start.18 = (bf16[128,512]{1,0:T(8,128)(2,1)S(1)}, bf16[128,512]{1,0:T(8,128)(2,1)S(1)}, u32[]{:S(2)}, u32[]{:S(2)}) collective-permute-start(bf16[128,512]{1,0:T(8,128)(2,1)S(1)} %get-tuple-element.143), channel_id=1, source_target_pairs={{0,4},{1,5},{2,6},{3,7},{4,0},{5,1},{6,2},{7,3},{8,12},{9,13},{10,... | collective-permute-start | bytes 393224 | tf_op jit(solution)/shard_map/ppermute | solution.py:363
  55.9 5.8 %collective-permute-start.19 = (bf16[128,512]{1,0:T(8,128)(2,1)S(1)}, bf16[128,512]{1,0:T(8,128)(2,1)S(1)}, u32[]{:S(2)}, u32[]{:S(2)}) collective-permute-start(bf16[128,512]{1,0:T(8,128)(2,1)S(1)} %get-tuple-element.144), channel_id=1, source_target_pairs={{0,6},{1,7},{2,0},{3,1},{4,2},{5,3},{6,4},{7,5},{8,14},{9,15},{10,... | collective-permute-start | bytes 393224 | tf_op jit(solution)/shard_map/ppermute | solution.py:363
  57.3 5.5 %collective-permute-start.24 = (bf16[128,512]{1,0:T(8,128)(2,1)S(1)}, bf16[128,512]{1,0:T(8,128)(2,1)S(1)}, u32[]{:S(2)}, u32[]{:S(2)}) collective-permute-start(bf16[128,512]{1,0:T(8,128)(2,1)S(1)} %pad_maximum_fusion.5), channel_id=1, source_target_pairs={{0,16},{1,65},{2,18},{3,67},{4,20},{5,69},{6,22},{7,71},{8,24},{9,... | collective-permute-start | bytes 393224 | tf_op jit(solution)/shard_map/ppermute | solution.py:363
  57.9 7.8 %collective-permute-start.23 = (bf16[128,512]{1,0:T(8,128)(2,1)S(1)}, bf16[128,512]{1,0:T(8,128)(2,1)S(1)}, u32[]{:S(2)}, u32[]{:S(2)}) collective-permute-start(bf16[128,512]{1,0:T(8,128)(2,1)S(1)} %pad_maximum_fusion.5), channel_id=1, source_target_pairs={{0,8},{1,33},{2,10},{3,35},{4,12},{5,37},{6,14},{7,39},{8,16},{9,4... | collective-permute-start | bytes 393224 | tf_op jit(solution)/shard_map/ppermute | solution.py:363
  67.6 6.8 %collective-permute-start.30 = (bf16[128,512]{1,0:T(8,128)(2,1)S(1)}, bf16[128,512]{1,0:T(8,128)(2,1)S(1)}, u32[]{:S(2)}, u32[]{:S(2)}) collective-permute-start(bf16[128,512]{1,0:T(8,128)(2,1)S(1)} %get-tuple-element.180.refs_1_.refs_0_), channel_id=1, source_target_pairs={{0,32},{1,9},{2,34},{3,11},{4,36},{5,13},{6,38},{7,15},{8,40},{9,1... | collective-permute-start | bytes 393224 | tf_op jit(solution)/shard_map/ppermute | solution.py:375
  69.3 8.3 %collective-permute-start.27 = (bf16[128,512]{1,0:T(8,128)(2,1)S(1)}, bf16[128,512]{1,0:T(8,128)(2,1)S(1)}, u32[]{:S(2)}, u32[]{:S(2)}) collective-permute-start(bf16[128,512]{1,0:T(8,128)(2,1)S(1)} %get-tuple-element.171), channel_id=1, source_target_pairs={{0,6},{1,7},{2,0},{3,1},{4,2},{5,3},{6,4},{7,5},{8,14},{9,15},{10,... | collective-permute-start | bytes 393224 | tf_op jit(solution)/shard_map/ppermute | solution.py:363
  69.8 7.8 %collective-permute-start.28 = (bf16[128,512]{1,0:T(8,128)(2,1)S(1)}, bf16[128,512]{1,0:T(8,128)(2,1)S(1)}, u32[]{:S(2)}, u32[]{:S(2)}) collective-permute-start(bf16[128,512]{1,0:T(8,128)(2,1)S(1)} %get-tuple-element.172), channel_id=1, source_target_pairs={{0,4},{1,5},{2,6},{3,7},{4,0},{5,1},{6,2},{7,3},{8,12},{9,13},{10,... | collective-permute-start | bytes 393224 | tf_op jit(solution)/shard_map/ppermute | solution.py:363
  71.9 7.2 %collective-permute-start.29 = (bf16[128,512]{1,0:T(8,128)(2,1)S(1)}, bf16[128,512]{1,0:T(8,128)(2,1)S(1)}, u32[]{:S(2)}, u32[]{:S(2)}) collective-permute-start(bf16[128,512]{1,0:T(8,128)(2,1)S(1)} %get-tuple-element.173), channel_id=1, source_target_pairs={{0,2},{1,3},{2,4},{3,5},{4,6},{5,7},{6,0},{7,1},{8,10},{9,11},{10,... | collective-permute-start | bytes 393224 | tf_op jit(solution)/shard_map/ppermute | solution.py:363
  72.7 6.5 %collective-permute-start.32 = (bf16[128,512]{1,0:T(8,128)(2,1)S(1)}, bf16[128,512]{1,0:T(8,128)(2,1)S(1)}, u32[]{:S(2)}, u32[]{:S(2)}) collective-permute-start(bf16[128,512]{1,0:T(8,128)(2,1)S(1)} %get-tuple-element.180.refs_1_.refs_0_), channel_id=1, source_target_pairs={{0,96},{1,25},{2,98},{3,27},{4,100},{5,29},{6,102},{7,31},{8,104},... | collective-permute-start | bytes 393224 | tf_op jit(solution)/shard_map/ppermute | solution.py:376
  74.4 5.3 %collective-permute-start.31 = (bf16[128,512]{1,0:T(8,128)(2,1)S(1)}, bf16[128,512]{1,0:T(8,128)(2,1)S(1)}, u32[]{:S(2)}, u32[]{:S(2)}) collective-permute-start(bf16[128,512]{1,0:T(8,128)(2,1)S(1)} %collective-permute-done.30.refs_1_), channel_id=1, source_target_pairs={{0,32},{1,9},{2,34},{3,11},{4,36},{5,13},{6,38},{7,15},{8,40},{9,1... | collective-permute-start | bytes 393224 | tf_op jit(solution)/shard_map/ppermute | solution.py:377
  85.1 14.3 %all-to-all-start = ((f32[128,1,128]{2,1,0:T(1,128)}), f32[128,1,128]{2,1,0:T(1,128)S(1)}, u32[]{:S(2)}, u32[]{:S(2)}) async-start(f32[128,1,128]{2,1,0:T(1,128)} %get-tuple-element.186), calls=%async_computation | async-start | bytes 131072 | tf_op jit(solution)/shard_map/all_to_all | solution.py:514
  (7 other events, 61.6 us)

commit v6 on v5

--- a/solution.py
+++ b/solution.py
@@ -452,7 +452,9 @@
         2 * unit,
     )
     back_leaf = ring_gather(extra_root, outer_ring)
-    back_node, (back_leaf, base) = swap_node(out_node, -1, (back_leaf, base))
+    back_node, (back_leaf[1], back_leaf[3], base) = swap_node(
+        out_node, -1, (back_leaf[1], back_leaf[3], base)
+    )
     later, *out_leaf = call(
         part_of(dual_leaf, False),
         [kids_field] + [block] * 4,

time: 103 us -> 103 us (level)
    ppermute x2, waiting for transfers between devices: 1.2 us -> 0.11 us  [ring_gather(): return [rows, one, lax.ppermute(one, *ring(1)), three]]
  transfers between devices with their start and end apart: 35 -> 35, of which waited for: 15 -> 13; matrix products, arithmetic and copies ran while one was open for 2% -> 2% of each run, Pallas kernels for 15% -> 15%
where the time goes in v6:
time: 103 us
  starting transfers between devices  49.4 us (48%)
  waiting for transfers between devices  24.7 us (24%)
  Pallas kernels  21.5 us (21%)
  between operations  4.27 us (4%)
  local copies, waits for them, and re-layouts  2.28 us (2%)
    ppermute x24, starting transfers between devices, shifted(): got[k] = lax.ppermute(blocks[k], *ring(sign * k % 4))  30.4 us
    pallas_call x15, Pallas kernels, call(): pl.pallas_call(kernel, out_shape=out_shapes, in_specs=[pl.BlockSpec(memor...  21.5 us
    ppermute x24, waiting for transfers between devices, shifted(): got[k] = lax.ppermute(blocks[k], *ring(sign * k % 4))  15.3 us
    ppermute x4, starting transfers between devices, sibling(): return lax.ppermute(array, *pairs_of(lambda y, z, x, c: (y, z, x, 1 - c)))  8.96 us
    all_to_all x1, waiting for transfers between devices, shards(): lax.all_to_all(load, ('leaf', 'node'), split_axis=0, concat_axis=0, tiled...  8.04 us
    all_to_all x1, starting transfers between devices, shards(): lax.all_to_all(load, ('leaf', 'node'), split_axis=0, concat_axis=0, tiled...  5.73 us
    ppermute x2, starting transfers between devices, ring_gather(): three = lax.ppermute(rows, *ring(3))  4.19 us
  transfers between devices with their start and end apart: 35, of which 13 were waited for; matrix products, arithmetic and copies ran while one was open for 2% of the time, Pallas kernels for 15%

profile of v6, /device:TPU:1, one launch (start us, length us, event | category | flops | bytes accessed | tf_op | source)
XLA Modules:
  0.0 102.7 jit_solution(3607699401620473502)
XLA Ops:
  0.6 4.4 %shard_map.112 = (bf16[128,640]{1,0:T(8,128)(2,1)S(1)}, bf16[128,640]{1,0:T(8,128)(2,1)S(1)}, bf16[128,640]{1,0:T(8,128)(2,1)S(1)}, bf16[128,640]{1,0:T(8,128)(2...) custom-call(s32[288]{0:T(512)} %parent_far.1, ...), custom_call_target="tpu_custom_call" | custom-call | flops 1073741824 | bytes 2150944 | tf_op jit(solution)/shard_map/pallas_call | solution.py:58
  5.1 2.5 %collective-permute-start.3 = (bf16[128,512]{1,0:T(8,128)(2,1)S(1)}, bf16[128,512]{1,0:T(8,128)(2,1)S(1)}, u32[]{:S(2)}, u32[]{:S(2)}) collective-permute-start(bf16[128,512]{1,0:T(8,128)(2,1)S(1)} %get-tuple-element.98), channel_id=1, source_target_pairs={{0,32},{1,9},{2,34},{3,11},{4,36},{5,13},{6,38},{7,15},{8,40},{9,1... | collective-permute-start | bytes 393224 | tf_op jit(solution)/shard_map/ppermute | solution.py:363
  7.6 3.3 %collective-permute-start.4 = (bf16[128,512]{1,0:T(8,128)(2,1)S(1)}, bf16[128,512]{1,0:T(8,128)(2,1)S(1)}, u32[]{:S(2)}, u32[]{:S(2)}) collective-permute-start(bf16[128,512]{1,0:T(8,128)(2,1)S(1)} %get-tuple-element.99), channel_id=1, source_target_pairs={{0,64},{1,17},{2,66},{3,19},{4,68},{5,21},{6,70},{7,23},{8,72},{9,... | collective-permute-start | bytes 393224 | tf_op jit(solution)/shard_map/ppermute | solution.py:363
  12.9 2.4 %collective-permute-start.1 = (bf16[128,640]{1,0:T(8,128)(2,1)S(1)}, bf16[128,640]{1,0:T(8,128)(2,1)S(1)}, u32[]{:S(2)}, u32[]{:S(2)}) collective-permute-start(bf16[128,640]{1,0:T(8,128)(2,1)S(1)} %get-tuple-element.95), channel_id=1, source_target_pairs={{0,4},{1,5},{2,6},{3,7},{4,0},{5,1},{6,2},{7,3},{8,12},{9,13},{10,... | collective-permute-start | bytes 491528 | tf_op jit(solution)/shard_map/ppermute | solution.py:363
  17.1 2.8 %collective-permute-start.8 = (bf16[160,512]{1,0:T(8,128)(2,1)S(1)}, bf16[160,512]{1,0:T(8,128)(2,1)S(1)}, u32[]{:S(2)}, u32[]{:S(2)}) collective-permute-start(bf16[160,512]{1,0:T(8,128)(2,1)S(1)} %pad_maximum_fusion.4), channel_id=1, source_target_pairs={{0,24},{1,97},{2,26},{3,99},{4,28},{5,101},{6,30},{7,103},{8,0},{9... | collective-permute-start | bytes 491528 | tf_op jit(solution)/shard_map/ppermute | solution.py:363
  22.4 1.5 %collective-permute-done.8.g3 = bf16[160,512]{1,0:T(8,128)(2,1)S(1)} collective-permute-done((bf16[160,512]{1,0:T(8,128)(2,1)S(1)}, bf16[160,512]{1,0:T(8,128)(2,1)S(1)}, u32[]{:S(2)}, u32[]{:S(2)}) %collective-permute-start.8) | collective-permute-done | bytes 163872 | tf_op jit(solution)/shard_map/ppermute | solution.py:363
  24.0 1.8 %collective-permute-done.7.g2 = bf16[160,512]{1,0:T(8,128)(2,1)S(1)} collective-permute-done((bf16[160,512]{1,0:T(8,128)(2,1)S(1)}, bf16[160,512]{1,0:T(8,128)(2,1)S(1)}, u32[]{:S(2)}, u32[]{:S(2)}) %collective-permute-start.7) | collective-permute-done | bytes 163872 | tf_op jit(solution)/shard_map/ppermute | solution.py:363
  25.7 1.9 %collective-permute-done.6.g1 = bf16[160,512]{1,0:T(8,128)(2,1)S(1)} collective-permute-done((bf16[160,512]{1,0:T(8,128)(2,1)S(1)}, bf16[160,512]{1,0:T(8,128)(2,1)S(1)}, u32[]{:S(2)}, u32[]{:S(2)}) %collective-permute-start.6) | collective-permute-done | bytes 163872 | tf_op jit(solution)/shard_map/ppermute | solution.py:363
  27.7 3.5 %collective-permute-start.9 = (bf16[256,640]{1,0:T(8,128)(2,1)S(1)}, bf16[256,640]{1,0:T(8,128)(2,1)S(1)}, u32[]{:S(2)}, u32[]{:S(2)}) collective-permute-start(bf16[256,640]{1,0:T(8,128)(2,1)S(1)} %pad_maximum_fusion), channel_id=1, source_target_pairs={{0,1},{1,0},{2,3},{3,2},{4,5},{5,4},{6,7},{7,6},{8,9},{9,8},{10,11... | collective-permute-start | bytes 983048 | tf_op jit(solution)/shard_map/ppermute | solution.py:357
  33.3 2.1 %collective-permute-start.11 = (bf16[128,512]{1,0:T(8,128)(2,1)S(1)}, bf16[128,512]{1,0:T(8,128)(2,1)S(1)}, u32[]{:S(2)}, u32[]{:S(2)}) collective-permute-start(bf16[128,512]{1,0:T(8,128)(2,1)S(1)} %get-tuple-element.121), channel_id=1, source_target_pairs={{0,4},{1,5},{2,6},{3,7},{4,0},{5,1},{6,2},{7,3},{8,12},{9,13},{10,... | collective-permute-start | bytes 393224 | tf_op jit(solution)/shard_map/ppermute | solution.py:363
  35.4 2.5 %collective-permute-start.14 = (bf16[128,512]{1,0:T(8,128)(2,1)S(1)}, bf16[128,512]{1,0:T(8,128)(2,1)S(1)}, u32[]{:S(2)}, u32[]{:S(2)}) collective-permute-start(bf16[128,512]{1,0:T(8,128)(2,1)S(1)} %get-tuple-element.123.refs_1_.refs_0_), channel_id=1, source_target_pairs={{0,96},{1,25},{2,98},{3,27},{4,100},{5,29},{6,102},{7,31},{8,104},... | collective-permute-start | bytes 393224 | tf_op jit(solution)/shard_map/ppermute | solution.py:376
  37.9 2.5 %shard_map.117 = (f32[288,2048]{1,0:T(8,128)S(1)}, f32[32,512]{1,0:T(8,128)S(1)}) custom-call(bf16[256,512]{1,0:T(8,128)(2,1)S(1)} %get-tuple-element.124.refs_0_, bf16[128,512]{1,0:T(8,128)(2,1)S(1)} %get-tuple-element.123.refs_1_.refs_0_, f32[256,128]{1,0:T(8,128)S(1)} %get-tuple-element.108.scol.refs_2_, bf16[3,2048,512]{2,1,0:T(8,128)(2,1)S(1)} %copy-done, ...), custom_call_target="tpu_custom_call" | custom-call | flops 1073741824 | bytes 1753216 | tf_op jit(solution)/shard_map/pallas_call | solution.py:58
  40.4 2.1 %collective-permute-done.12.g3 = bf16[128,512]{1,0:T(8,128)(2,1)S(1)} collective-permute-done((bf16[128,512]{1,0:T(8,128)(2,1)S(1)}, bf16[128,512]{1,0:T(8,128)(2,1)S(1)}, u32[]{:S(2)}, u32[]{:S(2)}) %collective-permute-start.12) | collective-permute-done | bytes 131104 | tf_op jit(solution)/shard_map/ppermute | solution.py:363
  42.5 1.4 %collective-permute-start.15 = (bf16[256,512]{1,0:T(8,128)(2,1)S(1)}, bf16[256,512]{1,0:T(8,128)(2,1)S(1)}, u32[]{:S(2)}, u32[]{:S(2)}) collective-permute-start(bf16[256,512]{1,0:T(8,128)(2,1)S(1)} %pad_maximum_fusion.1), channel_id=1, source_target_pairs={{0,1},{1,0},{2,3},{3,2},{4,5},{5,4},{6,7},{7,6},{8,9},{9,8},{10,11... | collective-permute-start | bytes 786440 | tf_op jit(solution)/shard_map/ppermute | solution.py:357
  43.9 1.9 %shard_map.118 = (f32[256,2048]{1,0:T(8,128)S(1)}, bf16[128,512]{1,0:T(8,128)(2,1)S(1)}, bf16[128,512]{1,0:T(8,128)(2,1)S(1)}, bf16[128,512]{1,0:T(8,128)(2,1)S(1)}, bf16[128,512]{1,0:T(8,128)(2,1)S(1)}) custom-call(bf16[128,512]{1,0:T(8,128)(2,1)S(1)} %get-tuple-element.123.refs_1_.refs_0_, bf16[128,512]{1,0:T(8,128)(2,1)S(1)} %collective-permute-done.13.refs_1_, ...), custom_call_target="tpu_custom_call" | custom-call | flops 1073741824 | bytes 1229056 | tf_op jit(solution)/shard_map/pallas_call | solution.py:58
  45.9 3.1 %collective-permute-start.21 = (bf16[128,512]{1,0:T(8,128)(2,1)S(1)}, bf16[128,512]{1,0:T(8,128)(2,1)S(1)}, u32[]{:S(2)}, u32[]{:S(2)}) collective-permute-start(bf16[128,512]{1,0:T(8,128)(2,1)S(1)} %get-tuple-element.143), channel_id=1, source_target_pairs={{0,64},{1,17},{2,66},{3,19},{4,68},{5,21},{6,70},{7,23},{8,72},{9,... | collective-permute-start | bytes 393224 | tf_op jit(solution)/shard_map/ppermute | solution.py:363
  49.6 1.9 %shard_map.119 = (f32[288,2048]{1,0:T(8,128)S(1)}, bf16[288,2048]{1,0:T(8,128)(2,1)S(1)}, bf16[128,512]{1,0:T(8,128)(2,1)S(1)}, bf16[128,512]{1,0:T(8,128)(2,1)S...) custom-call(bf16[128,512]{1,0:T(8,128)(2,1)S(1)} %get-tuple-element.119.g0, ...), custom_call_target="tpu_custom_call" | custom-call | flops 1073741824 | bytes 1704192 | tf_op jit(solution)/shard_map/pallas_call | solution.py:58
  51.9 1.5 %collective-permute-start.18 = (bf16[128,512]{1,0:T(8,128)(2,1)S(1)}, bf16[128,512]{1,0:T(8,128)(2,1)S(1)}, u32[]{:S(2)}, u32[]{:S(2)}) collective-permute-start(bf16[128,512]{1,0:T(8,128)(2,1)S(1)} %get-tuple-element.139), channel_id=1, source_target_pairs={{0,4},{1,5},{2,6},{3,7},{4,0},{5,1},{6,2},{7,3},{8,12},{9,13},{10,... | collective-permute-start | bytes 393224 | tf_op jit(solution)/shard_map/ppermute | solution.py:363
  53.4 1.7 %collective-permute-start.19 = (bf16[128,512]{1,0:T(8,128)(2,1)S(1)}, bf16[128,512]{1,0:T(8,128)(2,1)S(1)}, u32[]{:S(2)}, u32[]{:S(2)}) collective-permute-start(bf16[128,512]{1,0:T(8,128)(2,1)S(1)} %get-tuple-element.140), channel_id=1, source_target_pairs={{0,6},{1,7},{2,0},{3,1},{4,2},{5,3},{6,4},{7,5},{8,14},{9,15},{10,... | collective-permute-start | bytes 393224 | tf_op jit(solution)/shard_map/ppermute | solution.py:363
  55.2 1.8 %collective-permute-start.25 = (bf16[128,512]{1,0:T(8,128)(2,1)S(1)}, bf16[128,512]{1,0:T(8,128)(2,1)S(1)}, u32[]{:S(2)}, u32[]{:S(2)}) collective-permute-start(bf16[128,512]{1,0:T(8,128)(2,1)S(1)} %pad_maximum_fusion.5), channel_id=1, source_target_pairs={{0,24},{1,97},{2,26},{3,99},{4,28},{5,101},{6,30},{7,103},{8,0},{9... | collective-permute-start | bytes 393224 | tf_op jit(solution)/shard_map/ppermute | solution.py:363
  60.9 1.4 %collective-permute-done.24.g2 = bf16[128,512]{1,0:T(8,128)(2,1)S(1)} collective-permute-done((bf16[128,512]{1,0:T(8,128)(2,1)S(1)}, bf16[128,512]{1,0:T(8,128)(2,1)S(1)}, u32[]{:S(2)}, u32[]{:S(2)}) %collective-permute-start.24) | collective-permute-done | bytes 131104 | tf_op jit(solution)/shard_map/ppermute | solution.py:363
  62.3 3.3 %collective-permute-done.23.g1 = bf16[128,512]{1,0:T(8,128)(2,1)S(1)} collective-permute-done((bf16[128,512]{1,0:T(8,128)(2,1)S(1)}, bf16[128,512]{1,0:T(8,128)(2,1)S(1)}, u32[]{:S(2)}, u32[]{:S(2)}) %collective-permute-start.23) | collective-permute-done | bytes 131104 | tf_op jit(solution)/shard_map/ppermute | solution.py:363
  65.7 1.8 %collective-permute-start.26 = (bf16[256,512]{1,0:T(8,128)(2,1)S(1)}, bf16[256,512]{1,0:T(8,128)(2,1)S(1)}, u32[]{:S(2)}, u32[]{:S(2)}) collective-permute-start(bf16[256,512]{1,0:T(8,128)(2,1)S(1)} %pad_maximum_fusion.2), channel_id=1, source_target_pairs={{0,1},{1,0},{2,3},{3,2},{4,5},{5,4},{6,7},{7,6},{8,9},{9,8},{10,11... | collective-permute-start | bytes 786440 | tf_op jit(solution)/shard_map/ppermute | solution.py:357
  69.5 2.0 %collective-permute-start.28 = (bf16[128,512]{1,0:T(8,128)(2,1)S(1)}, bf16[128,512]{1,0:T(8,128)(2,1)S(1)}, u32[]{:S(2)}, u32[]{:S(2)}) collective-permute-start(bf16[128,512]{1,0:T(8,128)(2,1)S(1)} %get-tuple-element.168), channel_id=1, source_target_pairs={{0,4},{1,5},{2,6},{3,7},{4,0},{5,1},{6,2},{7,3},{8,12},{9,13},{10,... | collective-permute-start | bytes 393224 | tf_op jit(solution)/shard_map/ppermute | solution.py:363
  71.8 1.7 %collective-permute-start.32 = (bf16[128,512]{1,0:T(8,128)(2,1)S(1)}, bf16[128,512]{1,0:T(8,128)(2,1)S(1)}, u32[]{:S(2)}, u32[]{:S(2)}) collective-permute-start(bf16[128,512]{1,0:T(8,128)(2,1)S(1)} %get-tuple-element.176.refs_1_.refs_0_), channel_id=1, source_target_pairs={{0,96},{1,25},{2,98},{3,27},{4,100},{5,29},{6,102},{7,31},{8,104},... | collective-permute-start | bytes 393224 | tf_op jit(solution)/shard_map/ppermute | solution.py:376
  73.5 2.1 %shard_map.124.refs_6_.base = f32[288,2048]{1,0:T(8,128)S(1)} custom-call(bf16[256,512]{1,0:T(8,128)(2,1)S(1)} %get-tuple-element.171.refs_0_, bf16[128,512]{1,0:T(8,128)(2,1)S(1)} %get-tuple-element.176.refs_1_.refs_0_, f32[256,128]{1,0:T(8,128)S(1)} %get-tuple-element.108.scol.refs_2_, bf16[3,2048,512]{2,1,0:T(8,128)(2,1)S(1)} %copy-done, ...), custom_call_target="tpu_custom_call" | custom-call | flops 1073741824 | bytes 1745024 | tf_op jit(solution)/shard_map/pallas_call | solution.py:58
  76.7 2.0 %collective-permute-done.29.g3 = bf16[128,512]{1,0:T(8,128)(2,1)S(1)} collective-permute-done((bf16[128,512]{1,0:T(8,128)(2,1)S(1)}, bf16[128,512]{1,0:T(8,128)(2,1)S(1)}, u32[]{:S(2)}, u32[]{:S(2)}) %collective-permute-start.29) | collective-permute-done | bytes 131104 | tf_op jit(solution)/shard_map/ppermute | solution.py:363
  78.8 2.3 %collective-permute-start.33 = (bf16[256,512]{1,0:T(8,128)(2,1)S(1)}, bf16[256,512]{1,0:T(8,128)(2,1)S(1)}, u32[]{:S(2)}, u32[]{:S(2)}) collective-permute-start(bf16[256,512]{1,0:T(8,128)(2,1)S(1)} %pad_maximum_fusion.3), channel_id=1, source_target_pairs={{0,1},{1,0},{2,3},{3,2},{4,5},{5,4},{6,7},{7,6},{8,9},{9,8},{10,11... | collective-permute-start | bytes 786440 | tf_op jit(solution)/shard_map/ppermute | solution.py:357
  82.2 2.0 %shard_map.126 = (f32[288,2048]{1,0:T(8,128)S(1)}, f32[128,1,128]{2,1,0:T(1,128)}) custom-call(bf16[128,512]{1,0:T(8,128)(2,1)S(1)} %get-tuple-element.166.g0, bf16[128,512]{1,0:T(8,128)(2,1)S(1)} %collective-permute-done.27.g1, bf16[128,512]{1,0:T(8,128)(2,1)S(1)} %collective-permute-done.28.g2, bf16[128,512]{1,0:T(8,128)(2,1)S(1)} %collective-permute-done.29.g3, ...), custom_call_target="tpu_custom_call" | custom-call | flops 536870912 | bytes 2089600 | tf_op jit(solution)/shard_map/pallas_call | solution.py:58
  84.2 5.7 %all-to-all-start = ((f32[128,1,128]{2,1,0:T(1,128)}), f32[128,1,128]{2,1,0:T(1,128)S(1)}, u32[]{:S(2)}, u32[]{:S(2)}) async-start(f32[128,1,128]{2,1,0:T(1,128)} %get-tuple-element.182), calls=%async_computation | async-start | bytes 131072 | tf_op jit(solution)/shard_map/all_to_all | solution.py:516
  90.0 1.4 %copy.12 = f32[288,2048]{1,0:T(8,128)} copy(f32[288,2048]{1,0:T(8,128)S(1)} %get-tuple-element.190) | data formatting | bytes 4718592
  91.4 8.0 %all-to-all-done = f32[128,1,128]{2,1,0:T(1,128)S(1)} async-done(((f32[128,1,128]{2,1,0:T(1,128)}), f32[128,1,128]{2,1,0:T(1,128)S(1)}, u32[]{:S(2)}, u32[]{:S(2)}) %all-to-all-start) | async-done | bytes 65568 | tf_op jit(solution)/shard_map/all_to_all | solution.py:516
  (94 shorter events, 18.1 us)
Async XLA Ops:
  5.1 10.7 %collective-permute-start.3 = (bf16[128,512]{1,0:T(8,128)(2,1)S(1)}, bf16[128,512]{1,0:T(8,128)(2,1)S(1)}, u32[]{:S(2)}, u32[]{:S(2)}) collective-permute-start(bf16[128,512]{1,0:T(8,128)(2,1)S(1)} %get-tuple-element.98), channel_id=1, source_target_pairs={{0,32},{1,9},{2,34},{3,11},{4,36},{5,13},{6,38},{7,15},{8,40},{9,1... | collective-permute-start | bytes 393224 | tf_op jit(solution)/shard_map/ppermute | solution.py:363
  7.6 9.4 %collective-permute-start.4 = (bf16[128,512]{1,0:T(8,128)(2,1)S(1)}, bf16[128,512]{1,0:T(8,128)(2,1)S(1)}, u32[]{:S(2)}, u32[]{:S(2)}) collective-permute-start(bf16[128,512]{1,0:T(8,128)(2,1)S(1)} %get-tuple-element.99), channel_id=1, source_target_pairs={{0,64},{1,17},{2,66},{3,19},{4,68},{5,21},{6,70},{7,23},{8,72},{9,... | collective-permute-start | bytes 393224 | tf_op jit(solution)/shard_map/ppermute | solution.py:363
  10.9 6.1 %collective-permute-start.5 = (bf16[128,512]{1,0:T(8,128)(2,1)S(1)}, bf16[128,512]{1,0:T(8,128)(2,1)S(1)}, u32[]{:S(2)}, u32[]{:S(2)}) collective-permute-start(bf16[128,512]{1,0:T(8,128)(2,1)S(1)} %get-tuple-element.100), channel_id=1, source_target_pairs={{0,96},{1,25},{2,98},{3,27},{4,100},{5,29},{6,102},{7,31},{8,104},... | collective-permute-start | bytes 393224 | tf_op jit(solution)/shard_map/ppermute | solution.py:363
  11.6 8.6 %collective-permute-start = (bf16[128,640]{1,0:T(8,128)(2,1)S(1)}, bf16[128,640]{1,0:T(8,128)(2,1)S(1)}, u32[]{:S(2)}, u32[]{:S(2)}) collective-permute-start(bf16[128,640]{1,0:T(8,128)(2,1)S(1)} %get-tuple-element.94), channel_id=1, source_target_pairs={{0,2},{1,3},{2,4},{3,5},{4,6},{5,7},{6,0},{7,1},{8,10},{9,11},{10,... | collective-permute-start | bytes 491528 | tf_op jit(solution)/shard_map/ppermute | solution.py:363
  12.9 9.5 %collective-permute-start.1 = (bf16[128,640]{1,0:T(8,128)(2,1)S(1)}, bf16[128,640]{1,0:T(8,128)(2,1)S(1)}, u32[]{:S(2)}, u32[]{:S(2)}) collective-permute-start(bf16[128,640]{1,0:T(8,128)(2,1)S(1)} %get-tuple-element.95), channel_id=1, source_target_pairs={{0,4},{1,5},{2,6},{3,7},{4,0},{5,1},{6,2},{7,3},{8,12},{9,13},{10,... | collective-permute-start | bytes 491528 | tf_op jit(solution)/shard_map/ppermute | solution.py:363
  15.8 6.6 %collective-permute-start.2 = (bf16[128,640]{1,0:T(8,128)(2,1)S(1)}, bf16[128,640]{1,0:T(8,128)(2,1)S(1)}, u32[]{:S(2)}, u32[]{:S(2)}) collective-permute-start(bf16[128,640]{1,0:T(8,128)(2,1)S(1)} %get-tuple-element.96), channel_id=1, source_target_pairs={{0,6},{1,7},{2,0},{3,1},{4,2},{5,3},{6,4},{7,5},{8,14},{9,15},{10,... | collective-permute-start | bytes 491528 | tf_op jit(solution)/shard_map/ppermute | solution.py:363
  17.1 6.8 %collective-permute-start.8 = (bf16[160,512]{1,0:T(8,128)(2,1)S(1)}, bf16[160,512]{1,0:T(8,128)(2,1)S(1)}, u32[]{:S(2)}, u32[]{:S(2)}) collective-permute-start(bf16[160,512]{1,0:T(8,128)(2,1)S(1)} %pad_maximum_fusion.4), channel_id=1, source_target_pairs={{0,24},{1,97},{2,26},{3,99},{4,28},{5,101},{6,30},{7,103},{8,0},{9... | collective-permute-start | bytes 491528 | tf_op jit(solution)/shard_map/ppermute | solution.py:363
  20.0 5.8 %collective-permute-start.7 = (bf16[160,512]{1,0:T(8,128)(2,1)S(1)}, bf16[160,512]{1,0:T(8,128)(2,1)S(1)}, u32[]{:S(2)}, u32[]{:S(2)}) collective-permute-start(bf16[160,512]{1,0:T(8,128)(2,1)S(1)} %pad_maximum_fusion.4), channel_id=1, source_target_pairs={{0,16},{1,65},{2,18},{3,67},{4,20},{5,69},{6,22},{7,71},{8,24},{9,... | collective-permute-start | bytes 491528 | tf_op jit(solution)/shard_map/ppermute | solution.py:363
  20.3 7.4 %collective-permute-start.6 = (bf16[160,512]{1,0:T(8,128)(2,1)S(1)}, bf16[160,512]{1,0:T(8,128)(2,1)S(1)}, u32[]{:S(2)}, u32[]{:S(2)}) collective-permute-start(bf16[160,512]{1,0:T(8,128)(2,1)S(1)} %pad_maximum_fusion.4), channel_id=1, source_target_pairs={{0,8},{1,33},{2,10},{3,35},{4,12},{5,37},{6,14},{7,39},{8,16},{9,4... | collective-permute-start | bytes 491528 | tf_op jit(solution)/shard_map/ppermute | solution.py:363
  32.2 5.7 %collective-permute-start.13 = (bf16[128,512]{1,0:T(8,128)(2,1)S(1)}, bf16[128,512]{1,0:T(8,128)(2,1)S(1)}, u32[]{:S(2)}, u32[]{:S(2)}) collective-permute-start(bf16[128,512]{1,0:T(8,128)(2,1)S(1)} %get-tuple-element.123.refs_1_.refs_0_), channel_id=1, source_target_pairs={{0,32},{1,9},{2,34},{3,11},{4,36},{5,13},{6,38},{7,15},{8,40},{9,1... | collective-permute-start | bytes 393224 | tf_op jit(solution)/shard_map/ppermute | solution.py:375
  33.2 7.2 %collective-permute-start.10 = (bf16[128,512]{1,0:T(8,128)(2,1)S(1)}, bf16[128,512]{1,0:T(8,128)(2,1)S(1)}, u32[]{:S(2)}, u32[]{:S(2)}) collective-permute-start(bf16[128,512]{1,0:T(8,128)(2,1)S(1)} %get-tuple-element.120), channel_id=1, source_target_pairs={{0,6},{1,7},{2,0},{3,1},{4,2},{5,3},{6,4},{7,5},{8,14},{9,15},{10,... | collective-permute-start | bytes 393224 | tf_op jit(solution)/shard_map/ppermute | solution.py:363
  33.3 7.1 %collective-permute-start.11 = (bf16[128,512]{1,0:T(8,128)(2,1)S(1)}, bf16[128,512]{1,0:T(8,128)(2,1)S(1)}, u32[]{:S(2)}, u32[]{:S(2)}) collective-permute-start(bf16[128,512]{1,0:T(8,128)(2,1)S(1)} %get-tuple-element.121), channel_id=1, source_target_pairs={{0,4},{1,5},{2,6},{3,7},{4,0},{5,1},{6,2},{7,3},{8,12},{9,13},{10,... | collective-permute-start | bytes 393224 | tf_op jit(solution)/shard_map/ppermute | solution.py:363
  35.4 7.1 %collective-permute-start.12 = (bf16[128,512]{1,0:T(8,128)(2,1)S(1)}, bf16[128,512]{1,0:T(8,128)(2,1)S(1)}, u32[]{:S(2)}, u32[]{:S(2)}) collective-permute-start(bf16[128,512]{1,0:T(8,128)(2,1)S(1)} %get-tuple-element.122), channel_id=1, source_target_pairs={{0,2},{1,3},{2,4},{3,5},{4,6},{5,7},{6,0},{7,1},{8,10},{9,11},{10,... | collective-permute-start | bytes 393224 | tf_op jit(solution)/shard_map/ppermute | solution.py:363
  35.4 7.1 %collective-permute-start.14 = (bf16[128,512]{1,0:T(8,128)(2,1)S(1)}, bf16[128,512]{1,0:T(8,128)(2,1)S(1)}, u32[]{:S(2)}, u32[]{:S(2)}) collective-permute-start(bf16[128,512]{1,0:T(8,128)(2,1)S(1)} %get-tuple-element.123.refs_1_.refs_0_), channel_id=1, source_target_pairs={{0,96},{1,25},{2,98},{3,27},{4,100},{5,29},{6,102},{7,31},{8,104},... | collective-permute-start | bytes 393224 | tf_op jit(solution)/shard_map/ppermute | solution.py:376
  37.9 6.0 %collective-permute-start.16 = (bf16[128,512]{1,0:T(8,128)(2,1)S(1)}, bf16[128,512]{1,0:T(8,128)(2,1)S(1)}, u32[]{:S(2)}, u32[]{:S(2)}) collective-permute-start(bf16[128,512]{1,0:T(8,128)(2,1)S(1)} %collective-permute-done.13.refs_1_), channel_id=1, source_target_pairs={{0,32},{1,9},{2,34},{3,11},{4,36},{5,13},{6,38},{7,15},{8,40},{9,1... | collective-permute-start | bytes 393224 | tf_op jit(solution)/shard_map/ppermute | solution.py:377
  42.5 7.0 %collective-permute-start.15 = (bf16[256,512]{1,0:T(8,128)(2,1)S(1)}, bf16[256,512]{1,0:T(8,128)(2,1)S(1)}, u32[]{:S(2)}, u32[]{:S(2)}) collective-permute-start(bf16[256,512]{1,0:T(8,128)(2,1)S(1)} %pad_maximum_fusion.1), channel_id=1, source_target_pairs={{0,1},{1,0},{2,3},{3,2},{4,5},{5,4},{6,7},{7,6},{8,9},{9,8},{10,11... | collective-permute-start | bytes 786440 | tf_op jit(solution)/shard_map/ppermute | solution.py:357
  45.8 7.6 %collective-permute-start.20 = (bf16[128,512]{1,0:T(8,128)(2,1)S(1)}, bf16[128,512]{1,0:T(8,128)(2,1)S(1)}, u32[]{:S(2)}, u32[]{:S(2)}) collective-permute-start(bf16[128,512]{1,0:T(8,128)(2,1)S(1)} %get-tuple-element.142), channel_id=1, source_target_pairs={{0,32},{1,9},{2,34},{3,11},{4,36},{5,13},{6,38},{7,15},{8,40},{9,1... | collective-permute-start | bytes 393224 | tf_op jit(solution)/shard_map/ppermute | solution.py:363
  45.9 9.2 %collective-permute-start.21 = (bf16[128,512]{1,0:T(8,128)(2,1)S(1)}, bf16[128,512]{1,0:T(8,128)(2,1)S(1)}, u32[]{:S(2)}, u32[]{:S(2)}) collective-permute-start(bf16[128,512]{1,0:T(8,128)(2,1)S(1)} %get-tuple-element.143), channel_id=1, source_target_pairs={{0,64},{1,17},{2,66},{3,19},{4,68},{5,21},{6,70},{7,23},{8,72},{9,... | collective-permute-start | bytes 393224 | tf_op jit(solution)/shard_map/ppermute | solution.py:363
  49.0 6.0 %collective-permute-start.22 = (bf16[128,512]{1,0:T(8,128)(2,1)S(1)}, bf16[128,512]{1,0:T(8,128)(2,1)S(1)}, u32[]{:S(2)}, u32[]{:S(2)}) collective-permute-start(bf16[128,512]{1,0:T(8,128)(2,1)S(1)} %get-tuple-element.144), channel_id=1, source_target_pairs={{0,96},{1,25},{2,98},{3,27},{4,100},{5,29},{6,102},{7,31},{8,104},... | collective-permute-start | bytes 393224 | tf_op jit(solution)/shard_map/ppermute | solution.py:363
  51.4 7.4 %collective-permute-start.17 = (bf16[128,512]{1,0:T(8,128)(2,1)S(1)}, bf16[128,512]{1,0:T(8,128)(2,1)S(1)}, u32[]{:S(2)}, u32[]{:S(2)}) collective-permute-start(bf16[128,512]{1,0:T(8,128)(2,1)S(1)} %get-tuple-element.138), channel_id=1, source_target_pairs={{0,2},{1,3},{2,4},{3,5},{4,6},{5,7},{6,0},{7,1},{8,10},{9,11},{10,... | collective-permute-start | bytes 393224 | tf_op jit(solution)/shard_map/ppermute | solution.py:363
  51.9 9.0 %collective-permute-start.18 = (bf16[128,512]{1,0:T(8,128)(2,1)S(1)}, bf16[128,512]{1,0:T(8,128)(2,1)S(1)}, u32[]{:S(2)}, u32[]{:S(2)}) collective-permute-start(bf16[128,512]{1,0:T(8,128)(2,1)S(1)} %get-tuple-element.139), channel_id=1, source_target_pairs={{0,4},{1,5},{2,6},{3,7},{4,0},{5,1},{6,2},{7,3},{8,12},{9,13},{10,... | collective-permute-start | bytes 393224 | tf_op jit(solution)/shard_map/ppermute | solution.py:363
  53.4 7.5 %collective-permute-start.19 = (bf16[128,512]{1,0:T(8,128)(2,1)S(1)}, bf16[128,512]{1,0:T(8,128)(2,1)S(1)}, u32[]{:S(2)}, u32[]{:S(2)}) collective-permute-start(bf16[128,512]{1,0:T(8,128)(2,1)S(1)} %get-tuple-element.140), channel_id=1, source_target_pairs={{0,6},{1,7},{2,0},{3,1},{4,2},{5,3},{6,4},{7,5},{8,14},{9,15},{10,... | collective-permute-start | bytes 393224 | tf_op jit(solution)/shard_map/ppermute | solution.py:363
  55.2 5.7 %collective-permute-start.25 = (bf16[128,512]{1,0:T(8,128)(2,1)S(1)}, bf16[128,512]{1,0:T(8,128)(2,1)S(1)}, u32[]{:S(2)}, u32[]{:S(2)}) collective-permute-start(bf16[128,512]{1,0:T(8,128)(2,1)S(1)} %pad_maximum_fusion.5), channel_id=1, source_target_pairs={{0,24},{1,97},{2,26},{3,99},{4,28},{5,101},{6,30},{7,103},{8,0},{9... | collective-permute-start | bytes 393224 | tf_op jit(solution)/shard_map/ppermute | solution.py:363
  57.0 5.3 %collective-permute-start.24 = (bf16[128,512]{1,0:T(8,128)(2,1)S(1)}, bf16[128,512]{1,0:T(8,128)(2,1)S(1)}, u32[]{:S(2)}, u32[]{:S(2)}) collective-permute-start(bf16[128,512]{1,0:T(8,128)(2,1)S(1)} %pad_maximum_fusion.5), channel_id=1, source_target_pairs={{0,16},{1,65},{2,18},{3,67},{4,20},{5,69},{6,22},{7,71},{8,24},{9,... | collective-permute-start | bytes 393224 | tf_op jit(solution)/shard_map/ppermute | solution.py:363
  58.8 6.8 %collective-permute-start.23 = (bf16[128,512]{1,0:T(8,128)(2,1)S(1)}, bf16[128,512]{1,0:T(8,128)(2,1)S(1)}, u32[]{:S(2)}, u32[]{:S(2)}) collective-permute-start(bf16[128,512]{1,0:T(8,128)(2,1)S(1)} %pad_maximum_fusion.5), channel_id=1, source_target_pairs={{0,8},{1,33},{2,10},{3,35},{4,12},{5,37},{6,14},{7,39},{8,16},{9,4... | collective-permute-start | bytes 393224 | tf_op jit(solution)/shard_map/ppermute | solution.py:363
  67.6 5.9 %collective-permute-start.30 = (bf16[128,512]{1,0:T(8,128)(2,1)S(1)}, bf16[128,512]{1,0:T(8,128)(2,1)S(1)}, u32[]{:S(2)}, u32[]{:S(2)}) collective-permute-start(bf16[128,512]{1,0:T(8,128)(2,1)S(1)} %get-tuple-element.176.refs_1_.refs_0_), channel_id=1, source_target_pairs={{0,32},{1,9},{2,34},{3,11},{4,36},{5,13},{6,38},{7,15},{8,40},{9,1... | collective-permute-start | bytes 393224 | tf_op jit(solution)/shard_map/ppermute | solution.py:375
  69.3 7.4 %collective-permute-start.27 = (bf16[128,512]{1,0:T(8,128)(2,1)S(1)}, bf16[128,512]{1,0:T(8,128)(2,1)S(1)}, u32[]{:S(2)}, u32[]{:S(2)}) collective-permute-start(bf16[128,512]{1,0:T(8,128)(2,1)S(1)} %get-tuple-element.167), channel_id=1, source_target_pairs={{0,6},{1,7},{2,0},{3,1},{4,2},{5,3},{6,4},{7,5},{8,14},{9,15},{10,... | collective-permute-start | bytes 393224 | tf_op jit(solution)/shard_map/ppermute | solution.py:363
  69.5 7.2 %collective-permute-start.28 = (bf16[128,512]{1,0:T(8,128)(2,1)S(1)}, bf16[128,512]{1,0:T(8,128)(2,1)S(1)}, u32[]{:S(2)}, u32[]{:S(2)}) collective-permute-start(bf16[128,512]{1,0:T(8,128)(2,1)S(1)} %get-tuple-element.168), channel_id=1, source_target_pairs={{0,4},{1,5},{2,6},{3,7},{4,0},{5,1},{6,2},{7,3},{8,12},{9,13},{10,... | collective-permute-start | bytes 393224 | tf_op jit(solution)/shard_map/ppermute | solution.py:363
  71.5 7.2 %collective-permute-start.29 = (bf16[128,512]{1,0:T(8,128)(2,1)S(1)}, bf16[128,512]{1,0:T(8,128)(2,1)S(1)}, u32[]{:S(2)}, u32[]{:S(2)}) collective-permute-start(bf16[128,512]{1,0:T(8,128)(2,1)S(1)} %get-tuple-element.169), channel_id=1, source_target_pairs={{0,2},{1,3},{2,4},{3,5},{4,6},{5,7},{6,0},{7,1},{8,10},{9,11},{10,... | collective-permute-start | bytes 393224 | tf_op jit(solution)/shard_map/ppermute | solution.py:363
  71.8 6.9 %collective-permute-start.32 = (bf16[128,512]{1,0:T(8,128)(2,1)S(1)}, bf16[128,512]{1,0:T(8,128)(2,1)S(1)}, u32[]{:S(2)}, u32[]{:S(2)}) collective-permute-start(bf16[128,512]{1,0:T(8,128)(2,1)S(1)} %get-tuple-element.176.refs_1_.refs_0_), channel_id=1, source_target_pairs={{0,96},{1,25},{2,98},{3,27},{4,100},{5,29},{6,102},{7,31},{8,104},... | collective-permute-start | bytes 393224 | tf_op jit(solution)/shard_map/ppermute | solution.py:376
  73.5 5.3 %collective-permute-start.31 = (bf16[128,512]{1,0:T(8,128)(2,1)S(1)}, bf16[128,512]{1,0:T(8,128)(2,1)S(1)}, u32[]{:S(2)}, u32[]{:S(2)}) collective-permute-start(bf16[128,512]{1,0:T(8,128)(2,1)S(1)} %collective-permute-done.30.refs_1_), channel_id=1, source_target_pairs={{0,32},{1,9},{2,34},{3,11},{4,36},{5,13},{6,38},{7,15},{8,40},{9,1... | collective-permute-start | bytes 393224 | tf_op jit(solution)/shard_map/ppermute | solution.py:377
  84.2 15.2 %all-to-all-start = ((f32[128,1,128]{2,1,0:T(1,128)}), f32[128,1,128]{2,1,0:T(1,128)S(1)}, u32[]{:S(2)}, u32[]{:S(2)}) async-start(f32[128,1,128]{2,1,0:T(1,128)} %get-tuple-element.182), calls=%async_computation | async-start | bytes 131072 | tf_op jit(solution)/shard_map/all_to_all | solution.py:516
  (7 other events, 61.8 us)
